TPU v7x, 128 devices: a whole 4x4x4 slice. The times are simulated.
128 devices in a mesh: fac: 8 (over y, core), jac: 16 (over x, z).
Axes of the slice: x: 4, y: 4, z: 4, core: 2. Of those that a mesh axis runs over, the one named last changes fastest.
Arguments:
- statistics: float32 [8, 2048, 2048], P(None, ('fac', 'jac')), may hold values from -24 to 24, as said below
- assignment: int32 [8], replicated, may hold values from 0 to 7, each once
Outputs:
- rotated_factor: float32 [8, 2048, 2048], P('fac', None, 'jac')
- eigen_basis: float32 [8, 2048, 2048], P('fac', None, 'jac')
Inputs may be any that keep to these rules, and one draw needn't show every extreme that they name: `statistics`: each factor is symmetric. assignment is a permutation: each group takes one factor.
All inputs are finite; a program needn't handle non-finite values.
Results may differ from a plain program's by a relative error of at most 0.0025.
Values sent between devices are 32-bit elements; how exact they have to be, the bound alone decides.
No kernel may reach another device: no remote copies, remote signals or barrier semaphores. Data moves between devices by JAX's collectives and lax.ppermute only.
A program may use at most 128 MiB of HBM per device.

v0:
```python
import functools

import jax
import jax.numpy as jnp
import numpy as np
from jax import lax
from jax.experimental import pallas as pl
from jax.experimental.pallas import tpu as pltpu
from jax.sharding import PartitionSpec as P

ROUNDS = 3
HIGH = lax.Precision.HIGHEST
BLK = 64
WIDTH = 2 * BLK
SECTIONS = 16
SUB = 8
GROUPS = BLK // SUB


def lane_ids(rows):
    return lax.broadcasted_iota(jnp.int32, (rows, WIDTH), 1)


def angles(alpha, beta, gamma):
    diff = beta - alpha
    square = diff * diff + 4.0 * gamma * gamma
    turns = square > 0
    inverse = jnp.where(turns, lax.rsqrt(jnp.where(turns, square, 1.0)), 0.0)
    along = diff * inverse
    lead = 1.0 + jnp.abs(along)
    cross = 2.0 * gamma * inverse * along
    scale = lax.rsqrt(lead * lead + cross * cross)
    return lead * scale, cross * scale


def small_rotation(gram, store):
    lanes = lane_ids(WIDTH)
    rows = lax.broadcasted_iota(jnp.int32, (WIDTH, WIDTH), 0)
    upper_half = lanes & BLK
    skew = ((rows - lanes) & (BLK - 1)) + upper_half
    store[...] = jnp.take_along_axis(gram, skew, axis=1).T
    low = lane_ids(SUB) < BLK
    aa, bb, tt, dd = [], [], [], []
    for b in range(GROUPS):
        top = store[pl.ds(b, SUB, stride=SUB), :]
        bot = store[pl.ds(BLK + b, SUB, stride=SUB), :]
        top_swap = pltpu.roll(top, BLK, 1)
        bot_swap = pltpu.roll(bot, BLK, 1)
        aa.append(jnp.where(low, top, top_swap))
        tt.append(jnp.where(low, top_swap, top))
        bb.append(jnp.where(low, bot, bot_swap))
        dd.append(jnp.where(low, bot_swap, bot))
    first_rows = lax.broadcasted_iota(jnp.int32, (SUB, WIDTH), 0)
    start = jnp.where(first_rows == 0, 1.0, 0.0).astype(jnp.float32)
    zero = jnp.zeros((SUB, WIDTH), jnp.float32)
    ru = [jnp.where(low, start, 0.0)] + [zero] * (GROUPS - 1)
    rl = [jnp.where(low, 0.0, start)] + [zero] * (GROUPS - 1)

    def spread(x, row):
        return jnp.broadcast_to(x[row:row + 1], (SUB, WIDTH))

    alpha, beta, gamma = spread(aa[0], 0), spread(dd[0], 0), spread(bb[0], 0)
    for section in range(SECTIONS):
        c, s = angles(alpha, beta, gamma)
        cc = [pltpu.roll(c, b, 1, stride=SUB, stride_axis=0) for b in range(GROUPS)]
        ss = [pltpu.roll(s, b, 1, stride=SUB, stride_axis=0) for b in range(GROUPS)]
        new_ru = [cc[b] * ru[b] - ss[b] * rl[b] for b in range(GROUPS)]
        new_rl = [ss[b] * ru[b] + cc[b] * rl[b] for b in range(GROUPS)]
        ru, rl = new_ru, new_rl
        if section == SECTIONS - 1:
            break
        rl = [pltpu.roll(rl[-1], 1, 0)] + rl[:-1]
        a1 = [cc[b] * aa[b] - ss[b] * bb[b] for b in range(GROUPS)]
        b1 = [ss[b] * aa[b] + cc[b] * bb[b] for b in range(GROUPS)]
        t1 = [cc[b] * tt[b] - ss[b] * dd[b] for b in range(GROUPS)]
        d1 = [ss[b] * tt[b] + cc[b] * dd[b] for b in range(GROUPS)]
        aa = [c * a1[b] - s * t1[b] for b in range(GROUPS)]
        t2 = [s * a1[b] + c * t1[b] for b in range(GROUPS)]
        b2 = [c * b1[b] - s * d1[b] for b in range(GROUPS)]
        d2 = [s * b1[b] + c * d1[b] for b in range(GROUPS)]
        new_alpha = c * (c * alpha - s * gamma) - s * (c * gamma - s * beta)
        new_beta = s * (s * alpha + c * gamma) + c * (s * gamma + c * beta)
        alpha, beta = new_alpha, pltpu.roll(new_beta, WIDTH - 1, 1)
        gamma = spread(b2[-1], SUB - 1)
        bb = [pltpu.roll(b2[-1], 1, 0)] + b2[:-1]
        t2 = t2[1:] + [pltpu.roll(t2[0], SUB - 1, 0)]
        tt = [pltpu.roll(x, WIDTH - 1, 1) for x in t2]
        dd = [pltpu.roll(x, WIDTH - 1, 1) for x in d2]
    for b in range(GROUPS):
        store[pl.ds(b, SUB, stride=SUB), :] = ru[b]
        store[pl.ds(BLK + b, SUB, stride=SUB), :] = rl[b]
    offset = jnp.where(upper_half == 0, 0, SECTIONS - 1)
    unskew = ((rows - lanes + offset) & (BLK - 1)) + upper_half
    return jnp.take_along_axis(store[...].T, unskew, axis=1)


def deal_kernel(assignment, stats, out):
    factors, _, order = stats.shape
    count = order // WIDTH
    for factor in range(factors):
        group = assignment[factor]
        for place in range(count):
            out[group * count + place] = stats[factor, :, place * WIDTH:(place + 1) * WIDTH]


def product(a, b):
    return jnp.dot(a, b, precision=HIGH, preferred_element_type=jnp.float32)


def post(place, turned, right, left, columns):
    top, bottom = turned[:BLK], turned[BLK:]
    first = place == 0
    right[:, columns] = jnp.where(first, bottom, top)
    left[:, columns] = jnp.where(first, top, bottom)


def first_kernel(place_ref, work, right, left, store):
    place = place_ref[0]
    order = work.shape[0]
    straight = work[...]
    flat = straight.T
    rotation = small_rotation(product(flat, straight), store).T
    post(place, product(rotation, flat), right, left, pl.ds(0, order))
    post(place, rotation, right, left, pl.ds(order, WIDTH))


def gather_pair(place, last, own_right, own_left, came_right, came_left, pair, sems):
    upper, lower = pair.at[pl.ds(0, BLK)], pair.at[pl.ds(BLK, BLK)]

    @pl.when(place == 0)
    def _():
        pltpu.make_async_copy(own_left, upper, sems.at[0]).start()

    @pl.when(place != 0)
    def _():
        pltpu.make_async_copy(came_right, upper, sems.at[0]).start()

    @pl.when(place == last)
    def _():
        pltpu.make_async_copy(own_right, lower, sems.at[1]).start()

    @pl.when(place != last)
    def _():
        pltpu.make_async_copy(came_left, lower, sems.at[1]).start()

    pltpu.make_async_copy(came_right, upper, sems.at[0]).wait()
    pltpu.make_async_copy(came_left, lower, sems.at[1]).wait()


def next_kernel(last, order, place_ref, own_right, own_left, came_right, came_left, right, left, pair, store, sems):
    place = place_ref[0]
    gather_pair(place, last, own_right, own_left, came_right, came_left, pair, sems)
    support = pair.shape[1] - order
    flat = pair[:, :order]
    gram = lax.dot_general(
        flat, flat, (((1,), (1,)), ((), ())), precision=HIGH, preferred_element_type=jnp.float32
    )
    rotation = small_rotation(gram, store).T
    post(place, product(rotation, flat), right, left, pl.ds(0, order))
    upper = product(rotation[:, :BLK], pair[:BLK, order:])
    post(place, upper, right, left, pl.ds(order, support))
    lower = product(rotation[:, BLK:], pair[BLK:, order:])
    post(place, lower, right, left, pl.ds(order + support, support))


def last_kernel(last, order, place_ref, table, own_right, own_left, came_right, came_left, work, basis, pair, sems):
    place = place_ref[0]
    gather_pair(place, last, own_right, own_left, came_right, came_left, pair, sems)
    work[...] = pair[:, :order].T
    basis[...] = jnp.zeros_like(basis)
    chunks = (pair.shape[1] - order) // WIDTH
    tops = lane_ids(WIDTH) < BLK
    for half in range(2):
        for chunk in range(chunks):
            row = pl.multiple_of(table[place, half * chunks + chunk] * WIDTH, WIDTH)
            piece = pair[:, order + chunk * WIDTH:order + (chunk + 1) * WIDTH].T
            keep = tops if half == 0 else jnp.logical_not(tops)
            basis[pl.ds(row, WIDTH), :] += jnp.where(keep, piece, 0.0)


def support_table(count):
    source_top = [max(p - 1, 0) for p in range(count)]
    source_bottom = [min(p + 1, count - 1) for p in range(count)]
    support = [[p] for p in range(count)]
    for _ in range(ROUNDS - 1):
        support = [support[source_top[p]] + support[source_bottom[p]] for p in range(count)]
    return np.array([support[source_top[p]] + support[source_bottom[p]] for p in range(count)], np.int32)


def vmem():
    return pl.BlockSpec(memory_space=pltpu.VMEM)


def smem():
    return pl.BlockSpec(memory_space=pltpu.SMEM)


def anywhere():
    return pl.BlockSpec(memory_space=pl.ANY)


PARAMS = pltpu.CompilerParams(vmem_limit_bytes=40 * 1024 * 1024)


def shape(*dims):
    return jax.ShapeDtypeStruct(dims, jnp.float32)


def shards(statistics, assignment):
    factors, slab, order = statistics.shape
    count = order // WIDTH
    devices = factors * count
    last = count - 1
    place = lax.axis_index("jac").astype(jnp.int32).reshape(1)
    dealt = pl.pallas_call(
        deal_kernel,
        out_shape=shape(devices, slab, WIDTH),
        in_specs=[smem(), vmem()],
        out_specs=vmem(),
        compiler_params=PARAMS,
        name="deal",
    )(assignment, statistics)
    moved = lax.all_to_all(dealt, ("fac", "jac"), split_axis=0, concat_axis=0, tiled=True)
    work = moved.reshape(order, WIDTH)
    support = WIDTH
    right, left = pl.pallas_call(
        first_kernel,
        out_shape=[shape(BLK, order + support)] * 2,
        in_specs=[smem(), vmem()],
        out_specs=[vmem()] * 2,
        scratch_shapes=[pltpu.VMEM((WIDTH, WIDTH), jnp.float32)],
        compiler_params=PARAMS,
        name="first_round",
    )(place, work)
    forward = [(p, p + 1) for p in range(last)]
    backward = [(p + 1, p) for p in range(last)]
    for _ in range(ROUNDS - 1):
        came_right = lax.ppermute(right, "jac", forward)
        came_left = lax.ppermute(left, "jac", backward)
        right, left = pl.pallas_call(
            functools.partial(next_kernel, last, order),
            out_shape=[shape(BLK, order + 2 * support)] * 2,
            in_specs=[smem()] + [anywhere()] * 4,
            out_specs=[vmem()] * 2,
            scratch_shapes=[
                pltpu.VMEM((WIDTH, order + support), jnp.float32),
                pltpu.VMEM((WIDTH, WIDTH), jnp.float32),
                pltpu.SemaphoreType.DMA((2,)),
            ],
            compiler_params=PARAMS,
            name="next_round",
        )(place, right, left, came_right, came_left)
        support = 2 * support
    came_right = lax.ppermute(right, "jac", forward)
    came_left = lax.ppermute(left, "jac", backward)
    work, basis = pl.pallas_call(
        functools.partial(last_kernel, last, order),
        out_shape=[shape(order, WIDTH)] * 2,
        in_specs=[smem(), smem()] + [anywhere()] * 4,
        out_specs=[vmem()] * 2,
        scratch_shapes=[
            pltpu.VMEM((WIDTH, order + support), jnp.float32),
            pltpu.SemaphoreType.DMA((2,)),
        ],
        compiler_params=PARAMS,
        name="output",
    )(place, jnp.asarray(support_table(count)), right, left, came_right, came_left)
    return work[None], basis[None]


def solution(mesh):
    return jax.shard_map(
        shards,
        mesh=mesh,
        in_specs=(P(None, ("fac", "jac"), None), P()),
        out_specs=(P("fac", None, "jac"), P("fac", None, "jac")),
        check_vma=False,
    )
```

profile of v0, /device:TPU:100, one launch (start us, length us, event | category | flops | bytes accessed | tf_op | source)
XLA Modules:
  0.0 113.4 jit_solution(16263218704178017127)
XLA Ops:
  0.6 0.0 copy-start
  0.6 1.2 %copy-done = f32[8,16,2048]{2,1,0:T(8,128)S(1)} copy-done((f32[8,16,2048]{2,1,0:T(8,128)S(1)}, f32[8,16,2048]{2,1,0:T(8,128)}, u32[]{:S(2)}) %copy-start) | copy-done | bytes 1048600
  1.9 0.0 copy-start.2
  1.9 0.7 copy-done.2
  2.5 1.6 %deal.1 = f32[128,16,128]{2,1,0:T(8,128)} custom-call(s32[8]{0:T(128)S(1)} %copy-done.2, f32[8,16,2048]{2,1,0:T(8,128)S(1)} %copy-done), custom_call_target="tpu_custom_call" | custom-call | tf_op jit(solution)/shard_map/deal/pallas_call | solution.py:215
  4.1 9.8 %all-to-all-start = ((f32[128,16,128]{2,1,0:T(8,128)}), f32[128,16,128]{2,1,0:T(8,128)S(1)}, u32[]{:S(2)}, u32[]{:S(2)}) async-start(f32[128,16,128]{2,1,0:T(8,128)} %deal.1), calls=%async_computation | async-start | bytes 2097152 | tf_op jit(solution)/shard_map/all_to_all | solution.py:223
  13.9 14.9 %all-to-all-done = f32[128,16,128]{2,1,0:T(8,128)S(1)} async-done(((f32[128,16,128]{2,1,0:T(8,128)}), f32[128,16,128]{2,1,0:T(8,128)S(1)}, u32[]{:S(2)}, u32[]{:S(2)}) %all-to-all-start) | async-done | bytes 1048608 | tf_op jit(solution)/shard_map/all_to_all | solution.py:223
  28.9 4.3 %first_round.1 = (f32[64,2176]{1,0:T(8,128)S(1)}, f32[64,2176]{1,0:T(8,128)S(1)}) custom-call(s32[1]{0:T(128)} %bitcast.place_ref, f32[2048,128]{1,0:T(8,128)S(1)} %bitcast.4), custom_call_target="tpu_custom_call" | custom-call | tf_op jit(solution)/shard_map/first_round/pallas_call | solution.py:226
  33.2 4.7 %collective-permute-start = (f32[64,2176]{1,0:T(8,128)S(1)}, f32[64,2176]{1,0:T(8,128)S(1)}, u32[]{:S(2)}, u32[]{:S(2)}) collective-permute-start(f32[64,2176]{1,0:T(8,128)S(1)} %get-tuple-element.10.own_right), channel_id=1, source_target_pairs={{0,1},{1,2},{2,3},{3,4},{4,5},{5,6},{6,7},{7,8},{8,9},{9,10},{10,1... | collective-permute-start | bytes 1671176 | tf_op jit(solution)/shard_map/ppermute | solution.py:238
  37.9 1.9 %collective-permute-start.1 = (f32[64,2176]{1,0:T(8,128)S(1)}, f32[64,2176]{1,0:T(8,128)S(1)}, u32[]{:S(2)}, u32[]{:S(2)}) collective-permute-start(f32[64,2176]{1,0:T(8,128)S(1)} %get-tuple-element.11.own_left), channel_id=1, source_target_pairs={{1,0},{2,1},{3,2},{4,3},{5,4},{6,5},{7,6},{8,7},{9,8},{10,9},{11,1... | collective-permute-start | bytes 1671176 | tf_op jit(solution)/shard_map/ppermute | solution.py:239
  39.8 10.5 %collective-permute-done.came_right = f32[64,2176]{1,0:T(8,128)S(1)} collective-permute-done((f32[64,2176]{1,0:T(8,128)S(1)}, f32[64,2176]{1,0:T(8,128)S(1)}, u32[]{:S(2)}, u32[]{:S(2)}) %collective-permute-start) | collective-permute-done | bytes 557088 | tf_op jit(solution)/shard_map/ppermute | solution.py:238
  50.3 6.2 %collective-permute-done.1.came_left = f32[64,2176]{1,0:T(8,128)S(1)} collective-permute-done((f32[64,2176]{1,0:T(8,128)S(1)}, f32[64,2176]{1,0:T(8,128)S(1)}, u32[]{:S(2)}, u32[]{:S(2)}) %collective-permute-start.1) | collective-permute-done | bytes 557088 | tf_op jit(solution)/shard_map/ppermute | solution.py:239
  56.5 6.0 %next_round.2 = (f32[64,2304]{1,0:T(8,128)S(1)}, f32[64,2304]{1,0:T(8,128)S(1)}) custom-call(s32[1]{0:T(128)} %bitcast.place_ref, f32[64,2176]{1,0:T(8,128)S(1)} %get-tuple-element.10.own_right, f32[64,2176]{1,0:T(8,128)S(1)} %get-tuple-element.11.own_left, f32[64,2176]{1,0:T(8,128)S(1)} %collective-permute-done.came_right, ...), custom_call_target="tpu_custom_call" | custom-call | tf_op jit(solution)/shard_map/next_round/pallas_call | solution.py:240
  62.6 1.9 %collective-permute-start.2 = (f32[64,2304]{1,0:T(8,128)S(1)}, f32[64,2304]{1,0:T(8,128)S(1)}, u32[]{:S(2)}, u32[]{:S(2)}) collective-permute-start(f32[64,2304]{1,0:T(8,128)S(1)} %get-tuple-element.12.own_right), channel_id=1, source_target_pairs={{0,1},{1,2},{2,3},{3,4},{4,5},{5,6},{6,7},{7,8},{8,9},{9,10},{10,1... | collective-permute-start | bytes 1769480 | tf_op jit(solution)/shard_map/ppermute | solution.py:238
  64.5 3.9 %collective-permute-start.3 = (f32[64,2304]{1,0:T(8,128)S(1)}, f32[64,2304]{1,0:T(8,128)S(1)}, u32[]{:S(2)}, u32[]{:S(2)}) collective-permute-start(f32[64,2304]{1,0:T(8,128)S(1)} %get-tuple-element.13.own_left), channel_id=1, source_target_pairs={{1,0},{2,1},{3,2},{4,3},{5,4},{6,5},{7,6},{8,7},{9,8},{10,9},{11,1... | collective-permute-start | bytes 1769480 | tf_op jit(solution)/shard_map/ppermute | solution.py:239
  68.4 10.6 %collective-permute-done.2.came_right = f32[64,2304]{1,0:T(8,128)S(1)} collective-permute-done((f32[64,2304]{1,0:T(8,128)S(1)}, f32[64,2304]{1,0:T(8,128)S(1)}, u32[]{:S(2)}, u32[]{:S(2)}) %collective-permute-start.2) | collective-permute-done | bytes 589856 | tf_op jit(solution)/shard_map/ppermute | solution.py:238
  79.0 4.0 %collective-permute-done.3.came_left = f32[64,2304]{1,0:T(8,128)S(1)} collective-permute-done((f32[64,2304]{1,0:T(8,128)S(1)}, f32[64,2304]{1,0:T(8,128)S(1)}, u32[]{:S(2)}, u32[]{:S(2)}) %collective-permute-start.3) | collective-permute-done | bytes 589856 | tf_op jit(solution)/shard_map/ppermute | solution.py:239
  83.1 0.0 copy-start.1
  83.1 6.4 %next_round.3 = (f32[64,2560]{1,0:T(8,128)S(1)}, f32[64,2560]{1,0:T(8,128)S(1)}) custom-call(s32[1]{0:T(128)} %bitcast.place_ref, f32[64,2304]{1,0:T(8,128)S(1)} %get-tuple-element.12.own_right, f32[64,2304]{1,0:T(8,128)S(1)} %get-tuple-element.13.own_left, f32[64,2304]{1,0:T(8,128)S(1)} %collective-permute-done.2.came_right, ...), custom_call_target="tpu_custom_call" | custom-call | tf_op jit(solution)/shard_map/next_round/pallas_call | solution.py:240
  89.5 1.9 %collective-permute-start.4 = (f32[64,2560]{1,0:T(8,128)S(1)}, f32[64,2560]{1,0:T(8,128)S(1)}, u32[]{:S(2)}, u32[]{:S(2)}) collective-permute-start(f32[64,2560]{1,0:T(8,128)S(1)} %get-tuple-element.14.own_right), channel_id=1, source_target_pairs={{0,1},{1,2},{2,3},{3,4},{4,5},{5,6},{6,7},{7,8},{8,9},{9,10},{10,1... | collective-permute-start | bytes 1966088 | tf_op jit(solution)/shard_map/ppermute | solution.py:254
  91.4 3.9 %collective-permute-start.5 = (f32[64,2560]{1,0:T(8,128)S(1)}, f32[64,2560]{1,0:T(8,128)S(1)}, u32[]{:S(2)}, u32[]{:S(2)}) collective-permute-start(f32[64,2560]{1,0:T(8,128)S(1)} %get-tuple-element.15.own_left), channel_id=1, source_target_pairs={{1,0},{2,1},{3,2},{4,3},{5,4},{6,5},{7,6},{8,7},{9,8},{10,9},{11,1... | collective-permute-start | bytes 1966088 | tf_op jit(solution)/shard_map/ppermute | solution.py:255
  95.3 11.1 %collective-permute-done.4.came_right = f32[64,2560]{1,0:T(8,128)S(1)} collective-permute-done((f32[64,2560]{1,0:T(8,128)S(1)}, f32[64,2560]{1,0:T(8,128)S(1)}, u32[]{:S(2)}, u32[]{:S(2)}) %collective-permute-start.4) | collective-permute-done | bytes 655392 | tf_op jit(solution)/shard_map/ppermute | solution.py:254
  106.4 4.0 %collective-permute-done.5.came_left = f32[64,2560]{1,0:T(8,128)S(1)} collective-permute-done((f32[64,2560]{1,0:T(8,128)S(1)}, f32[64,2560]{1,0:T(8,128)S(1)}, u32[]{:S(2)}, u32[]{:S(2)}) %collective-permute-start.5) | collective-permute-done | bytes 655392 | tf_op jit(solution)/shard_map/ppermute | solution.py:255
  110.5 0.0 copy-done.1
  110.5 2.8 %output.1 = (f32[2048,128]{1,0:T(8,128)}, f32[2048,128]{1,0:T(8,128)}) custom-call(s32[1]{0:T(128)} %bitcast.place_ref, s32[16,8]{1,0:T(8,128)S(1)} %copy-done.1, f32[64,2560]{1,0:T(8,128)S(1)} %get-tuple-element.14.own_right, f32[64,2560]{1,0:T(8,128)S(1)} %get-tuple-element.15.own_left, f32[64,2560]{1,0:T(8,128)S(1)} %collective-permute-done.4.came_right, ...), custom_call_target="tpu_custom_call" | custom-call | tf_op jit(solution)/shard_map/output/pallas_call | solution.py:256
Async XLA Ops:
  0.6 1.2 %copy-start = (f32[8,16,2048]{2,1,0:T(8,128)S(1)}, f32[8,16,2048]{2,1,0:T(8,128)}, u32[]{:S(2)}) copy-start(f32[8,16,2048]{2,1,0:T(8,128)} %stats.1) | copy-start | bytes 3145732
  1.9 0.7 copy-start.2
  4.1 24.8 %all-to-all-start = ((f32[128,16,128]{2,1,0:T(8,128)}), f32[128,16,128]{2,1,0:T(8,128)S(1)}, u32[]{:S(2)}, u32[]{:S(2)}) async-start(f32[128,16,128]{2,1,0:T(8,128)} %deal.1), calls=%async_computation | async-start | bytes 2097152 | tf_op jit(solution)/shard_map/all_to_all | solution.py:223
  33.2 17.1 %collective-permute-start = (f32[64,2176]{1,0:T(8,128)S(1)}, f32[64,2176]{1,0:T(8,128)S(1)}, u32[]{:S(2)}, u32[]{:S(2)}) collective-permute-start(f32[64,2176]{1,0:T(8,128)S(1)} %get-tuple-element.10.own_right), channel_id=1, source_target_pairs={{0,1},{1,2},{2,3},{3,4},{4,5},{5,6},{6,7},{7,8},{8,9},{9,10},{10,1... | collective-permute-start | bytes 1671176 | tf_op jit(solution)/shard_map/ppermute | solution.py:238
  37.9 18.7 %collective-permute-start.1 = (f32[64,2176]{1,0:T(8,128)S(1)}, f32[64,2176]{1,0:T(8,128)S(1)}, u32[]{:S(2)}, u32[]{:S(2)}) collective-permute-start(f32[64,2176]{1,0:T(8,128)S(1)} %get-tuple-element.11.own_left), channel_id=1, source_target_pairs={{1,0},{2,1},{3,2},{4,3},{5,4},{6,5},{7,6},{8,7},{9,8},{10,9},{11,1... | collective-permute-start | bytes 1671176 | tf_op jit(solution)/shard_map/ppermute | solution.py:239
  62.6 16.4 %collective-permute-start.2 = (f32[64,2304]{1,0:T(8,128)S(1)}, f32[64,2304]{1,0:T(8,128)S(1)}, u32[]{:S(2)}, u32[]{:S(2)}) collective-permute-start(f32[64,2304]{1,0:T(8,128)S(1)} %get-tuple-element.12.own_right), channel_id=1, source_target_pairs={{0,1},{1,2},{2,3},{3,4},{4,5},{5,6},{6,7},{7,8},{8,9},{9,10},{10,1... | collective-permute-start | bytes 1769480 | tf_op jit(solution)/shard_map/ppermute | solution.py:238
  64.5 18.6 %collective-permute-start.3 = (f32[64,2304]{1,0:T(8,128)S(1)}, f32[64,2304]{1,0:T(8,128)S(1)}, u32[]{:S(2)}, u32[]{:S(2)}) collective-permute-start(f32[64,2304]{1,0:T(8,128)S(1)} %get-tuple-element.13.own_left), channel_id=1, source_target_pairs={{1,0},{2,1},{3,2},{4,3},{5,4},{6,5},{7,6},{8,7},{9,8},{10,9},{11,1... | collective-permute-start | bytes 1769480 | tf_op jit(solution)/shard_map/ppermute | solution.py:239
  83.1 27.4 %copy-start.1 = (s32[16,8]{1,0:T(8,128)S(1)}, s32[16,8]{1,0:T(8,128)}, u32[]{:S(2)}) copy-start(s32[16,8]{1,0:T(8,128)} %constant.6.clone.table) | copy-start | bytes 1540
  89.5 16.9 %collective-permute-start.4 = (f32[64,2560]{1,0:T(8,128)S(1)}, f32[64,2560]{1,0:T(8,128)S(1)}, u32[]{:S(2)}, u32[]{:S(2)}) collective-permute-start(f32[64,2560]{1,0:T(8,128)S(1)} %get-tuple-element.14.own_right), channel_id=1, source_target_pairs={{0,1},{1,2},{2,3},{3,4},{4,5},{5,6},{6,7},{7,8},{8,9},{9,10},{10,1... | collective-permute-start | bytes 1966088 | tf_op jit(solution)/shard_map/ppermute | solution.py:254
  91.4 19.0 %collective-permute-start.5 = (f32[64,2560]{1,0:T(8,128)S(1)}, f32[64,2560]{1,0:T(8,128)S(1)}, u32[]{:S(2)}, u32[]{:S(2)}) collective-permute-start(f32[64,2560]{1,0:T(8,128)S(1)} %get-tuple-element.15.own_left), channel_id=1, source_target_pairs={{1,0},{2,1},{3,2},{4,3},{5,4},{6,5},{7,6},{8,7},{9,8},{10,9},{11,1... | collective-permute-start | bytes 1966088 | tf_op jit(solution)/shard_map/ppermute | solution.py:255
where the time goes:
time: 114 us; the launch traced here: 113 us
  waiting for transfers between devices  61.4 us (54%)
  starting transfers between devices  28.1 us (25%)
  Pallas kernels  21.1 us (19%)
  local copies, waits for them, and re-layouts  1.88 us (2%)
    ppermute x3, waiting for transfers between devices, shards(): came_right = lax.ppermute(right, 'jac', forward)  32.2 us
    all_to_all x1, waiting for transfers between devices, shards(): lax.all_to_all(dealt, ('fac', 'jac'), split_axis=0, concat_axis=0, tiled=...  14.9 us
    ppermute x3, waiting for transfers between devices, shards(): came_left = lax.ppermute(left, 'jac', backward)  14.3 us
    pallas_call x2, Pallas kernels, shards(): pl.pallas_call(functools.partial(next_kernel, last, order), out_shape=[sh...  12.5 us
    all_to_all x1, starting transfers between devices, shards(): lax.all_to_all(dealt, ('fac', 'jac'), split_axis=0, concat_axis=0, tiled=...  9.83 us
    ppermute x3, starting transfers between devices, shards(): came_left = lax.ppermute(left, 'jac', backward)  9.76 us
    ppermute x3, starting transfers between devices, shards(): came_right = lax.ppermute(right, 'jac', forward)  8.5 us
    pallas_call x1, Pallas kernels, shards(): pl.pallas_call(first_kernel, out_shape=[shape(BLK, order + support)] * 2,...  4.32 us
  transfers between devices with their start and end apart: 7, of which 7 were waited for; matrix products, arithmetic and copies ran while one was open for 0% of the time, Pallas kernels for 0%

commit v1 on v0

v1 whole, which is shorter than its diff:
```python
import functools

import jax
import jax.numpy as jnp
import numpy as np
from jax import lax
from jax.experimental import pallas as pl
from jax.experimental.pallas import tpu as pltpu
from jax.sharding import PartitionSpec as P

ROUNDS = 3
HIGH = lax.Precision.HIGHEST
BLK = 64
WIDTH = 2 * BLK
SECTIONS = 16
SUB = 8
GROUPS = BLK // SUB


def lane_ids(rows):
    return lax.broadcasted_iota(jnp.int32, (rows, WIDTH), 1)


def angles(alpha, beta, gamma):
    diff = beta - alpha
    square = diff * diff + 4.0 * gamma * gamma
    turns = square > 0
    inverse = jnp.where(turns, lax.rsqrt(jnp.where(turns, square, 1.0)), 0.0)
    along = diff * inverse
    lead = 1.0 + jnp.abs(along)
    cross = 2.0 * gamma * inverse * along
    scale = lax.rsqrt(lead * lead + cross * cross)
    return lead * scale, cross * scale


def small_rotation(gram, store, swapped):
    lanes = lane_ids(WIDTH)
    rows = lax.broadcasted_iota(jnp.int32, (WIDTH, WIDTH), 0)
    upper_half = lanes & BLK
    skew = ((rows - lanes) & (BLK - 1)) + upper_half
    store[...] = jnp.take_along_axis(gram, skew, axis=1).T
    low = lane_ids(SUB) < BLK
    aa, bb, tt, dd = [], [], [], []
    for b in range(GROUPS):
        top = store[pl.ds(b, SUB, stride=SUB), :]
        bot = store[pl.ds(BLK + b, SUB, stride=SUB), :]
        top_swap = pltpu.roll(top, BLK, 1)
        bot_swap = pltpu.roll(bot, BLK, 1)
        blocks = (
            jnp.where(low, top, top_swap),
            jnp.where(low, bot, bot_swap),
            jnp.where(low, top_swap, top),
            jnp.where(low, bot_swap, bot),
        )
        aa.append(jnp.where(swapped, blocks[3], blocks[0]))
        bb.append(jnp.where(swapped, blocks[2], blocks[1]))
        tt.append(jnp.where(swapped, blocks[1], blocks[2]))
        dd.append(jnp.where(swapped, blocks[0], blocks[3]))
    first_rows = lax.broadcasted_iota(jnp.int32, (SUB, WIDTH), 0)
    start = jnp.where(first_rows == 0, 1.0, 0.0).astype(jnp.float32)
    zero = jnp.zeros((SUB, WIDTH), jnp.float32)
    ru = [jnp.where(low, start, 0.0)] + [zero] * (GROUPS - 1)
    rl = [jnp.where(low, 0.0, start)] + [zero] * (GROUPS - 1)

    def spread(x, row):
        return jnp.broadcast_to(x[row:row + 1], (SUB, WIDTH))

    alpha, beta, gamma = spread(aa[0], 0), spread(dd[0], 0), spread(bb[0], 0)
    for section in range(SECTIONS):
        c, s = angles(alpha, beta, gamma)
        cc = [pltpu.roll(c, b, 1, stride=SUB, stride_axis=0) for b in range(GROUPS)]
        ss = [pltpu.roll(s, b, 1, stride=SUB, stride_axis=0) for b in range(GROUPS)]
        new_ru = [cc[b] * ru[b] - ss[b] * rl[b] for b in range(GROUPS)]
        new_rl = [ss[b] * ru[b] + cc[b] * rl[b] for b in range(GROUPS)]
        ru, rl = new_ru, new_rl
        if section == SECTIONS - 1:
            break
        rl = [pltpu.roll(rl[-1], 1, 0)] + rl[:-1]
        a1 = [cc[b] * aa[b] - ss[b] * bb[b] for b in range(GROUPS)]
        b1 = [ss[b] * aa[b] + cc[b] * bb[b] for b in range(GROUPS)]
        t1 = [cc[b] * tt[b] - ss[b] * dd[b] for b in range(GROUPS)]
        d1 = [ss[b] * tt[b] + cc[b] * dd[b] for b in range(GROUPS)]
        aa = [c * a1[b] - s * t1[b] for b in range(GROUPS)]
        t2 = [s * a1[b] + c * t1[b] for b in range(GROUPS)]
        b2 = [c * b1[b] - s * d1[b] for b in range(GROUPS)]
        d2 = [s * b1[b] + c * d1[b] for b in range(GROUPS)]
        new_alpha = c * (c * alpha - s * gamma) - s * (c * gamma - s * beta)
        new_beta = s * (s * alpha + c * gamma) + c * (s * gamma + c * beta)
        alpha, beta = new_alpha, pltpu.roll(new_beta, WIDTH - 1, 1)
        gamma = spread(b2[-1], SUB - 1)
        bb = [pltpu.roll(b2[-1], 1, 0)] + b2[:-1]
        t2 = t2[1:] + [pltpu.roll(t2[0], SUB - 1, 0)]
        tt = [pltpu.roll(x, WIDTH - 1, 1) for x in t2]
        dd = [pltpu.roll(x, WIDTH - 1, 1) for x in d2]
    for b in range(GROUPS):
        store[pl.ds(b, SUB, stride=SUB), :] = ru[b]
        store[pl.ds(BLK + b, SUB, stride=SUB), :] = rl[b]
    offset = jnp.where(upper_half == 0, 0, SECTIONS - 1)
    unskew = ((rows - lanes + offset) & (BLK - 1)) + upper_half
    return jnp.take_along_axis(store[...].T, unskew, axis=1)


def deal_kernel(assignment, home, stats, out):
    factors, _, order = stats.shape
    count = order // WIDTH
    for factor in range(factors):
        group = assignment[factor]
        for place in range(count):
            out[home[group * count + place]] = stats[factor, :, place * WIDTH:(place + 1) * WIDTH]


def product(a, b):
    return jnp.dot(a, b, precision=HIGH, preferred_element_type=jnp.float32)


def swap_halves(x, axis, swapped):
    return jnp.where(swapped, pltpu.roll(x, BLK, axis), x)


def leave_rotation(gram, store, place, swapped):
    rotation = small_rotation(gram, store, swapped).T
    bottom_first = jnp.logical_or(place == 0, place % 2 == 1)
    return swap_halves(rotation, 0, bottom_first)


def post(near, far, columns, block):
    near[:, columns] = block[:BLK]
    far[:, columns] = block[BLK:]


def first_kernel(me, places, work, near, far, store):
    place = places[me[0]]
    order = work.shape[0]
    straight = work[...]
    flat = straight.T
    rotation = leave_rotation(product(flat, straight), store, place, False)
    post(near, far, pl.ds(0, order), product(rotation, flat))
    post(near, far, pl.ds(order, WIDTH), rotation)


def next_kernel(order, me, places, from_near, from_far, near, far, store):
    place = places[me[0]]
    support = from_near.shape[1] - order
    swapped = place % 2 == 0
    flat = jnp.concatenate([from_near[:, :order], from_far[:, :order]], axis=0)
    rotation = leave_rotation(product(flat, flat.T), store, place, swapped)
    rotation = swap_halves(rotation, 1, swapped)
    post(near, far, pl.ds(0, order), product(rotation, flat))
    side, other = rotation[:, :BLK], rotation[:, BLK:]
    if support == WIDTH:
        post(near, far, pl.ds(order, WIDTH), product(side, from_near[:, order:]))
        post(near, far, pl.ds(order + WIDTH, WIDTH), product(other, from_far[:, order:]))
    else:
        shared = jnp.concatenate([from_near[:, order:order + WIDTH], from_far[:, order + WIDTH:]], axis=0)
        post(near, far, pl.ds(order, WIDTH), product(rotation, shared))
        post(near, far, pl.ds(order + WIDTH, WIDTH), product(side, from_near[:, order + WIDTH:]))
        post(near, far, pl.ds(order + 2 * WIDTH, WIDTH), product(other, from_far[:, order:order + WIDTH]))


def last_kernel(me, table, from_near, from_far, work, basis):
    order = work.shape[0]
    place = me[0] % table.shape[0]
    even = place % 2 == 0
    near, far = from_near[:, :order], from_far[:, :order]
    top, bottom = jnp.where(even, far, near), jnp.where(even, near, far)
    work[...] = jnp.concatenate([top, bottom], axis=0).T
    basis[...] = jnp.zeros_like(basis)
    chunks = (from_near.shape[1] - order) // WIDTH
    left_half = lane_ids(WIDTH) < BLK
    for chunk in range(chunks):
        columns = pl.ds(order + chunk * WIDTH, WIDTH)
        piece = jnp.concatenate([from_near[:, columns], from_far[:, columns]], axis=0).T
        piece = swap_halves(piece, 1, even)
        for half in range(2):
            row = pl.multiple_of(table[place, half * chunks + chunk] * WIDTH, WIDTH)
            left = jnp.logical_xor(even, half == 0)
            basis[pl.ds(row, WIDTH), :] += jnp.where(left_half == left, piece, 0.0)


def far_place(place, count):
    return min(max(place + (1 if place % 2 else -1), 0), count - 1)


def support_table(count):
    far = [far_place(p, count) for p in range(count)]
    second = [[p ^ 1, far[p]] for p in range(count)]
    third = [[p, second[p ^ 1][1], second[far[p]][0]] for p in range(count)]
    return np.array([third[p ^ 1] + third[far[p]] for p in range(count)], np.int32)


def homes(factors, count):
    return np.arange(factors * count, dtype=np.int32)


def vmem():
    return pl.BlockSpec(memory_space=pltpu.VMEM)


def smem():
    return pl.BlockSpec(memory_space=pltpu.SMEM)


PARAMS = pltpu.CompilerParams(vmem_limit_bytes=40 * 1024 * 1024)


def shape(*dims):
    return jax.ShapeDtypeStruct(dims, jnp.float32)


def shards(statistics, assignment):
    factors, slab, order = statistics.shape
    count = order // WIDTH
    devices = factors * count
    axes = ("fac", "jac")
    home = homes(factors, count)
    places = np.zeros(devices, np.int32)
    places[home] = np.arange(devices) % count
    me = lax.axis_index(axes).astype(jnp.int32).reshape(1)
    dealt = pl.pallas_call(
        deal_kernel,
        out_shape=shape(devices, slab, WIDTH),
        in_specs=[smem(), smem(), vmem()],
        out_specs=vmem(),
        compiler_params=PARAMS,
        name="deal",
    )(assignment, jnp.asarray(home), statistics)
    moved = lax.all_to_all(dealt, axes, split_axis=0, concat_axis=0, tiled=True)
    work = moved.reshape(order, WIDTH)
    places = jnp.asarray(places)
    store = pltpu.VMEM((WIDTH, WIDTH), jnp.float32)
    near, far = pl.pallas_call(
        first_kernel,
        out_shape=[shape(BLK, order + WIDTH)] * 2,
        in_specs=[smem(), smem(), vmem()],
        out_specs=[vmem()] * 2,
        scratch_shapes=[store],
        compiler_params=PARAMS,
        name="first_round",
    )(me, places, work)
    for later in range(1, ROUNDS + 1):
        goal = home if later < ROUNDS else np.arange(devices, dtype=np.int32)
        near_route, far_route = [], []
        for group in range(factors):
            for place in range(count):
                start = int(home[group * count + place])
                near_route.append((start, int(goal[group * count + (place ^ 1)])))
                far_route.append((start, int(goal[group * count + far_place(place, count)])))
        from_far = lax.ppermute(far, axes, far_route)
        from_near = lax.ppermute(near, axes, near_route)
        if later < ROUNDS:
            near, far = pl.pallas_call(
                functools.partial(next_kernel, order),
                out_shape=[shape(BLK, order + (later + 1) * WIDTH)] * 2,
                in_specs=[smem(), smem(), vmem(), vmem()],
                out_specs=[vmem()] * 2,
                scratch_shapes=[store],
                compiler_params=PARAMS,
                name="next_round",
            )(me, places, from_near, from_far)
    work, basis = pl.pallas_call(
        last_kernel,
        out_shape=[shape(order, WIDTH)] * 2,
        in_specs=[smem(), smem(), vmem(), vmem()],
        out_specs=[vmem()] * 2,
        compiler_params=PARAMS,
        name="output",
    )(me, jnp.asarray(support_table(count)), from_near, from_far)
    return work[None], basis[None]


def solution(mesh):
    return jax.shard_map(
        shards,
        mesh=mesh,
        in_specs=(P(None, ("fac", "jac"), None), P()),
        out_specs=(P("fac", None, "jac"), P("fac", None, "jac")),
        check_vma=False,
    )
```

time: 114 us -> 110 us (0.965)
  the two profiles are of different devices: /device:TPU:100 before, /device:TPU:6 now
where the time goes in v1:
time: 110 us; the launch traced here: 109 us
  waiting for transfers between devices  64.2 us (58%)
  Pallas kernels  21.9 us (20%)
  starting transfers between devices  19.9 us (18%)
  local copies, waits for them, and re-layouts  2.52 us (2%)
    ppermute x3, waiting for transfers between devices, shards(): from_near = lax.ppermute(near, axes, near_route)  34.4 us
    all_to_all x1, waiting for transfers between devices, shards(): moved = lax.all_to_all(dealt, axes, split_axis=0, concat_axis=0, tiled=True)  17.2 us
    pallas_call x2, Pallas kernels, shards(): pl.pallas_call(functools.partial(next_kernel, order), out_shape=[shape(BL...  13 us
    ppermute x3, waiting for transfers between devices, shards(): from_far = lax.ppermute(far, axes, far_route)  12.7 us
    all_to_all x1, starting transfers between devices, shards(): moved = lax.all_to_all(dealt, axes, split_axis=0, concat_axis=0, tiled=True)  10.5 us
    ppermute x3, starting transfers between devices, shards(): from_far = lax.ppermute(far, axes, far_route)  8.19 us
    pallas_call x1, Pallas kernels, shards(): pl.pallas_call(first_kernel, out_shape=[shape(BLK, order + WIDTH)] * 2, i...  4.86 us
    unnamed x8, local copies, waits for them, and re-layouts  2.52 us
  transfers between devices with their start and end apart: 7, of which 7 were waited for; matrix products, arithmetic and copies ran while one was open for 0% of the time, Pallas kernels for 0%

profile of v1, /device:TPU:6, one launch (start us, length us, event | category | flops | bytes accessed | tf_op | source)
XLA Modules:
  0.0 109.3 jit_solution(807012143463087103)
XLA Ops:
  0.6 0.0 copy-start.3
  0.6 0.6 copy-done.3
  1.3 0.0 copy-start
  1.3 1.2 %copy-done = f32[8,16,2048]{2,1,0:T(8,128)S(1)} copy-done((f32[8,16,2048]{2,1,0:T(8,128)S(1)}, f32[8,16,2048]{2,1,0:T(8,128)}, u32[]{:S(2)}) %copy-start) | copy-done | bytes 1048600
  2.5 1.7 %deal.1 = f32[128,16,128]{2,1,0:T(8,128)} custom-call(s32[8]{0:T(128)S(1)} %copy-done.3, s32[128]{0:T(128)S(1)} %call_exported.0.home, f32[8,16,2048]{2,1,0:T(8,128)S(1)} %copy-done), custom_call_target="tpu_custom_call" | custom-call | tf_op jit(solution)/shard_map/deal/pallas_call | solution.py:219
  4.2 10.5 %all-to-all-start = ((f32[128,16,128]{2,1,0:T(8,128)}), f32[128,16,128]{2,1,0:T(8,128)S(1)}, u32[]{:S(2)}, u32[]{:S(2)}) async-start(f32[128,16,128]{2,1,0:T(8,128)} %deal.1), calls=%async_computation | async-start | bytes 2097152 | tf_op jit(solution)/shard_map/all_to_all | solution.py:227
  14.7 17.2 %all-to-all-done = f32[128,16,128]{2,1,0:T(8,128)S(1)} async-done(((f32[128,16,128]{2,1,0:T(8,128)}), f32[128,16,128]{2,1,0:T(8,128)S(1)}, u32[]{:S(2)}, u32[]{:S(2)}) %all-to-all-start) | async-done | bytes 1048608 | tf_op jit(solution)/shard_map/all_to_all | solution.py:227
  31.9 0.0 copy-start.2
  31.9 0.7 copy-done.2
  32.5 4.9 %first_round.1 = (f32[64,2176]{1,0:T(8,128)S(1)}, f32[64,2176]{1,0:T(8,128)S(1)}) custom-call(s32[1]{0:T(128)} %bitcast.me, s32[128]{0:T(128)S(1)} %copy-done.2, f32[2048,128]{1,0:T(8,128)S(1)} %bitcast.4), custom_call_target="tpu_custom_call" | custom-call | tf_op jit(solution)/shard_map/first_round/pallas_call | solution.py:231
  37.4 1.1 collective-permute-start
  38.5 3.3 %collective-permute-start.1 = (f32[64,2176]{1,0:T(8,128)S(1)}, f32[64,2176]{1,0:T(8,128)S(1)}, u32[]{:S(2)}, u32[]{:S(2)}) collective-permute-start(f32[64,2176]{1,0:T(8,128)S(1)} %get-tuple-element.11), channel_id=1, source_target_pairs={{0,0},{1,2},{2,1},{3,4},{4,3},{5,6},{6,5},{7,8},{8,7},{9,10},{10,9... | collective-permute-start | bytes 1671176 | tf_op jit(solution)/shard_map/ppermute | solution.py:248
  41.8 10.6 %collective-permute-done.from_near = f32[64,2176]{1,0:T(8,128)S(1)} collective-permute-done((f32[64,2176]{1,0:T(8,128)S(1)}, f32[64,2176]{1,0:T(8,128)S(1)}, u32[]{:S(2)}, u32[]{:S(2)}) %collective-permute-start) | collective-permute-done | bytes 557088 | tf_op jit(solution)/shard_map/ppermute | solution.py:249
  52.4 4.6 %collective-permute-done.1.from_far = f32[64,2176]{1,0:T(8,128)S(1)} collective-permute-done((f32[64,2176]{1,0:T(8,128)S(1)}, f32[64,2176]{1,0:T(8,128)S(1)}, u32[]{:S(2)}, u32[]{:S(2)}) %collective-permute-start.1) | collective-permute-done | bytes 557088 | tf_op jit(solution)/shard_map/ppermute | solution.py:248
  57.0 6.5 %next_round.2 = (f32[64,2304]{1,0:T(8,128)S(1)}, f32[64,2304]{1,0:T(8,128)S(1)}) custom-call(s32[1]{0:T(128)} %bitcast.me, s32[128]{0:T(128)S(1)} %copy-done.2, f32[64,2176]{1,0:T(8,128)S(1)} %collective-permute-done.from_near, f32[64,2176]{1,0:T(8,128)S(1)} %collective-permute-done.1.from_far), custom_call_target="tpu_custom_call" | custom-call | tf_op jit(solution)/shard_map/next_round/pallas_call | solution.py:251
  63.5 0.1 collective-permute-start.2
  63.6 2.4 %collective-permute-start.3 = (f32[64,2304]{1,0:T(8,128)S(1)}, f32[64,2304]{1,0:T(8,128)S(1)}, u32[]{:S(2)}, u32[]{:S(2)}) collective-permute-start(f32[64,2304]{1,0:T(8,128)S(1)} %get-tuple-element.13), channel_id=1, source_target_pairs={{0,0},{1,2},{2,1},{3,4},{4,3},{5,6},{6,5},{7,8},{8,7},{9,10},{10,9... | collective-permute-start | bytes 1769480 | tf_op jit(solution)/shard_map/ppermute | solution.py:248
  66.0 12.0 %collective-permute-done.2.from_near = f32[64,2304]{1,0:T(8,128)S(1)} collective-permute-done((f32[64,2304]{1,0:T(8,128)S(1)}, f32[64,2304]{1,0:T(8,128)S(1)}, u32[]{:S(2)}, u32[]{:S(2)}) %collective-permute-start.2) | collective-permute-done | bytes 589856 | tf_op jit(solution)/shard_map/ppermute | solution.py:249
  78.1 4.0 %collective-permute-done.3.from_far = f32[64,2304]{1,0:T(8,128)S(1)} collective-permute-done((f32[64,2304]{1,0:T(8,128)S(1)}, f32[64,2304]{1,0:T(8,128)S(1)}, u32[]{:S(2)}, u32[]{:S(2)}) %collective-permute-start.3) | collective-permute-done | bytes 589856 | tf_op jit(solution)/shard_map/ppermute | solution.py:248
  82.1 0.0 copy-start.1
  82.1 6.6 %next_round.3 = (f32[64,2432]{1,0:T(8,128)S(1)}, f32[64,2432]{1,0:T(8,128)S(1)}) custom-call(s32[1]{0:T(128)} %bitcast.me, s32[128]{0:T(128)S(1)} %copy-done.2, f32[64,2304]{1,0:T(8,128)S(1)} %collective-permute-done.2.from_near, f32[64,2304]{1,0:T(8,128)S(1)} %collective-permute-done.3.from_far), custom_call_target="tpu_custom_call" | custom-call | tf_op jit(solution)/shard_map/next_round/pallas_call | solution.py:251
  88.6 0.1 collective-permute-start.4
  88.7 2.5 %collective-permute-start.5 = (f32[64,2432]{1,0:T(8,128)S(1)}, f32[64,2432]{1,0:T(8,128)S(1)}, u32[]{:S(2)}, u32[]{:S(2)}) collective-permute-start(f32[64,2432]{1,0:T(8,128)S(1)} %get-tuple-element.15), channel_id=1, source_target_pairs={{0,0},{1,2},{2,1},{3,4},{4,3},{5,6},{6,5},{7,8},{8,7},{9,10},{10,9... | collective-permute-start | bytes 1867784 | tf_op jit(solution)/shard_map/ppermute | solution.py:248
  91.2 11.7 %collective-permute-done.4.from_near = f32[64,2432]{1,0:T(8,128)S(1)} collective-permute-done((f32[64,2432]{1,0:T(8,128)S(1)}, f32[64,2432]{1,0:T(8,128)S(1)}, u32[]{:S(2)}, u32[]{:S(2)}) %collective-permute-start.4) | collective-permute-done | bytes 622624 | tf_op jit(solution)/shard_map/ppermute | solution.py:249
  102.9 4.0 %collective-permute-done.5.from_far = f32[64,2432]{1,0:T(8,128)S(1)} collective-permute-done((f32[64,2432]{1,0:T(8,128)S(1)}, f32[64,2432]{1,0:T(8,128)S(1)}, u32[]{:S(2)}, u32[]{:S(2)}) %collective-permute-start.5) | collective-permute-done | bytes 622624 | tf_op jit(solution)/shard_map/ppermute | solution.py:248
  107.0 0.0 copy-done.1
  107.0 2.4 %output.1 = (f32[2048,128]{1,0:T(8,128)}, f32[2048,128]{1,0:T(8,128)}) custom-call(s32[1]{0:T(128)} %bitcast.me, s32[16,6]{1,0:T(8,128)S(1)} %copy-done.1, f32[64,2432]{1,0:T(8,128)S(1)} %collective-permute-done.4.from_near, f32[64,2432]{1,0:T(8,128)S(1)} %collective-permute-done.5.from_far), custom_call_target="tpu_custom_call" | custom-call | tf_op jit(solution)/shard_map/output/pallas_call | solution.py:260
  (1 shorter events, 0.0 us)
Async XLA Ops:
  0.6 0.7 copy-start.3
  1.3 1.2 %copy-start = (f32[8,16,2048]{2,1,0:T(8,128)S(1)}, f32[8,16,2048]{2,1,0:T(8,128)}, u32[]{:S(2)}) copy-start(f32[8,16,2048]{2,1,0:T(8,128)} %stats.1) | copy-start | bytes 3145732
  4.2 27.7 %all-to-all-start = ((f32[128,16,128]{2,1,0:T(8,128)}), f32[128,16,128]{2,1,0:T(8,128)S(1)}, u32[]{:S(2)}, u32[]{:S(2)}) async-start(f32[128,16,128]{2,1,0:T(8,128)} %deal.1), calls=%async_computation | async-start | bytes 2097152 | tf_op jit(solution)/shard_map/all_to_all | solution.py:227
  31.9 0.7 copy-start.2
  37.4 15.0 %collective-permute-start = (f32[64,2176]{1,0:T(8,128)S(1)}, f32[64,2176]{1,0:T(8,128)S(1)}, u32[]{:S(2)}, u32[]{:S(2)}) collective-permute-start(f32[64,2176]{1,0:T(8,128)S(1)} %get-tuple-element.10), channel_id=1, source_target_pairs={{0,1},{1,0},{2,3},{3,2},{4,5},{5,4},{6,7},{7,6},{8,9},{9,8},{10,11... | collective-permute-start | bytes 1671176 | tf_op jit(solution)/shard_map/ppermute | solution.py:249
  38.5 18.6 %collective-permute-start.1 = (f32[64,2176]{1,0:T(8,128)S(1)}, f32[64,2176]{1,0:T(8,128)S(1)}, u32[]{:S(2)}, u32[]{:S(2)}) collective-permute-start(f32[64,2176]{1,0:T(8,128)S(1)} %get-tuple-element.11), channel_id=1, source_target_pairs={{0,0},{1,2},{2,1},{3,4},{4,3},{5,6},{6,5},{7,8},{8,7},{9,10},{10,9... | collective-permute-start | bytes 1671176 | tf_op jit(solution)/shard_map/ppermute | solution.py:248
  63.5 14.5 %collective-permute-start.2 = (f32[64,2304]{1,0:T(8,128)S(1)}, f32[64,2304]{1,0:T(8,128)S(1)}, u32[]{:S(2)}, u32[]{:S(2)}) collective-permute-start(f32[64,2304]{1,0:T(8,128)S(1)} %get-tuple-element.12), channel_id=1, source_target_pairs={{0,1},{1,0},{2,3},{3,2},{4,5},{5,4},{6,7},{7,6},{8,9},{9,8},{10,11... | collective-permute-start | bytes 1769480 | tf_op jit(solution)/shard_map/ppermute | solution.py:249
  63.6 18.4 %collective-permute-start.3 = (f32[64,2304]{1,0:T(8,128)S(1)}, f32[64,2304]{1,0:T(8,128)S(1)}, u32[]{:S(2)}, u32[]{:S(2)}) collective-permute-start(f32[64,2304]{1,0:T(8,128)S(1)} %get-tuple-element.13), channel_id=1, source_target_pairs={{0,0},{1,2},{2,1},{3,4},{4,3},{5,6},{6,5},{7,8},{8,7},{9,10},{10,9... | collective-permute-start | bytes 1769480 | tf_op jit(solution)/shard_map/ppermute | solution.py:248
  82.1 24.9 %copy-start.1 = (s32[16,6]{1,0:T(8,128)S(1)}, s32[16,6]{1,0:T(8,128)}, u32[]{:S(2)}) copy-start(s32[16,6]{1,0:T(8,128)} %constant.18.clone.table) | copy-start | bytes 1156
  88.6 14.3 %collective-permute-start.4 = (f32[64,2432]{1,0:T(8,128)S(1)}, f32[64,2432]{1,0:T(8,128)S(1)}, u32[]{:S(2)}, u32[]{:S(2)}) collective-permute-start(f32[64,2432]{1,0:T(8,128)S(1)} %get-tuple-element.14), channel_id=1, source_target_pairs={{0,1},{1,0},{2,3},{3,2},{4,5},{5,4},{6,7},{7,6},{8,9},{9,8},{10,11... | collective-permute-start | bytes 1867784 | tf_op jit(solution)/shard_map/ppermute | solution.py:249
  88.7 18.2 %collective-permute-start.5 = (f32[64,2432]{1,0:T(8,128)S(1)}, f32[64,2432]{1,0:T(8,128)S(1)}, u32[]{:S(2)}, u32[]{:S(2)}) collective-permute-start(f32[64,2432]{1,0:T(8,128)S(1)} %get-tuple-element.15), channel_id=1, source_target_pairs={{0,0},{1,2},{2,1},{3,4},{4,3},{5,6},{6,5},{7,8},{8,7},{9,10},{10,9... | collective-permute-start | bytes 1867784 | tf_op jit(solution)/shard_map/ppermute | solution.py:248

commit v2 on v1

--- a/solution.py
+++ b/solution.py
@@ -9,7 +9,7 @@
 from jax.sharding import PartitionSpec as P
 
 ROUNDS = 3
-HIGH = lax.Precision.HIGHEST
+CHUNK = 512
 BLK = 64
 WIDTH = 2 * BLK
 SECTIONS = 16
@@ -109,8 +109,41 @@
             out[home[group * count + place]] = stats[factor, :, place * WIDTH:(place + 1) * WIDTH]
 
 
-def product(a, b):
-    return jnp.dot(a, b, precision=HIGH, preferred_element_type=jnp.float32)
+def pieces(x):
+    high = x.astype(jnp.bfloat16)
+    rest = x - high.astype(jnp.float32)
+    middle = rest.astype(jnp.bfloat16)
+    low = (rest - middle.astype(jnp.float32)).astype(jnp.bfloat16)
+    return high, middle, low
+
+
+def gram_of(parts):
+    high, middle, low = parts
+    left = jnp.concatenate([high, middle, low], axis=0)
+    right = jnp.concatenate([high, middle], axis=0)
+    full = lax.dot_general(left, right, (((1,), (1,)), ((), ())), preferred_element_type=jnp.float32)
+    crossed = full[2 * WIDTH:, :WIDTH]
+    small = full[WIDTH:2 * WIDTH, WIDTH:] + (crossed + crossed.T)
+    return full[:WIDTH, :WIDTH] + (full[:WIDTH, WIDTH:] + full[WIDTH:2 * WIDTH, :WIDTH] + small)
+
+
+def apply(rotation, parts, near, far, start, exact):
+    high, middle, low = pieces(rotation)
+    first = jnp.concatenate(
+        [jnp.concatenate([high, middle], axis=1), jnp.concatenate([middle, high], axis=1)], axis=0
+    )
+    last = jnp.concatenate([low, high], axis=1)
+    total = parts[0].shape[1]
+    for begin in range(0, total, CHUNK):
+        end = min(begin + CHUNK, total)
+        part = [x[:, begin:end] for x in parts]
+        both = jnp.dot(first, jnp.concatenate(part[:2], axis=0), preferred_element_type=jnp.float32)
+        small = both[WIDTH:]
+        if exact:
+            small = small + jnp.dot(
+                last, jnp.concatenate([part[0], part[2]], axis=0), preferred_element_type=jnp.float32
+            )
+        post(near, far, pl.ds(start + begin, end - begin), both[:WIDTH] + small)
 
 
 def swap_halves(x, axis, swapped):
@@ -131,30 +164,28 @@
 def first_kernel(me, places, work, near, far, store):
     place = places[me[0]]
     order = work.shape[0]
-    straight = work[...]
-    flat = straight.T
-    rotation = leave_rotation(product(flat, straight), store, place, False)
-    post(near, far, pl.ds(0, order), product(rotation, flat))
+    parts = pieces(work[...].T)
+    rotation = leave_rotation(gram_of(parts), store, place, False)
+    apply(rotation, parts, near, far, 0, True)
     post(near, far, pl.ds(order, WIDTH), rotation)
 
 
-def next_kernel(order, me, places, from_near, from_far, near, far, store):
+def next_kernel(order, final, me, places, from_near, from_far, near, far, store):
     place = places[me[0]]
-    support = from_near.shape[1] - order
     swapped = place % 2 == 0
-    flat = jnp.concatenate([from_near[:, :order], from_far[:, :order]], axis=0)
-    rotation = leave_rotation(product(flat, flat.T), store, place, swapped)
+    parts = pieces(jnp.concatenate([from_near[:, :order], from_far[:, :order]], axis=0))
+    rotation = leave_rotation(gram_of(parts), store, place, swapped)
     rotation = swap_halves(rotation, 1, swapped)
-    post(near, far, pl.ds(0, order), product(rotation, flat))
-    side, other = rotation[:, :BLK], rotation[:, BLK:]
-    if support == WIDTH:
-        post(near, far, pl.ds(order, WIDTH), product(side, from_near[:, order:]))
-        post(near, far, pl.ds(order + WIDTH, WIDTH), product(other, from_far[:, order:]))
+    apply(rotation, parts, near, far, 0, not final)
+    blank = jnp.zeros((BLK, WIDTH), jnp.float32)
+    near_basis = [from_near[:, c:c + WIDTH] for c in range(order, from_near.shape[1], WIDTH)]
+    far_basis = [from_far[:, c:c + WIDTH] for c in range(order, from_far.shape[1], WIDTH)]
+    if final:
+        near_basis, far_basis = near_basis + [blank], [far_basis[1], blank, far_basis[0]]
     else:
-        shared = jnp.concatenate([from_near[:, order:order + WIDTH], from_far[:, order + WIDTH:]], axis=0)
-        post(near, far, pl.ds(order, WIDTH), product(rotation, shared))
-        post(near, far, pl.ds(order + WIDTH, WIDTH), product(side, from_near[:, order + WIDTH:]))
-        post(near, far, pl.ds(order + 2 * WIDTH, WIDTH), product(other, from_far[:, order:order + WIDTH]))
+        near_basis, far_basis = near_basis + [blank], [blank] + far_basis
+    columns = [jnp.concatenate(halves, axis=0) for halves in zip(near_basis, far_basis)]
+    apply(rotation, pieces(jnp.concatenate(columns, axis=1)), near, far, order, False)
 
 
 def last_kernel(me, table, from_near, from_far, work, basis):
@@ -188,8 +219,17 @@
     return np.array([third[p ^ 1] + third[far[p]] for p in range(count)], np.int32)
 
 
+PAIR_Z = (((1, 0), (3, 2)), ((3, 2), (1, 0)))
+
+
 def homes(factors, count):
-    return np.arange(factors * count, dtype=np.int32)
+    home = np.zeros(factors * count, np.int32)
+    for group in range(factors):
+        for place in range(count):
+            x, pair, core = place // 4, place % 4 // 2, place % 2
+            z = PAIR_Z[x % 2][group % 2][pair]
+            home[group * count + place] = (group // 2 * 2 + core) * count + 4 * x + z
+    return home
 
 
 def vmem():
@@ -249,7 +289,7 @@
         from_near = lax.ppermute(near, axes, near_route)
         if later < ROUNDS:
             near, far = pl.pallas_call(
-                functools.partial(next_kernel, order),
+                functools.partial(next_kernel, order, later == ROUNDS - 1),
                 out_shape=[shape(BLK, order + (later + 1) * WIDTH)] * 2,
                 in_specs=[smem(), smem(), vmem(), vmem()],
                 out_specs=[vmem()] * 2,

time: 110 us -> 103 us (0.936)
  the two profiles are of different devices: /device:TPU:6 before, /device:TPU:0 now
where the time goes in v2:
time: 103 us; the launch traced here: 102 us
  waiting for transfers between devices  59.1 us (57%)
  starting transfers between devices  20.7 us (20%)
  Pallas kernels  18.5 us (18%)
  local copies, waits for them, and re-layouts  3.19 us (3%)
    ppermute x3, waiting for transfers between devices, shards(): from_near = lax.ppermute(near, axes, near_route)  22.2 us
    all_to_all x1, waiting for transfers between devices, shards(): moved = lax.all_to_all(dealt, axes, split_axis=0, concat_axis=0, tiled=True)  19 us
    ppermute x3, waiting for transfers between devices, shards(): from_far = lax.ppermute(far, axes, far_route)  17.8 us
    all_to_all x1, starting transfers between devices, shards(): moved = lax.all_to_all(dealt, axes, split_axis=0, concat_axis=0, tiled=True)  11.1 us
    pallas_call x2, Pallas kernels, shards(): pl.pallas_call(functools.partial(next_kernel, order, later == ROUNDS - 1)...  9.6 us
    ppermute x3, starting transfers between devices, shards(): from_far = lax.ppermute(far, axes, far_route)  4.91 us
    pallas_call x1, Pallas kernels, shards(): pl.pallas_call(first_kernel, out_shape=[shape(BLK, order + WIDTH)] * 2, i...  4.88 us
    ppermute x3, starting transfers between devices, shards(): from_near = lax.ppermute(near, axes, near_route)  4.68 us
  transfers between devices with their start and end apart: 7, of which 5 were waited for; matrix products, arithmetic and copies ran while one was open for 0% of the time, Pallas kernels for 0%

profile of v2, /device:TPU:0, one launch (start us, length us, event | category | flops | bytes accessed | tf_op | source)
XLA Modules:
  0.0 102.3 jit_solution(7844102296652114282)
XLA Ops:
  0.6 0.0 copy-start.4
  0.6 0.6 copy-done.4
  1.3 0.0 copy-start
  1.3 1.2 %copy-done = f32[8,16,2048]{2,1,0:T(8,128)S(1)} copy-done((f32[8,16,2048]{2,1,0:T(8,128)S(1)}, f32[8,16,2048]{2,1,0:T(8,128)}, u32[]{:S(2)}) %copy-start) | copy-done | bytes 1048600
  2.5 0.0 copy-start.3
  2.5 0.7 copy-done.3
  3.2 1.7 %deal.1 = f32[128,16,128]{2,1,0:T(8,128)} custom-call(s32[8]{0:T(128)S(1)} %copy-done.3, s32[128]{0:T(128)S(1)} %copy-done.4, f32[8,16,2048]{2,1,0:T(8,128)S(1)} %copy-done), custom_call_target="tpu_custom_call" | custom-call | tf_op jit(solution)/shard_map/deal/pallas_call | solution.py:259
  4.8 11.1 %all-to-all-start = ((f32[128,16,128]{2,1,0:T(8,128)}), f32[128,16,128]{2,1,0:T(8,128)S(1)}, u32[]{:S(2)}, u32[]{:S(2)}) async-start(f32[128,16,128]{2,1,0:T(8,128)} %deal.1), calls=%async_computation | async-start | bytes 2097152 | tf_op jit(solution)/shard_map/all_to_all | solution.py:267
  16.0 19.0 %all-to-all-done = f32[128,16,128]{2,1,0:T(8,128)S(1)} async-done(((f32[128,16,128]{2,1,0:T(8,128)}), f32[128,16,128]{2,1,0:T(8,128)S(1)}, u32[]{:S(2)}, u32[]{:S(2)}) %all-to-all-start) | async-done | bytes 1048608 | tf_op jit(solution)/shard_map/all_to_all | solution.py:267
  35.0 0.0 copy-start.2
  35.0 0.7 copy-done.2
  35.7 4.9 %first_round.1 = (f32[64,2176]{1,0:T(8,128)S(1)}, f32[64,2176]{1,0:T(8,128)S(1)}) custom-call(s32[1]{0:T(128)} %bitcast.me, s32[128]{0:T(128)S(1)} %copy-done.2, f32[2048,128]{1,0:T(8,128)S(1)} %bitcast.4), custom_call_target="tpu_custom_call" | custom-call | tf_op jit(solution)/shard_map/first_round/pallas_call | solution.py:271
  40.6 0.1 collective-permute-start
  40.7 2.9 %collective-permute-start.1 = (f32[64,2176]{1,0:T(8,128)S(1)}, f32[64,2176]{1,0:T(8,128)S(1)}, u32[]{:S(2)}, u32[]{:S(2)}) collective-permute-start(f32[64,2176]{1,0:T(8,128)S(1)} %get-tuple-element.11), channel_id=1, source_target_pairs={{1,1},{17,0},{0,17},{16,7},{7,16},{23,6},{6,23},{22,9},{9,22},{25,... | collective-permute-start | bytes 1671176 | tf_op jit(solution)/shard_map/ppermute | solution.py:288
  43.6 0.0 collective-permute-done.from_near
  43.6 7.9 %collective-permute-done.1.from_far = f32[64,2176]{1,0:T(8,128)S(1)} collective-permute-done((f32[64,2176]{1,0:T(8,128)S(1)}, f32[64,2176]{1,0:T(8,128)S(1)}, u32[]{:S(2)}, u32[]{:S(2)}) %collective-permute-start.1) | collective-permute-done | bytes 557088 | tf_op jit(solution)/shard_map/ppermute | solution.py:288
  51.5 4.9 %next_round.2 = (f32[64,2304]{1,0:T(8,128)S(1)}, f32[64,2304]{1,0:T(8,128)S(1)}) custom-call(s32[1]{0:T(128)} %bitcast.me, s32[128]{0:T(128)S(1)} %copy-done.2, f32[64,2176]{1,0:T(8,128)S(1)} %collective-permute-done.from_near, f32[64,2176]{1,0:T(8,128)S(1)} %collective-permute-done.1.from_far), custom_call_target="tpu_custom_call" | custom-call | tf_op jit(solution)/shard_map/next_round/pallas_call | solution.py:291
  56.5 2.7 %collective-permute-start.2 = (f32[64,2304]{1,0:T(8,128)S(1)}, f32[64,2304]{1,0:T(8,128)S(1)}, u32[]{:S(2)}, u32[]{:S(2)}) collective-permute-start(f32[64,2304]{1,0:T(8,128)S(1)} %get-tuple-element.12), channel_id=1, source_target_pairs={{1,17},{17,1},{0,16},{16,0},{7,23},{23,7},{6,22},{22,6},{9,25},{25... | collective-permute-start | bytes 1769480 | tf_op jit(solution)/shard_map/ppermute | solution.py:289
  59.1 1.9 %collective-permute-start.3 = (f32[64,2304]{1,0:T(8,128)S(1)}, f32[64,2304]{1,0:T(8,128)S(1)}, u32[]{:S(2)}, u32[]{:S(2)}) collective-permute-start(f32[64,2304]{1,0:T(8,128)S(1)} %get-tuple-element.13), channel_id=1, source_target_pairs={{1,1},{17,0},{0,17},{16,7},{7,16},{23,6},{6,23},{22,9},{9,22},{25,... | collective-permute-start | bytes 1769480 | tf_op jit(solution)/shard_map/ppermute | solution.py:288
  61.1 0.0 collective-permute-done.2.from_near
  61.1 9.3 %collective-permute-done.3.from_far = f32[64,2304]{1,0:T(8,128)S(1)} collective-permute-done((f32[64,2304]{1,0:T(8,128)S(1)}, f32[64,2304]{1,0:T(8,128)S(1)}, u32[]{:S(2)}, u32[]{:S(2)}) %collective-permute-start.3) | collective-permute-done | bytes 589856 | tf_op jit(solution)/shard_map/ppermute | solution.py:288
  70.3 0.0 copy-start.1
  70.3 4.7 %next_round.3 = (f32[64,2432]{1,0:T(8,128)S(1)}, f32[64,2432]{1,0:T(8,128)S(1)}) custom-call(s32[1]{0:T(128)} %bitcast.me, s32[128]{0:T(128)S(1)} %copy-done.2, f32[64,2304]{1,0:T(8,128)S(1)} %collective-permute-done.2.from_near, f32[64,2304]{1,0:T(8,128)S(1)} %collective-permute-done.3.from_far), custom_call_target="tpu_custom_call" | custom-call | tf_op jit(solution)/shard_map/next_round/pallas_call | solution.py:291
  75.0 1.9 %collective-permute-start.4 = (f32[64,2432]{1,0:T(8,128)S(1)}, f32[64,2432]{1,0:T(8,128)S(1)}, u32[]{:S(2)}, u32[]{:S(2)}) collective-permute-start(f32[64,2432]{1,0:T(8,128)S(1)} %get-tuple-element.14), channel_id=1, source_target_pairs={{1,1},{17,0},{0,3},{16,2},{7,5},{23,4},{6,7},{22,6},{9,9},{25,8},{... | collective-permute-start | bytes 1867784 | tf_op jit(solution)/shard_map/ppermute | solution.py:289
  76.9 0.1 collective-permute-start.5
  77.0 22.2 %collective-permute-done.4.from_near = f32[64,2432]{1,0:T(8,128)S(1)} collective-permute-done((f32[64,2432]{1,0:T(8,128)S(1)}, f32[64,2432]{1,0:T(8,128)S(1)}, u32[]{:S(2)}, u32[]{:S(2)}) %collective-permute-start.4) | collective-permute-done | bytes 622624 | tf_op jit(solution)/shard_map/ppermute | solution.py:289
  99.3 0.6 collective-permute-done.5.from_far
  99.9 0.0 copy-done.1
  99.9 2.4 %output.1 = (f32[2048,128]{1,0:T(8,128)}, f32[2048,128]{1,0:T(8,128)}) custom-call(s32[1]{0:T(128)} %bitcast.me, s32[16,6]{1,0:T(8,128)S(1)} %copy-done.1, f32[64,2432]{1,0:T(8,128)S(1)} %collective-permute-done.4.from_near, f32[64,2432]{1,0:T(8,128)S(1)} %collective-permute-done.5.from_far), custom_call_target="tpu_custom_call" | custom-call | tf_op jit(solution)/shard_map/output/pallas_call | solution.py:300
Async XLA Ops:
  0.6 0.7 copy-start.4
  1.3 1.2 %copy-start = (f32[8,16,2048]{2,1,0:T(8,128)S(1)}, f32[8,16,2048]{2,1,0:T(8,128)}, u32[]{:S(2)}) copy-start(f32[8,16,2048]{2,1,0:T(8,128)} %stats.1) | copy-start | bytes 3145732
  2.5 0.7 copy-start.3
  4.8 30.2 %all-to-all-start = ((f32[128,16,128]{2,1,0:T(8,128)}), f32[128,16,128]{2,1,0:T(8,128)S(1)}, u32[]{:S(2)}, u32[]{:S(2)}) async-start(f32[128,16,128]{2,1,0:T(8,128)} %deal.1), calls=%async_computation | async-start | bytes 2097152 | tf_op jit(solution)/shard_map/all_to_all | solution.py:267
  35.0 0.7 copy-start.2
  40.6 3.0 %collective-permute-start = (f32[64,2176]{1,0:T(8,128)S(1)}, f32[64,2176]{1,0:T(8,128)S(1)}, u32[]{:S(2)}, u32[]{:S(2)}) collective-permute-start(f32[64,2176]{1,0:T(8,128)S(1)} %get-tuple-element.10), channel_id=1, source_target_pairs={{1,17},{17,1},{0,16},{16,0},{7,23},{23,7},{6,22},{22,6},{9,25},{25... | collective-permute-start | bytes 1671176 | tf_op jit(solution)/shard_map/ppermute | solution.py:289
  40.7 10.9 %collective-permute-start.1 = (f32[64,2176]{1,0:T(8,128)S(1)}, f32[64,2176]{1,0:T(8,128)S(1)}, u32[]{:S(2)}, u32[]{:S(2)}) collective-permute-start(f32[64,2176]{1,0:T(8,128)S(1)} %get-tuple-element.11), channel_id=1, source_target_pairs={{1,1},{17,0},{0,17},{16,7},{7,16},{23,6},{6,23},{22,9},{9,22},{25,... | collective-permute-start | bytes 1671176 | tf_op jit(solution)/shard_map/ppermute | solution.py:288
  56.5 4.6 %collective-permute-start.2 = (f32[64,2304]{1,0:T(8,128)S(1)}, f32[64,2304]{1,0:T(8,128)S(1)}, u32[]{:S(2)}, u32[]{:S(2)}) collective-permute-start(f32[64,2304]{1,0:T(8,128)S(1)} %get-tuple-element.12), channel_id=1, source_target_pairs={{1,17},{17,1},{0,16},{16,0},{7,23},{23,7},{6,22},{22,6},{9,25},{25... | collective-permute-start | bytes 1769480 | tf_op jit(solution)/shard_map/ppermute | solution.py:289
  59.1 11.2 %collective-permute-start.3 = (f32[64,2304]{1,0:T(8,128)S(1)}, f32[64,2304]{1,0:T(8,128)S(1)}, u32[]{:S(2)}, u32[]{:S(2)}) collective-permute-start(f32[64,2304]{1,0:T(8,128)S(1)} %get-tuple-element.13), channel_id=1, source_target_pairs={{1,1},{17,0},{0,17},{16,7},{7,16},{23,6},{6,23},{22,9},{9,22},{25,... | collective-permute-start | bytes 1769480 | tf_op jit(solution)/shard_map/ppermute | solution.py:288
  70.3 29.6 %copy-start.1 = (s32[16,6]{1,0:T(8,128)S(1)}, s32[16,6]{1,0:T(8,128)}, u32[]{:S(2)}) copy-start(s32[16,6]{1,0:T(8,128)} %constant.19.clone.table) | copy-start | bytes 1156
  75.0 24.3 %collective-permute-start.4 = (f32[64,2432]{1,0:T(8,128)S(1)}, f32[64,2432]{1,0:T(8,128)S(1)}, u32[]{:S(2)}, u32[]{:S(2)}) collective-permute-start(f32[64,2432]{1,0:T(8,128)S(1)} %get-tuple-element.14), channel_id=1, source_target_pairs={{1,1},{17,0},{0,3},{16,2},{7,5},{23,4},{6,7},{22,6},{9,9},{25,8},{... | collective-permute-start | bytes 1867784 | tf_op jit(solution)/shard_map/ppermute | solution.py:289
  76.9 23.0 %collective-permute-start.5 = (f32[64,2432]{1,0:T(8,128)S(1)}, f32[64,2432]{1,0:T(8,128)S(1)}, u32[]{:S(2)}, u32[]{:S(2)}) collective-permute-start(f32[64,2432]{1,0:T(8,128)S(1)} %get-tuple-element.15), channel_id=1, source_target_pairs={{1,0},{17,2},{0,1},{16,4},{7,3},{23,6},{6,5},{22,8},{9,7},{25,10},... | collective-permute-start | bytes 1867784 | tf_op jit(solution)/shard_map/ppermute | solution.py:288

commit v3 on v2

--- a/solution.py
+++ b/solution.py
@@ -10,6 +10,10 @@
 
 ROUNDS = 3
 CHUNK = 512
+CHAINS = (
+    ((0, 1), (1, 1), (1, 0), (1, 3), (2, 3), (2, 0), (3, 0), (3, 3)),
+    ((0, 0), (0, 3), (0, 2), (1, 2), (2, 2), (2, 1), (3, 1), (3, 2)),
+)
 BLK = 64
 WIDTH = 2 * BLK
 SECTIONS = 16
@@ -100,13 +104,23 @@
     return jnp.take_along_axis(store[...].T, unskew, axis=1)
 
 
-def deal_kernel(assignment, home, stats, out):
+def deal_kernel(assignment, stats, out, owners, slabs, sems):
     factors, _, order = stats.shape
     count = order // WIDTH
+    copies = [pltpu.make_async_copy(stats.at[f], slabs.at[f], sems.at[f]) for f in range(factors)]
+    for copy in copies:
+        copy.start()
+    table = pltpu.make_async_copy(assignment, owners, sems.at[factors])
+    table.start()
+    table.wait()
     for factor in range(factors):
-        group = assignment[factor]
+        group = owners[factor]
+        odd = group % 2 == 1
+        base = group // 2 * (2 * count)
+        copies[factor].wait()
         for place in range(count):
-            out[home[group * count + place]] = stats[factor, :, place * WIDTH:(place + 1) * WIDTH]
+            home = base + jnp.where(odd, home_of(1, place, count), home_of(0, place, count))
+            out[home] = slabs[factor, :, place * WIDTH:(place + 1) * WIDTH]
 
 
 def pieces(x):
@@ -161,7 +175,7 @@
     far[:, columns] = block[BLK:]
 
 
-def first_kernel(me, places, work, near, far, store):
+def first_kernel(me, places, work, far, near, store):
     place = places[me[0]]
     order = work.shape[0]
     parts = pieces(work[...].T)
@@ -170,7 +184,7 @@
     post(near, far, pl.ds(order, WIDTH), rotation)
 
 
-def next_kernel(order, final, me, places, from_near, from_far, near, far, store):
+def next_kernel(order, final, me, places, from_far, from_near, far, near, store):
     place = places[me[0]]
     swapped = place % 2 == 0
     parts = pieces(jnp.concatenate([from_near[:, :order], from_far[:, :order]], axis=0))
@@ -188,14 +202,11 @@
     apply(rotation, pieces(jnp.concatenate(columns, axis=1)), near, far, order, False)
 
 
-def last_kernel(me, table, from_near, from_far, work, basis):
+def last_kernel(me, table, from_far, from_near, work, basis, work_store, basis_store, sems):
     order = work.shape[0]
     place = me[0] % table.shape[0]
     even = place % 2 == 0
-    near, far = from_near[:, :order], from_far[:, :order]
-    top, bottom = jnp.where(even, far, near), jnp.where(even, near, far)
-    work[...] = jnp.concatenate([top, bottom], axis=0).T
-    basis[...] = jnp.zeros_like(basis)
+    basis_store[...] = jnp.zeros_like(basis_store)
     chunks = (from_near.shape[1] - order) // WIDTH
     left_half = lane_ids(WIDTH) < BLK
     for chunk in range(chunks):
@@ -205,7 +216,18 @@
         for half in range(2):
             row = pl.multiple_of(table[place, half * chunks + chunk] * WIDTH, WIDTH)
             left = jnp.logical_xor(even, half == 0)
-            basis[pl.ds(row, WIDTH), :] += jnp.where(left_half == left, piece, 0.0)
+            basis_store[pl.ds(row, WIDTH), :] += jnp.where(left_half == left, piece, 0.0)
+    copies = [pltpu.make_async_copy(basis_store, basis, sems.at[0])]
+    copies[0].start()
+    for number, begin in enumerate(range(0, order, CHUNK)):
+        rows = pl.ds(begin, CHUNK)
+        near, far = from_near[:, rows], from_far[:, rows]
+        pair = [jnp.where(even, far, near), jnp.where(even, near, far)]
+        work_store[rows, :] = jnp.concatenate(pair, axis=0).T
+        copies.append(pltpu.make_async_copy(work_store.at[rows], work.at[rows], sems.at[number + 1]))
+        copies[-1].start()
+    for copy in copies:
+        copy.wait()
 
 
 def far_place(place, count):
@@ -219,17 +241,9 @@
     return np.array([third[p ^ 1] + third[far[p]] for p in range(count)], np.int32)
 
 
-PAIR_Z = (((1, 0), (3, 2)), ((3, 2), (1, 0)))
-
-
-def homes(factors, count):
-    home = np.zeros(factors * count, np.int32)
-    for group in range(factors):
-        for place in range(count):
-            x, pair, core = place // 4, place % 4 // 2, place % 2
-            z = PAIR_Z[x % 2][group % 2][pair]
-            home[group * count + place] = (group // 2 * 2 + core) * count + 4 * x + z
-    return home
+def home_of(group, place, count):
+    x, z = CHAINS[group % 2][place // 2]
+    return (group // 2 * 2 + place % 2) * count + 4 * x + z
 
 
 def vmem():
@@ -240,7 +254,13 @@
     return pl.BlockSpec(memory_space=pltpu.SMEM)
 
 
-PARAMS = pltpu.CompilerParams(vmem_limit_bytes=40 * 1024 * 1024)
+def hbm():
+    return pl.BlockSpec(memory_space=pltpu.HBM)
+
+
+MIB = 1024 * 1024
+PARAMS = pltpu.CompilerParams(vmem_limit_bytes=40 * MIB)
+DEAL_PARAMS = pltpu.CompilerParams(vmem_limit_bytes=62 * MIB + MIB // 2)
 
 
 def shape(*dims):
@@ -252,23 +272,28 @@
     count = order // WIDTH
     devices = factors * count
     axes = ("fac", "jac")
-    home = homes(factors, count)
+    home = np.array([home_of(g, p, count) for g in range(factors) for p in range(count)], np.int32)
     places = np.zeros(devices, np.int32)
     places[home] = np.arange(devices) % count
     me = lax.axis_index(axes).astype(jnp.int32).reshape(1)
     dealt = pl.pallas_call(
         deal_kernel,
         out_shape=shape(devices, slab, WIDTH),
-        in_specs=[smem(), smem(), vmem()],
+        in_specs=[hbm(), hbm()],
         out_specs=vmem(),
-        compiler_params=PARAMS,
+        scratch_shapes=[
+            pltpu.SMEM((factors,), jnp.int32),
+            pltpu.VMEM((factors, slab, order), jnp.float32),
+            pltpu.SemaphoreType.DMA((factors + 1,)),
+        ],
+        compiler_params=DEAL_PARAMS,
         name="deal",
-    )(assignment, jnp.asarray(home), statistics)
+    )(assignment, statistics)
     moved = lax.all_to_all(dealt, axes, split_axis=0, concat_axis=0, tiled=True)
     work = moved.reshape(order, WIDTH)
     places = jnp.asarray(places)
     store = pltpu.VMEM((WIDTH, WIDTH), jnp.float32)
-    near, far = pl.pallas_call(
+    far, near = pl.pallas_call(
         first_kernel,
         out_shape=[shape(BLK, order + WIDTH)] * 2,
         in_specs=[smem(), smem(), vmem()],
@@ -288,7 +313,7 @@
         from_far = lax.ppermute(far, axes, far_route)
         from_near = lax.ppermute(near, axes, near_route)
         if later < ROUNDS:
-            near, far = pl.pallas_call(
+            far, near = pl.pallas_call(
                 functools.partial(next_kernel, order, later == ROUNDS - 1),
                 out_shape=[shape(BLK, order + (later + 1) * WIDTH)] * 2,
                 in_specs=[smem(), smem(), vmem(), vmem()],
@@ -296,15 +321,17 @@
                 scratch_shapes=[store],
                 compiler_params=PARAMS,
                 name="next_round",
-            )(me, places, from_near, from_far)
+            )(me, places, from_far, from_near)
     work, basis = pl.pallas_call(
         last_kernel,
         out_shape=[shape(order, WIDTH)] * 2,
         in_specs=[smem(), smem(), vmem(), vmem()],
-        out_specs=[vmem()] * 2,
+        out_specs=[hbm()] * 2,
+        scratch_shapes=[pltpu.VMEM((order, WIDTH), jnp.float32)] * 2
+        + [pltpu.SemaphoreType.DMA((1 + order // CHUNK,))],
         compiler_params=PARAMS,
         name="output",
-    )(me, jnp.asarray(support_table(count)), from_near, from_far)
+    )(me, jnp.asarray(support_table(count)), from_far, from_near)
     return work[None], basis[None]
 
 

time: 103 us -> 105 us (1.019)
  the two profiles are of different devices: /device:TPU:0 before, /device:TPU:4 now
where the time goes in v3:
time: 105 us
  waiting for transfers between devices  62.9 us (60%)
  starting transfers between devices  21.5 us (20%)
  Pallas kernels  19.2 us (18%)
    ppermute x3, waiting for transfers between devices, shards(): from_far = lax.ppermute(far, axes, far_route)  34.7 us
    all_to_all x1, waiting for transfers between devices, shards(): moved = lax.all_to_all(dealt, axes, split_axis=0, concat_axis=0, tiled=True)  17.6 us
    ppermute x3, waiting for transfers between devices, shards(): from_near = lax.ppermute(near, axes, near_route)  10.6 us
    all_to_all x1, starting transfers between devices, shards(): moved = lax.all_to_all(dealt, axes, split_axis=0, concat_axis=0, tiled=True)  10.5 us
    pallas_call x2, Pallas kernels, shards(): pl.pallas_call(functools.partial(next_kernel, order, later == ROUNDS - 1)...  9.6 us
    ppermute x3, starting transfers between devices, shards(): from_far = lax.ppermute(far, axes, far_route)  5.76 us
    ppermute x3, starting transfers between devices, shards(): from_near = lax.ppermute(near, axes, near_route)  5.24 us
    pallas_call x1, Pallas kernels, shards(): pl.pallas_call(first_kernel, out_shape=[shape(BLK, order + WIDTH)] * 2, i...  4.88 us
  transfers between devices with their start and end apart: 7, of which 5 were waited for; matrix products, arithmetic and copies ran while one was open for 0% of the time, Pallas kernels for 0%

profile of v3, /device:TPU:4, one launch (start us, length us, event | category | flops | bytes accessed | tf_op | source)
XLA Modules:
  0.0 105.0 jit_solution(1612262467906427019)
XLA Ops:
  0.6 2.3 %deal.1 = f32[128,16,128]{2,1,0:T(8,128)} custom-call(s32[8]{0:T(128)} %assignment.1, f32[8,16,2048]{2,1,0:T(8,128)} %stats.1), custom_call_target="tpu_custom_call" | custom-call | tf_op jit(solution)/shard_map/deal/pallas_call | solution.py:279
  3.0 10.5 %all-to-all-start = ((f32[128,16,128]{2,1,0:T(8,128)}), f32[128,16,128]{2,1,0:T(8,128)S(1)}, u32[]{:S(2)}, u32[]{:S(2)}) async-start(f32[128,16,128]{2,1,0:T(8,128)} %deal.1), calls=%async_computation | async-start | bytes 2097152 | tf_op jit(solution)/shard_map/all_to_all | solution.py:292
  13.5 17.6 %all-to-all-done = f32[128,16,128]{2,1,0:T(8,128)S(1)} async-done(((f32[128,16,128]{2,1,0:T(8,128)}), f32[128,16,128]{2,1,0:T(8,128)S(1)}, u32[]{:S(2)}, u32[]{:S(2)}) %all-to-all-start) | async-done | bytes 1048608 | tf_op jit(solution)/shard_map/all_to_all | solution.py:292
  31.1 0.0 copy-start.1
  31.1 0.7 copy-done.1
  31.8 4.9 %first_round.1 = (f32[64,2176]{1,0:T(8,128)S(1)}, f32[64,2176]{1,0:T(8,128)S(1)}) custom-call(s32[1]{0:T(128)} %bitcast.me, s32[128]{0:T(128)S(1)} %copy-done.1, f32[2048,128]{1,0:T(8,128)S(1)} %bitcast.4), custom_call_target="tpu_custom_call" | custom-call | tf_op jit(solution)/shard_map/first_round/pallas_call | solution.py:296
  36.7 1.9 %collective-permute-start = (f32[64,2176]{1,0:T(8,128)S(1)}, f32[64,2176]{1,0:T(8,128)S(1)}, u32[]{:S(2)}, u32[]{:S(2)}) collective-permute-start(f32[64,2176]{1,0:T(8,128)S(1)} %get-tuple-element.10), channel_id=1, source_target_pairs={{1,1},{17,5},{5,17},{21,4},{4,21},{20,7},{7,20},{23,11},{11,23},{2... | collective-permute-start | bytes 1671176 | tf_op jit(solution)/shard_map/ppermute | solution.py:313
  38.6 0.9 collective-permute-start.1
  39.5 9.2 %collective-permute-done.from_far = f32[64,2176]{1,0:T(8,128)S(1)} collective-permute-done((f32[64,2176]{1,0:T(8,128)S(1)}, f32[64,2176]{1,0:T(8,128)S(1)}, u32[]{:S(2)}, u32[]{:S(2)}) %collective-permute-start) | collective-permute-done | bytes 557088 | tf_op jit(solution)/shard_map/ppermute | solution.py:313
  48.7 0.0 collective-permute-done.1.from_near
  48.8 4.9 %next_round.2 = (f32[64,2304]{1,0:T(8,128)S(1)}, f32[64,2304]{1,0:T(8,128)S(1)}) custom-call(s32[1]{0:T(128)} %bitcast.me, s32[128]{0:T(128)S(1)} %copy-done.1, f32[64,2176]{1,0:T(8,128)S(1)} %collective-permute-done.from_far, f32[64,2176]{1,0:T(8,128)S(1)} %collective-permute-done.1.from_near), custom_call_target="tpu_custom_call" | custom-call | tf_op jit(solution)/shard_map/next_round/pallas_call | solution.py:316
  53.7 1.9 %collective-permute-start.2 = (f32[64,2304]{1,0:T(8,128)S(1)}, f32[64,2304]{1,0:T(8,128)S(1)}, u32[]{:S(2)}, u32[]{:S(2)}) collective-permute-start(f32[64,2304]{1,0:T(8,128)S(1)} %get-tuple-element.12), channel_id=1, source_target_pairs={{1,1},{17,5},{5,17},{21,4},{4,21},{20,7},{7,20},{23,11},{11,23},{2... | collective-permute-start | bytes 1769480 | tf_op jit(solution)/shard_map/ppermute | solution.py:313
  55.6 0.1 collective-permute-start.3
  55.7 10.4 %collective-permute-done.2.from_far = f32[64,2304]{1,0:T(8,128)S(1)} collective-permute-done((f32[64,2304]{1,0:T(8,128)S(1)}, f32[64,2304]{1,0:T(8,128)S(1)}, u32[]{:S(2)}, u32[]{:S(2)}) %collective-permute-start.2) | collective-permute-done | bytes 589856 | tf_op jit(solution)/shard_map/ppermute | solution.py:313
  66.1 0.0 collective-permute-done.3.from_near
  66.1 0.0 copy-start
  66.1 4.7 %next_round.3 = (f32[64,2432]{1,0:T(8,128)S(1)}, f32[64,2432]{1,0:T(8,128)S(1)}) custom-call(s32[1]{0:T(128)} %bitcast.me, s32[128]{0:T(128)S(1)} %copy-done.1, f32[64,2304]{1,0:T(8,128)S(1)} %collective-permute-done.2.from_far, f32[64,2304]{1,0:T(8,128)S(1)} %collective-permute-done.3.from_near), custom_call_target="tpu_custom_call" | custom-call | tf_op jit(solution)/shard_map/next_round/pallas_call | solution.py:316
  70.8 1.9 %collective-permute-start.4 = (f32[64,2432]{1,0:T(8,128)S(1)}, f32[64,2432]{1,0:T(8,128)S(1)}, u32[]{:S(2)}, u32[]{:S(2)}) collective-permute-start(f32[64,2432]{1,0:T(8,128)S(1)} %get-tuple-element.14), channel_id=1, source_target_pairs={{1,0},{17,2},{5,1},{21,4},{4,3},{20,6},{7,5},{23,8},{11,7},{27,10}... | collective-permute-start | bytes 1867784 | tf_op jit(solution)/shard_map/ppermute | solution.py:313
  72.7 4.3 %collective-permute-start.5 = (f32[64,2432]{1,0:T(8,128)S(1)}, f32[64,2432]{1,0:T(8,128)S(1)}, u32[]{:S(2)}, u32[]{:S(2)}) collective-permute-start(f32[64,2432]{1,0:T(8,128)S(1)} %get-tuple-element.15), channel_id=1, source_target_pairs={{1,1},{17,0},{5,3},{21,2},{4,5},{20,4},{7,7},{23,6},{11,9},{27,8},... | collective-permute-start | bytes 1867784 | tf_op jit(solution)/shard_map/ppermute | solution.py:314
  77.0 15.0 %collective-permute-done.4.from_far = f32[64,2432]{1,0:T(8,128)S(1)} collective-permute-done((f32[64,2432]{1,0:T(8,128)S(1)}, f32[64,2432]{1,0:T(8,128)S(1)}, u32[]{:S(2)}, u32[]{:S(2)}) %collective-permute-start.4) | collective-permute-done | bytes 622624 | tf_op jit(solution)/shard_map/ppermute | solution.py:313
  92.0 10.6 %collective-permute-done.5.from_near = f32[64,2432]{1,0:T(8,128)S(1)} collective-permute-done((f32[64,2432]{1,0:T(8,128)S(1)}, f32[64,2432]{1,0:T(8,128)S(1)}, u32[]{:S(2)}, u32[]{:S(2)}) %collective-permute-start.5) | collective-permute-done | bytes 622624 | tf_op jit(solution)/shard_map/ppermute | solution.py:314
  102.6 0.0 copy-done
  102.6 2.4 %output.1 = (f32[2048,128]{1,0:T(8,128)}, f32[2048,128]{1,0:T(8,128)}) custom-call(s32[1]{0:T(128)} %bitcast.me, s32[16,6]{1,0:T(8,128)S(1)} %copy-done, f32[64,2432]{1,0:T(8,128)S(1)} %collective-permute-done.4.from_far, f32[64,2432]{1,0:T(8,128)S(1)} %collective-permute-done.5.from_near), custom_call_target="tpu_custom_call" | custom-call | tf_op jit(solution)/shard_map/output/pallas_call | solution.py:325
Async XLA Ops:
  3.0 28.2 %all-to-all-start = ((f32[128,16,128]{2,1,0:T(8,128)}), f32[128,16,128]{2,1,0:T(8,128)S(1)}, u32[]{:S(2)}, u32[]{:S(2)}) async-start(f32[128,16,128]{2,1,0:T(8,128)} %deal.1), calls=%async_computation | async-start | bytes 2097152 | tf_op jit(solution)/shard_map/all_to_all | solution.py:292
  31.1 0.7 copy-start.1
  36.7 12.1 %collective-permute-start = (f32[64,2176]{1,0:T(8,128)S(1)}, f32[64,2176]{1,0:T(8,128)S(1)}, u32[]{:S(2)}, u32[]{:S(2)}) collective-permute-start(f32[64,2176]{1,0:T(8,128)S(1)} %get-tuple-element.10), channel_id=1, source_target_pairs={{1,1},{17,5},{5,17},{21,4},{4,21},{20,7},{7,20},{23,11},{11,23},{2... | collective-permute-start | bytes 1671176 | tf_op jit(solution)/shard_map/ppermute | solution.py:313
  38.6 10.1 %collective-permute-start.1 = (f32[64,2176]{1,0:T(8,128)S(1)}, f32[64,2176]{1,0:T(8,128)S(1)}, u32[]{:S(2)}, u32[]{:S(2)}) collective-permute-start(f32[64,2176]{1,0:T(8,128)S(1)} %get-tuple-element.11), channel_id=1, source_target_pairs={{1,17},{17,1},{5,21},{21,5},{4,20},{20,4},{7,23},{23,7},{11,27},{2... | collective-permute-start | bytes 1671176 | tf_op jit(solution)/shard_map/ppermute | solution.py:314
  53.7 12.4 %collective-permute-start.2 = (f32[64,2304]{1,0:T(8,128)S(1)}, f32[64,2304]{1,0:T(8,128)S(1)}, u32[]{:S(2)}, u32[]{:S(2)}) collective-permute-start(f32[64,2304]{1,0:T(8,128)S(1)} %get-tuple-element.12), channel_id=1, source_target_pairs={{1,1},{17,5},{5,17},{21,4},{4,21},{20,7},{7,20},{23,11},{11,23},{2... | collective-permute-start | bytes 1769480 | tf_op jit(solution)/shard_map/ppermute | solution.py:313
  55.6 10.5 %collective-permute-start.3 = (f32[64,2304]{1,0:T(8,128)S(1)}, f32[64,2304]{1,0:T(8,128)S(1)}, u32[]{:S(2)}, u32[]{:S(2)}) collective-permute-start(f32[64,2304]{1,0:T(8,128)S(1)} %get-tuple-element.13), channel_id=1, source_target_pairs={{1,17},{17,1},{5,21},{21,5},{4,20},{20,4},{7,23},{23,7},{11,27},{2... | collective-permute-start | bytes 1769480 | tf_op jit(solution)/shard_map/ppermute | solution.py:314
  66.1 36.5 %copy-start = (s32[16,6]{1,0:T(8,128)S(1)}, s32[16,6]{1,0:T(8,128)}, u32[]{:S(2)}) copy-start(s32[16,6]{1,0:T(8,128)} %constant.16.clone.table) | copy-start | bytes 1156
  70.8 21.2 %collective-permute-start.4 = (f32[64,2432]{1,0:T(8,128)S(1)}, f32[64,2432]{1,0:T(8,128)S(1)}, u32[]{:S(2)}, u32[]{:S(2)}) collective-permute-start(f32[64,2432]{1,0:T(8,128)S(1)} %get-tuple-element.14), channel_id=1, source_target_pairs={{1,0},{17,2},{5,1},{21,4},{4,3},{20,6},{7,5},{23,8},{11,7},{27,10}... | collective-permute-start | bytes 1867784 | tf_op jit(solution)/shard_map/ppermute | solution.py:313
  72.7 29.9 %collective-permute-start.5 = (f32[64,2432]{1,0:T(8,128)S(1)}, f32[64,2432]{1,0:T(8,128)S(1)}, u32[]{:S(2)}, u32[]{:S(2)}) collective-permute-start(f32[64,2432]{1,0:T(8,128)S(1)} %get-tuple-element.15), channel_id=1, source_target_pairs={{1,1},{17,0},{5,3},{21,2},{4,5},{20,4},{7,7},{23,6},{11,9},{27,8},... | collective-permute-start | bytes 1867784 | tf_op jit(solution)/shard_map/ppermute | solution.py:314

commit v4 on v3

--- a/solution.py
+++ b/solution.py
@@ -11,8 +11,8 @@
 ROUNDS = 3
 CHUNK = 512
 CHAINS = (
-    ((0, 1), (1, 1), (1, 0), (1, 3), (2, 3), (2, 0), (3, 0), (3, 3)),
-    ((0, 0), (0, 3), (0, 2), (1, 2), (2, 2), (2, 1), (3, 1), (3, 2)),
+    ((0, 1), (0, 0), (1, 3), (1, 2), (2, 1), (2, 0), (3, 3), (3, 2)),
+    ((0, 3), (0, 2), (1, 1), (1, 0), (2, 3), (2, 2), (3, 1), (3, 0)),
 )
 BLK = 64
 WIDTH = 2 * BLK

time: 105 us -> 96.7 us (0.921)
  the two profiles are of different devices: /device:TPU:4 before, /device:TPU:0 now
where the time goes in v4:
time: 96.7 us; the launch traced here: 96.4 us
  waiting for transfers between devices  48.8 us (50%)
  starting transfers between devices  27.1 us (28%)
  Pallas kernels  19.2 us (20%)
    ppermute x3, waiting for transfers between devices, shards(): from_far = lax.ppermute(far, axes, far_route)  28.9 us
    all_to_all x1, waiting for transfers between devices, shards(): moved = lax.all_to_all(dealt, axes, split_axis=0, concat_axis=0, tiled=True)  19 us
    ppermute x3, starting transfers between devices, shards(): from_near = lax.ppermute(near, axes, near_route)  12 us
    all_to_all x1, starting transfers between devices, shards(): moved = lax.all_to_all(dealt, axes, split_axis=0, concat_axis=0, tiled=True)  11.1 us
    pallas_call x2, Pallas kernels, shards(): pl.pallas_call(functools.partial(next_kernel, order, later == ROUNDS - 1)...  9.6 us
    pallas_call x1, Pallas kernels, shards(): pl.pallas_call(first_kernel, out_shape=[shape(BLK, order + WIDTH)] * 2, i...  4.88 us
    ppermute x3, starting transfers between devices, shards(): from_far = lax.ppermute(far, axes, far_route)  3.92 us
    pallas_call x1, Pallas kernels, shards(): pl.pallas_call(last_kernel, out_shape=[shape(order, WIDTH)] * 2, in_specs...  2.36 us
  transfers between devices with their start and end apart: 7, of which 5 were waited for; matrix products, arithmetic and copies ran while one was open for 0% of the time, Pallas kernels for 0%

profile of v4, /device:TPU:0, one launch (start us, length us, event | category | flops | bytes accessed | tf_op | source)
XLA Modules:
  0.0 96.4 jit_solution(16360678605771649843)
XLA Ops:
  0.6 2.3 %deal.1 = f32[128,16,128]{2,1,0:T(8,128)} custom-call(s32[8]{0:T(128)} %assignment.1, f32[8,16,2048]{2,1,0:T(8,128)} %stats.1), custom_call_target="tpu_custom_call" | custom-call | tf_op jit(solution)/shard_map/deal/pallas_call | solution.py:279
  3.0 11.1 %all-to-all-start = ((f32[128,16,128]{2,1,0:T(8,128)}), f32[128,16,128]{2,1,0:T(8,128)S(1)}, u32[]{:S(2)}, u32[]{:S(2)}) async-start(f32[128,16,128]{2,1,0:T(8,128)} %deal.1), calls=%async_computation | async-start | bytes 2097152 | tf_op jit(solution)/shard_map/all_to_all | solution.py:292
  14.1 19.0 %all-to-all-done = f32[128,16,128]{2,1,0:T(8,128)S(1)} async-done(((f32[128,16,128]{2,1,0:T(8,128)}), f32[128,16,128]{2,1,0:T(8,128)S(1)}, u32[]{:S(2)}, u32[]{:S(2)}) %all-to-all-start) | async-done | bytes 1048608 | tf_op jit(solution)/shard_map/all_to_all | solution.py:292
  33.2 0.0 copy-start.1
  33.2 0.7 copy-done.1
  33.8 4.9 %first_round.1 = (f32[64,2176]{1,0:T(8,128)S(1)}, f32[64,2176]{1,0:T(8,128)S(1)}) custom-call(s32[1]{0:T(128)} %bitcast.me, s32[128]{0:T(128)S(1)} %copy-done.1, f32[2048,128]{1,0:T(8,128)S(1)} %bitcast.4), custom_call_target="tpu_custom_call" | custom-call | tf_op jit(solution)/shard_map/first_round/pallas_call | solution.py:296
  38.7 1.9 %collective-permute-start = (f32[64,2176]{1,0:T(8,128)S(1)}, f32[64,2176]{1,0:T(8,128)S(1)}, u32[]{:S(2)}, u32[]{:S(2)}) collective-permute-start(f32[64,2176]{1,0:T(8,128)S(1)} %get-tuple-element.10), channel_id=1, source_target_pairs={{1,1},{17,0},{0,17},{16,7},{7,16},{23,6},{6,23},{22,9},{9,22},{25,... | collective-permute-start | bytes 1671176 | tf_op jit(solution)/shard_map/ppermute | solution.py:313
  40.7 1.0 %collective-permute-start.1 = (f32[64,2176]{1,0:T(8,128)S(1)}, f32[64,2176]{1,0:T(8,128)S(1)}, u32[]{:S(2)}, u32[]{:S(2)}) collective-permute-start(f32[64,2176]{1,0:T(8,128)S(1)} %get-tuple-element.11), channel_id=1, source_target_pairs={{1,17},{17,1},{0,16},{16,0},{7,23},{23,7},{6,22},{22,6},{9,25},{25... | collective-permute-start | bytes 1671176 | tf_op jit(solution)/shard_map/ppermute | solution.py:314
  41.6 8.0 %collective-permute-done.from_far = f32[64,2176]{1,0:T(8,128)S(1)} collective-permute-done((f32[64,2176]{1,0:T(8,128)S(1)}, f32[64,2176]{1,0:T(8,128)S(1)}, u32[]{:S(2)}, u32[]{:S(2)}) %collective-permute-start) | collective-permute-done | bytes 557088 | tf_op jit(solution)/shard_map/ppermute | solution.py:313
  49.6 0.0 collective-permute-done.1.from_near
  49.6 4.9 %next_round.2 = (f32[64,2304]{1,0:T(8,128)S(1)}, f32[64,2304]{1,0:T(8,128)S(1)}) custom-call(s32[1]{0:T(128)} %bitcast.me, s32[128]{0:T(128)S(1)} %copy-done.1, f32[64,2176]{1,0:T(8,128)S(1)} %collective-permute-done.from_far, f32[64,2176]{1,0:T(8,128)S(1)} %collective-permute-done.1.from_near), custom_call_target="tpu_custom_call" | custom-call | tf_op jit(solution)/shard_map/next_round/pallas_call | solution.py:316
  54.5 1.9 %collective-permute-start.2 = (f32[64,2304]{1,0:T(8,128)S(1)}, f32[64,2304]{1,0:T(8,128)S(1)}, u32[]{:S(2)}, u32[]{:S(2)}) collective-permute-start(f32[64,2304]{1,0:T(8,128)S(1)} %get-tuple-element.12), channel_id=1, source_target_pairs={{1,1},{17,0},{0,17},{16,7},{7,16},{23,6},{6,23},{22,9},{9,22},{25,... | collective-permute-start | bytes 1769480 | tf_op jit(solution)/shard_map/ppermute | solution.py:313
  56.5 3.1 %collective-permute-start.3 = (f32[64,2304]{1,0:T(8,128)S(1)}, f32[64,2304]{1,0:T(8,128)S(1)}, u32[]{:S(2)}, u32[]{:S(2)}) collective-permute-start(f32[64,2304]{1,0:T(8,128)S(1)} %get-tuple-element.13), channel_id=1, source_target_pairs={{1,17},{17,1},{0,16},{16,0},{7,23},{23,7},{6,22},{22,6},{9,25},{25... | collective-permute-start | bytes 1769480 | tf_op jit(solution)/shard_map/ppermute | solution.py:314
  59.5 6.2 %collective-permute-done.2.from_far = f32[64,2304]{1,0:T(8,128)S(1)} collective-permute-done((f32[64,2304]{1,0:T(8,128)S(1)}, f32[64,2304]{1,0:T(8,128)S(1)}, u32[]{:S(2)}, u32[]{:S(2)}) %collective-permute-start.2) | collective-permute-done | bytes 589856 | tf_op jit(solution)/shard_map/ppermute | solution.py:313
  65.7 0.0 collective-permute-done.3.from_near
  65.7 0.0 copy-start
  65.7 4.7 %next_round.3 = (f32[64,2432]{1,0:T(8,128)S(1)}, f32[64,2432]{1,0:T(8,128)S(1)}) custom-call(s32[1]{0:T(128)} %bitcast.me, s32[128]{0:T(128)S(1)} %copy-done.1, f32[64,2304]{1,0:T(8,128)S(1)} %collective-permute-done.2.from_far, f32[64,2304]{1,0:T(8,128)S(1)} %collective-permute-done.3.from_near), custom_call_target="tpu_custom_call" | custom-call | tf_op jit(solution)/shard_map/next_round/pallas_call | solution.py:316
  70.4 0.1 collective-permute-start.4
  70.5 8.0 %collective-permute-start.5 = (f32[64,2432]{1,0:T(8,128)S(1)}, f32[64,2432]{1,0:T(8,128)S(1)}, u32[]{:S(2)}, u32[]{:S(2)}) collective-permute-start(f32[64,2432]{1,0:T(8,128)S(1)} %get-tuple-element.15), channel_id=1, source_target_pairs={{1,1},{17,0},{0,3},{16,2},{7,5},{23,4},{6,7},{22,6},{9,9},{25,8},{... | collective-permute-start | bytes 1867784 | tf_op jit(solution)/shard_map/ppermute | solution.py:314
  78.5 14.7 %collective-permute-done.4.from_far = f32[64,2432]{1,0:T(8,128)S(1)} collective-permute-done((f32[64,2432]{1,0:T(8,128)S(1)}, f32[64,2432]{1,0:T(8,128)S(1)}, u32[]{:S(2)}, u32[]{:S(2)}) %collective-permute-start.4) | collective-permute-done | bytes 622624 | tf_op jit(solution)/shard_map/ppermute | solution.py:313
  93.2 0.9 collective-permute-done.5.from_near
  94.1 0.0 copy-done
  94.1 2.4 %output.1 = (f32[2048,128]{1,0:T(8,128)}, f32[2048,128]{1,0:T(8,128)}) custom-call(s32[1]{0:T(128)} %bitcast.me, s32[16,6]{1,0:T(8,128)S(1)} %copy-done, f32[64,2432]{1,0:T(8,128)S(1)} %collective-permute-done.4.from_far, f32[64,2432]{1,0:T(8,128)S(1)} %collective-permute-done.5.from_near), custom_call_target="tpu_custom_call" | custom-call | tf_op jit(solution)/shard_map/output/pallas_call | solution.py:325
Async XLA Ops:
  3.0 30.2 %all-to-all-start = ((f32[128,16,128]{2,1,0:T(8,128)}), f32[128,16,128]{2,1,0:T(8,128)S(1)}, u32[]{:S(2)}, u32[]{:S(2)}) async-start(f32[128,16,128]{2,1,0:T(8,128)} %deal.1), calls=%async_computation | async-start | bytes 2097152 | tf_op jit(solution)/shard_map/all_to_all | solution.py:292
  33.2 0.7 copy-start.1
  38.7 10.9 %collective-permute-start = (f32[64,2176]{1,0:T(8,128)S(1)}, f32[64,2176]{1,0:T(8,128)S(1)}, u32[]{:S(2)}, u32[]{:S(2)}) collective-permute-start(f32[64,2176]{1,0:T(8,128)S(1)} %get-tuple-element.10), channel_id=1, source_target_pairs={{1,1},{17,0},{0,17},{16,7},{7,16},{23,6},{6,23},{22,9},{9,22},{25,... | collective-permute-start | bytes 1671176 | tf_op jit(solution)/shard_map/ppermute | solution.py:313
  40.7 8.9 %collective-permute-start.1 = (f32[64,2176]{1,0:T(8,128)S(1)}, f32[64,2176]{1,0:T(8,128)S(1)}, u32[]{:S(2)}, u32[]{:S(2)}) collective-permute-start(f32[64,2176]{1,0:T(8,128)S(1)} %get-tuple-element.11), channel_id=1, source_target_pairs={{1,17},{17,1},{0,16},{16,0},{7,23},{23,7},{6,22},{22,6},{9,25},{25... | collective-permute-start | bytes 1671176 | tf_op jit(solution)/shard_map/ppermute | solution.py:314
  54.5 11.2 %collective-permute-start.2 = (f32[64,2304]{1,0:T(8,128)S(1)}, f32[64,2304]{1,0:T(8,128)S(1)}, u32[]{:S(2)}, u32[]{:S(2)}) collective-permute-start(f32[64,2304]{1,0:T(8,128)S(1)} %get-tuple-element.12), channel_id=1, source_target_pairs={{1,1},{17,0},{0,17},{16,7},{7,16},{23,6},{6,23},{22,9},{9,22},{25,... | collective-permute-start | bytes 1769480 | tf_op jit(solution)/shard_map/ppermute | solution.py:313
  56.5 9.3 %collective-permute-start.3 = (f32[64,2304]{1,0:T(8,128)S(1)}, f32[64,2304]{1,0:T(8,128)S(1)}, u32[]{:S(2)}, u32[]{:S(2)}) collective-permute-start(f32[64,2304]{1,0:T(8,128)S(1)} %get-tuple-element.13), channel_id=1, source_target_pairs={{1,17},{17,1},{0,16},{16,0},{7,23},{23,7},{6,22},{22,6},{9,25},{25... | collective-permute-start | bytes 1769480 | tf_op jit(solution)/shard_map/ppermute | solution.py:314
  65.7 28.3 %copy-start = (s32[16,6]{1,0:T(8,128)S(1)}, s32[16,6]{1,0:T(8,128)}, u32[]{:S(2)}) copy-start(s32[16,6]{1,0:T(8,128)} %constant.16.clone.table) | copy-start | bytes 1156
  70.4 22.8 %collective-permute-start.4 = (f32[64,2432]{1,0:T(8,128)S(1)}, f32[64,2432]{1,0:T(8,128)S(1)}, u32[]{:S(2)}, u32[]{:S(2)}) collective-permute-start(f32[64,2432]{1,0:T(8,128)S(1)} %get-tuple-element.14), channel_id=1, source_target_pairs={{1,0},{17,2},{0,1},{16,4},{7,3},{23,6},{6,5},{22,8},{9,7},{25,10},... | collective-permute-start | bytes 1867784 | tf_op jit(solution)/shard_map/ppermute | solution.py:313
  70.5 23.6 %collective-permute-start.5 = (f32[64,2432]{1,0:T(8,128)S(1)}, f32[64,2432]{1,0:T(8,128)S(1)}, u32[]{:S(2)}, u32[]{:S(2)}) collective-permute-start(f32[64,2432]{1,0:T(8,128)S(1)} %get-tuple-element.15), channel_id=1, source_target_pairs={{1,1},{17,0},{0,3},{16,2},{7,5},{23,4},{6,7},{22,6},{9,9},{25,8},{... | collective-permute-start | bytes 1867784 | tf_op jit(solution)/shard_map/ppermute | solution.py:314

commit v5 on v4

--- a/solution.py
+++ b/solution.py
@@ -28,11 +28,10 @@
 def angles(alpha, beta, gamma):
     diff = beta - alpha
     square = diff * diff + 4.0 * gamma * gamma
-    turns = square > 0
-    inverse = jnp.where(turns, lax.rsqrt(jnp.where(turns, square, 1.0)), 0.0)
+    inverse = jnp.where(square > 0, lax.rsqrt(square), 0.0)
     along = diff * inverse
     lead = 1.0 + jnp.abs(along)
-    cross = 2.0 * gamma * inverse * along
+    cross = (2.0 * gamma) * inverse * along
     scale = lax.rsqrt(lead * lead + cross * cross)
     return lead * scale, cross * scale
 
@@ -71,6 +70,7 @@
 
     alpha, beta, gamma = spread(aa[0], 0), spread(dd[0], 0), spread(bb[0], 0)
     for section in range(SECTIONS):
+        ahead = [spread(x[-1], SUB - 1) for x in (aa, bb, tt, dd)]
         c, s = angles(alpha, beta, gamma)
         cc = [pltpu.roll(c, b, 1, stride=SUB, stride_axis=0) for b in range(GROUPS)]
         ss = [pltpu.roll(s, b, 1, stride=SUB, stride_axis=0) for b in range(GROUPS)]
@@ -90,8 +90,10 @@
         d2 = [s * b1[b] + c * d1[b] for b in range(GROUPS)]
         new_alpha = c * (c * alpha - s * gamma) - s * (c * gamma - s * beta)
         new_beta = s * (s * alpha + c * gamma) + c * (s * gamma + c * beta)
-        alpha, beta = new_alpha, pltpu.roll(new_beta, WIDTH - 1, 1)
-        gamma = spread(b2[-1], SUB - 1)
+        c_up, s_up = pltpu.roll(c, WIDTH - 1, 1), pltpu.roll(s, WIDTH - 1, 1)
+        above = s_up * ahead[0] + c_up * ahead[1]
+        below = s_up * ahead[2] + c_up * ahead[3]
+        alpha, beta, gamma = new_alpha, pltpu.roll(new_beta, WIDTH - 1, 1), c * above - s * below
         bb = [pltpu.roll(b2[-1], 1, 0)] + b2[:-1]
         t2 = t2[1:] + [pltpu.roll(t2[0], SUB - 1, 0)]
         tt = [pltpu.roll(x, WIDTH - 1, 1) for x in t2]
@@ -164,6 +166,15 @@
     return jnp.where(swapped, pltpu.roll(x, BLK, axis), x)
 
 
+def place_here():
+    cell = lax.axis_index("jac")
+    pair = 0
+    for chain in CHAINS:
+        for number, (x, z) in enumerate(chain):
+            pair = jnp.where(cell == 4 * x + z, number, pair)
+    return 2 * pair + lax.axis_index("fac") % 2
+
+
 def leave_rotation(gram, store, place, swapped):
     rotation = small_rotation(gram, store, swapped).T
     bottom_first = jnp.logical_or(place == 0, place % 2 == 1)
@@ -175,8 +186,8 @@
     far[:, columns] = block[BLK:]
 
 
-def first_kernel(me, places, work, far, near, store):
-    place = places[me[0]]
+def first_kernel(work, far, near, store):
+    place = place_here()
     order = work.shape[0]
     parts = pieces(work[...].T)
     rotation = leave_rotation(gram_of(parts), store, place, False)
@@ -184,8 +195,8 @@
     post(near, far, pl.ds(order, WIDTH), rotation)
 
 
-def next_kernel(order, final, me, places, from_far, from_near, far, near, store):
-    place = places[me[0]]
+def next_kernel(order, final, from_far, from_near, far, near, store):
+    place = place_here()
     swapped = place % 2 == 0
     parts = pieces(jnp.concatenate([from_near[:, :order], from_far[:, :order]], axis=0))
     rotation = leave_rotation(gram_of(parts), store, place, swapped)
@@ -202,9 +213,15 @@
     apply(rotation, pieces(jnp.concatenate(columns, axis=1)), near, far, order, False)
 
 
-def last_kernel(me, table, from_far, from_near, work, basis, work_store, basis_store, sems):
+def last_kernel(from_far, from_near, work, basis, work_store, basis_store, sems):
     order = work.shape[0]
-    place = me[0] % table.shape[0]
+    place = lax.axis_index("jac")
+    count = lax.axis_size("jac")
+    next_chip = far_place(place, count)
+    rows = [
+        [place ^ 1, next_chip, far_place(place ^ 1, count) ^ 1],
+        [next_chip, far_place(next_chip ^ 1, count), far_place(next_chip, count) ^ 1],
+    ]
     even = place % 2 == 0
     basis_store[...] = jnp.zeros_like(basis_store)
     chunks = (from_near.shape[1] - order) // WIDTH
@@ -214,7 +231,7 @@
         piece = jnp.concatenate([from_near[:, columns], from_far[:, columns]], axis=0).T
         piece = swap_halves(piece, 1, even)
         for half in range(2):
-            row = pl.multiple_of(table[place, half * chunks + chunk] * WIDTH, WIDTH)
+            row = pl.multiple_of(rows[half][chunk] * WIDTH, WIDTH)
             left = jnp.logical_xor(even, half == 0)
             basis_store[pl.ds(row, WIDTH), :] += jnp.where(left_half == left, piece, 0.0)
     copies = [pltpu.make_async_copy(basis_store, basis, sems.at[0])]
@@ -231,14 +248,7 @@
 
 
 def far_place(place, count):
-    return min(max(place + (1 if place % 2 else -1), 0), count - 1)
-
-
-def support_table(count):
-    far = [far_place(p, count) for p in range(count)]
-    second = [[p ^ 1, far[p]] for p in range(count)]
-    third = [[p, second[p ^ 1][1], second[far[p]][0]] for p in range(count)]
-    return np.array([third[p ^ 1] + third[far[p]] for p in range(count)], np.int32)
+    return jnp.clip(place + 2 * (place % 2) - 1, 0, count - 1)
 
 
 def home_of(group, place, count):
@@ -248,10 +258,6 @@
 
 def vmem():
     return pl.BlockSpec(memory_space=pltpu.VMEM)
-
-
-def smem():
-    return pl.BlockSpec(memory_space=pltpu.SMEM)
 
 
 def hbm():
@@ -273,9 +279,6 @@
     devices = factors * count
     axes = ("fac", "jac")
     home = np.array([home_of(g, p, count) for g in range(factors) for p in range(count)], np.int32)
-    places = np.zeros(devices, np.int32)
-    places[home] = np.arange(devices) % count
-    me = lax.axis_index(axes).astype(jnp.int32).reshape(1)
     dealt = pl.pallas_call(
         deal_kernel,
         out_shape=shape(devices, slab, WIDTH),
@@ -291,17 +294,16 @@
     )(assignment, statistics)
     moved = lax.all_to_all(dealt, axes, split_axis=0, concat_axis=0, tiled=True)
     work = moved.reshape(order, WIDTH)
-    places = jnp.asarray(places)
     store = pltpu.VMEM((WIDTH, WIDTH), jnp.float32)
     far, near = pl.pallas_call(
         first_kernel,
         out_shape=[shape(BLK, order + WIDTH)] * 2,
-        in_specs=[smem(), smem(), vmem()],
+        in_specs=[vmem()],
         out_specs=[vmem()] * 2,
         scratch_shapes=[store],
         compiler_params=PARAMS,
         name="first_round",
-    )(me, places, work)
+    )(work)
     for later in range(1, ROUNDS + 1):
         goal = home if later < ROUNDS else np.arange(devices, dtype=np.int32)
         near_route, far_route = [], []
@@ -309,29 +311,30 @@
             for place in range(count):
                 start = int(home[group * count + place])
                 near_route.append((start, int(goal[group * count + (place ^ 1)])))
-                far_route.append((start, int(goal[group * count + far_place(place, count)])))
+                other = min(max(place + 2 * (place % 2) - 1, 0), count - 1)
+                far_route.append((start, int(goal[group * count + other])))
         from_far = lax.ppermute(far, axes, far_route)
         from_near = lax.ppermute(near, axes, near_route)
         if later < ROUNDS:
             far, near = pl.pallas_call(
                 functools.partial(next_kernel, order, later == ROUNDS - 1),
                 out_shape=[shape(BLK, order + (later + 1) * WIDTH)] * 2,
-                in_specs=[smem(), smem(), vmem(), vmem()],
+                in_specs=[vmem(), vmem()],
                 out_specs=[vmem()] * 2,
                 scratch_shapes=[store],
                 compiler_params=PARAMS,
                 name="next_round",
-            )(me, places, from_far, from_near)
+            )(from_far, from_near)
     work, basis = pl.pallas_call(
         last_kernel,
         out_shape=[shape(order, WIDTH)] * 2,
-        in_specs=[smem(), smem(), vmem(), vmem()],
+        in_specs=[vmem(), vmem()],
         out_specs=[hbm()] * 2,
         scratch_shapes=[pltpu.VMEM((order, WIDTH), jnp.float32)] * 2
         + [pltpu.SemaphoreType.DMA((1 + order // CHUNK,))],
         compiler_params=PARAMS,
         name="output",
-    )(me, jnp.asarray(support_table(count)), from_far, from_near)
+    )(from_far, from_near)
     return work[None], basis[None]
 
 

time: 96.7 us -> 93.7 us (0.969)
  blocking collectives: 0 us -> 30.2 us
  waiting for transfers between devices: 48.8 us -> 29.7 us
  starting transfers between devices: 27.1 us -> 15.9 us
  Pallas kernels: 19.2 us -> 16.9 us
    all_to_all x0 -> x1, blocking collectives: none -> 30.2 us  [shards(): moved = lax.all_to_all(dealt, axes, split_axis=0, concat_axis=0, tiled=True)]
    all_to_all x1 -> x0, waiting for transfers between devices: 19 us -> none  [shards(): moved = lax.all_to_all(dealt, axes, split_axis=0, concat_axis=0, tiled=True)]
    all_to_all x1 -> x0, starting transfers between devices: 11.1 us -> none  [shards(): moved = lax.all_to_all(dealt, axes, split_axis=0, concat_axis=0, tiled=True)]
    pallas_call x2, Pallas kernels: 9.6 us -> 8.52 us  [shards(): pl.pallas_call(functools.partial(next_kernel, order, later == ROUNDS - 1)...]
  transfers between devices with their start and end apart: 7 -> 6, of which waited for: 5 -> 4; matrix products, arithmetic and copies ran while one was open for 0% -> 0% of each run, Pallas kernels for 0% -> 0%
where the time goes in v5:
time: 93.7 us; the launch traced here: 93.5 us
  blocking collectives  30.2 us (32%)
  waiting for transfers between devices  29.7 us (32%)
  Pallas kernels  16.9 us (18%)
  starting transfers between devices  15.9 us (17%)
    all_to_all x1, blocking collectives, shards(): moved = lax.all_to_all(dealt, axes, split_axis=0, concat_axis=0, tiled=True)  30.2 us
    ppermute x3, waiting for transfers between devices, shards(): from_far = lax.ppermute(far, axes, far_route)  28.9 us
    ppermute x3, starting transfers between devices, shards(): from_near = lax.ppermute(near, axes, near_route)  12 us
    pallas_call x2, Pallas kernels, shards(): pl.pallas_call(functools.partial(next_kernel, order, later == ROUNDS - 1)...  8.52 us
    pallas_call x1, Pallas kernels, shards(): pl.pallas_call(first_kernel, out_shape=[shape(BLK, order + WIDTH)] * 2, i...  4.34 us
    ppermute x3, starting transfers between devices, shards(): from_far = lax.ppermute(far, axes, far_route)  3.92 us
    pallas_call x1, Pallas kernels, shards(): pl.pallas_call(deal_kernel, out_shape=shape(devices, slab, WIDTH), in_spe...  2.34 us
  transfers between devices with their start and end apart: 6, of which 4 were waited for; matrix products, arithmetic and copies ran while one was open for 0% of the time, Pallas kernels for 0%

profile of v5, /device:TPU:0, one launch (start us, length us, event | category | flops | bytes accessed | tf_op | source)
XLA Modules:
  0.0 93.5 jit_solution(5816164812295431608)
XLA Ops:
  0.6 2.3 %deal.1 = f32[128,16,128]{2,1,0:T(8,128)} custom-call(s32[8]{0:T(128)} %assignment.1, f32[8,16,2048]{2,1,0:T(8,128)} %stats.1), custom_call_target="tpu_custom_call" | custom-call | tf_op jit(solution)/shard_map/deal/pallas_call | solution.py:282
  3.0 30.2 %all_to_all.5 = f32[128,16,128]{2,1,0:T(8,128)S(1)} all-to-all(f32[128,16,128]{2,1,0:T(8,128)} %deal.1), channel_id=1, replica_groups=mesh['fac'=8,'jac'=16] {'fac','jac'}, dimensions={0} | all-to-all | bytes 2097152 | tf_op jit(solution)/shard_map/all_to_all | solution.py:295
  33.2 4.3 %first_round.1 = (f32[64,2176]{1,0:T(8,128)S(1)}, f32[64,2176]{1,0:T(8,128)S(1)}) custom-call(f32[2048,128]{1,0:T(8,128)S(1)} %bitcast.3), custom_call_target="tpu_custom_call" | custom-call | tf_op jit(solution)/shard_map/first_round/pallas_call | solution.py:298
  37.5 1.9 %collective-permute-start = (f32[64,2176]{1,0:T(8,128)S(1)}, f32[64,2176]{1,0:T(8,128)S(1)}, u32[]{:S(2)}, u32[]{:S(2)}) collective-permute-start(f32[64,2176]{1,0:T(8,128)S(1)} %get-tuple-element.10), channel_id=1, source_target_pairs={{1,1},{17,0},{0,17},{16,7},{7,16},{23,6},{6,23},{22,9},{9,22},{25,... | collective-permute-start | bytes 1671176 | tf_op jit(solution)/shard_map/ppermute | solution.py:316
  39.5 1.0 %collective-permute-start.1 = (f32[64,2176]{1,0:T(8,128)S(1)}, f32[64,2176]{1,0:T(8,128)S(1)}, u32[]{:S(2)}, u32[]{:S(2)}) collective-permute-start(f32[64,2176]{1,0:T(8,128)S(1)} %get-tuple-element.11), channel_id=1, source_target_pairs={{1,17},{17,1},{0,16},{16,0},{7,23},{23,7},{6,22},{22,6},{9,25},{25... | collective-permute-start | bytes 1671176 | tf_op jit(solution)/shard_map/ppermute | solution.py:317
  40.4 8.0 %collective-permute-done.from_far = f32[64,2176]{1,0:T(8,128)S(1)} collective-permute-done((f32[64,2176]{1,0:T(8,128)S(1)}, f32[64,2176]{1,0:T(8,128)S(1)}, u32[]{:S(2)}, u32[]{:S(2)}) %collective-permute-start) | collective-permute-done | bytes 557088 | tf_op jit(solution)/shard_map/ppermute | solution.py:316
  48.4 0.0 collective-permute-done.1.from_near
  48.4 4.4 %next_round.2 = (f32[64,2304]{1,0:T(8,128)S(1)}, f32[64,2304]{1,0:T(8,128)S(1)}) custom-call(f32[64,2176]{1,0:T(8,128)S(1)} %collective-permute-done.from_far, f32[64,2176]{1,0:T(8,128)S(1)} %collective-permute-done.1.from_near), custom_call_target="tpu_custom_call" | custom-call | tf_op jit(solution)/shard_map/next_round/pallas_call | solution.py:319
  52.8 1.9 %collective-permute-start.2 = (f32[64,2304]{1,0:T(8,128)S(1)}, f32[64,2304]{1,0:T(8,128)S(1)}, u32[]{:S(2)}, u32[]{:S(2)}) collective-permute-start(f32[64,2304]{1,0:T(8,128)S(1)} %get-tuple-element.12), channel_id=1, source_target_pairs={{1,1},{17,0},{0,17},{16,7},{7,16},{23,6},{6,23},{22,9},{9,22},{25,... | collective-permute-start | bytes 1769480 | tf_op jit(solution)/shard_map/ppermute | solution.py:316
  54.7 3.1 %collective-permute-start.3 = (f32[64,2304]{1,0:T(8,128)S(1)}, f32[64,2304]{1,0:T(8,128)S(1)}, u32[]{:S(2)}, u32[]{:S(2)}) collective-permute-start(f32[64,2304]{1,0:T(8,128)S(1)} %get-tuple-element.13), channel_id=1, source_target_pairs={{1,17},{17,1},{0,16},{16,0},{7,23},{23,7},{6,22},{22,6},{9,25},{25... | collective-permute-start | bytes 1769480 | tf_op jit(solution)/shard_map/ppermute | solution.py:317
  57.8 6.2 %collective-permute-done.2.from_far = f32[64,2304]{1,0:T(8,128)S(1)} collective-permute-done((f32[64,2304]{1,0:T(8,128)S(1)}, f32[64,2304]{1,0:T(8,128)S(1)}, u32[]{:S(2)}, u32[]{:S(2)}) %collective-permute-start.2) | collective-permute-done | bytes 589856 | tf_op jit(solution)/shard_map/ppermute | solution.py:316
  64.0 0.0 collective-permute-done.3.from_near
  64.0 4.1 %next_round.3 = (f32[64,2432]{1,0:T(8,128)S(1)}, f32[64,2432]{1,0:T(8,128)S(1)}) custom-call(f32[64,2304]{1,0:T(8,128)S(1)} %collective-permute-done.2.from_far, f32[64,2304]{1,0:T(8,128)S(1)} %collective-permute-done.3.from_near), custom_call_target="tpu_custom_call" | custom-call | tf_op jit(solution)/shard_map/next_round/pallas_call | solution.py:319
  68.1 0.1 collective-permute-start.4
  68.2 8.0 %collective-permute-start.5 = (f32[64,2432]{1,0:T(8,128)S(1)}, f32[64,2432]{1,0:T(8,128)S(1)}, u32[]{:S(2)}, u32[]{:S(2)}) collective-permute-start(f32[64,2432]{1,0:T(8,128)S(1)} %get-tuple-element.15), channel_id=1, source_target_pairs={{1,1},{17,0},{0,3},{16,2},{7,5},{23,4},{6,7},{22,6},{9,9},{25,8},{... | collective-permute-start | bytes 1867784 | tf_op jit(solution)/shard_map/ppermute | solution.py:317
  76.2 14.7 %collective-permute-done.4.from_far = f32[64,2432]{1,0:T(8,128)S(1)} collective-permute-done((f32[64,2432]{1,0:T(8,128)S(1)}, f32[64,2432]{1,0:T(8,128)S(1)}, u32[]{:S(2)}, u32[]{:S(2)}) %collective-permute-start.4) | collective-permute-done | bytes 622624 | tf_op jit(solution)/shard_map/ppermute | solution.py:316
  90.9 0.9 collective-permute-done.5.from_near
  91.8 1.7 %output.1 = (f32[2048,128]{1,0:T(8,128)}, f32[2048,128]{1,0:T(8,128)}) custom-call(f32[64,2432]{1,0:T(8,128)S(1)} %collective-permute-done.4.from_far, f32[64,2432]{1,0:T(8,128)S(1)} %collective-permute-done.5.from_near), custom_call_target="tpu_custom_call" | custom-call | tf_op jit(solution)/shard_map/output/pallas_call | solution.py:328
Async XLA Ops:
  37.5 10.9 %collective-permute-start = (f32[64,2176]{1,0:T(8,128)S(1)}, f32[64,2176]{1,0:T(8,128)S(1)}, u32[]{:S(2)}, u32[]{:S(2)}) collective-permute-start(f32[64,2176]{1,0:T(8,128)S(1)} %get-tuple-element.10), channel_id=1, source_target_pairs={{1,1},{17,0},{0,17},{16,7},{7,16},{23,6},{6,23},{22,9},{9,22},{25,... | collective-permute-start | bytes 1671176 | tf_op jit(solution)/shard_map/ppermute | solution.py:316
  39.5 8.9 %collective-permute-start.1 = (f32[64,2176]{1,0:T(8,128)S(1)}, f32[64,2176]{1,0:T(8,128)S(1)}, u32[]{:S(2)}, u32[]{:S(2)}) collective-permute-start(f32[64,2176]{1,0:T(8,128)S(1)} %get-tuple-element.11), channel_id=1, source_target_pairs={{1,17},{17,1},{0,16},{16,0},{7,23},{23,7},{6,22},{22,6},{9,25},{25... | collective-permute-start | bytes 1671176 | tf_op jit(solution)/shard_map/ppermute | solution.py:317
  52.8 11.2 %collective-permute-start.2 = (f32[64,2304]{1,0:T(8,128)S(1)}, f32[64,2304]{1,0:T(8,128)S(1)}, u32[]{:S(2)}, u32[]{:S(2)}) collective-permute-start(f32[64,2304]{1,0:T(8,128)S(1)} %get-tuple-element.12), channel_id=1, source_target_pairs={{1,1},{17,0},{0,17},{16,7},{7,16},{23,6},{6,23},{22,9},{9,22},{25,... | collective-permute-start | bytes 1769480 | tf_op jit(solution)/shard_map/ppermute | solution.py:316
  54.7 9.3 %collective-permute-start.3 = (f32[64,2304]{1,0:T(8,128)S(1)}, f32[64,2304]{1,0:T(8,128)S(1)}, u32[]{:S(2)}, u32[]{:S(2)}) collective-permute-start(f32[64,2304]{1,0:T(8,128)S(1)} %get-tuple-element.13), channel_id=1, source_target_pairs={{1,17},{17,1},{0,16},{16,0},{7,23},{23,7},{6,22},{22,6},{9,25},{25... | collective-permute-start | bytes 1769480 | tf_op jit(solution)/shard_map/ppermute | solution.py:317
  68.1 22.8 %collective-permute-start.4 = (f32[64,2432]{1,0:T(8,128)S(1)}, f32[64,2432]{1,0:T(8,128)S(1)}, u32[]{:S(2)}, u32[]{:S(2)}) collective-permute-start(f32[64,2432]{1,0:T(8,128)S(1)} %get-tuple-element.14), channel_id=1, source_target_pairs={{1,0},{17,2},{0,1},{16,4},{7,3},{23,6},{6,5},{22,8},{9,7},{25,10},... | collective-permute-start | bytes 1867784 | tf_op jit(solution)/shard_map/ppermute | solution.py:316
  68.2 23.6 %collective-permute-start.5 = (f32[64,2432]{1,0:T(8,128)S(1)}, f32[64,2432]{1,0:T(8,128)S(1)}, u32[]{:S(2)}, u32[]{:S(2)}) collective-permute-start(f32[64,2432]{1,0:T(8,128)S(1)} %get-tuple-element.15), channel_id=1, source_target_pairs={{1,1},{17,0},{0,3},{16,2},{7,5},{23,4},{6,7},{22,6},{9,9},{25,8},{... | collective-permute-start | bytes 1867784 | tf_op jit(solution)/shard_map/ppermute | solution.py:317

commit v6 on v5

--- a/solution.py
+++ b/solution.py
@@ -18,7 +18,7 @@
 WIDTH = 2 * BLK
 SECTIONS = 16
 SUB = 8
-GROUPS = BLK // SUB
+GROUPS = SECTIONS // SUB
 
 
 def lane_ids(rows):
@@ -39,16 +39,16 @@
 def small_rotation(gram, store, swapped):
     lanes = lane_ids(WIDTH)
     rows = lax.broadcasted_iota(jnp.int32, (WIDTH, WIDTH), 0)
-    upper_half = lanes & BLK
-    skew = ((rows - lanes) & (BLK - 1)) + upper_half
+    reach = SECTIONS - 1 - (lanes & (SECTIONS - 1))
+    skew = ((rows + reach) & (BLK - 1)) + jnp.where((lanes & SECTIONS) == 0, 0, BLK)
     store[...] = jnp.take_along_axis(gram, skew, axis=1).T
     low = lane_ids(SUB) < BLK
+    sublane = lax.broadcasted_iota(jnp.int32, (SUB, WIDTH), 0)
     aa, bb, tt, dd = [], [], [], []
-    for b in range(GROUPS):
-        top = store[pl.ds(b, SUB, stride=SUB), :]
-        bot = store[pl.ds(BLK + b, SUB, stride=SUB), :]
-        top_swap = pltpu.roll(top, BLK, 1)
-        bot_swap = pltpu.roll(bot, BLK, 1)
+    for v in range(GROUPS):
+        begin = SECTIONS - SUB * (v + 1)
+        top, bot = store[begin:begin + SUB, :], store[SECTIONS + begin:SECTIONS + begin + SUB, :]
+        top_swap, bot_swap = pltpu.roll(top, BLK, 1), pltpu.roll(bot, BLK, 1)
         blocks = (
             jnp.where(low, top, top_swap),
             jnp.where(low, bot, bot_swap),
@@ -59,8 +59,7 @@
         bb.append(jnp.where(swapped, blocks[2], blocks[1]))
         tt.append(jnp.where(swapped, blocks[1], blocks[2]))
         dd.append(jnp.where(swapped, blocks[0], blocks[3]))
-    first_rows = lax.broadcasted_iota(jnp.int32, (SUB, WIDTH), 0)
-    start = jnp.where(first_rows == 0, 1.0, 0.0).astype(jnp.float32)
+    start = jnp.where(sublane == 0, 1.0, 0.0).astype(jnp.float32)
     zero = jnp.zeros((SUB, WIDTH), jnp.float32)
     ru = [jnp.where(low, start, 0.0)] + [zero] * (GROUPS - 1)
     rl = [jnp.where(low, 0.0, start)] + [zero] * (GROUPS - 1)
@@ -68,42 +67,51 @@
     def spread(x, row):
         return jnp.broadcast_to(x[row:row + 1], (SUB, WIDTH))
 
-    alpha, beta, gamma = spread(aa[0], 0), spread(dd[0], 0), spread(bb[0], 0)
+    alpha, beta, gamma = (spread(x[0], SUB - 1) for x in (aa, dd, bb))
+    a_next, b_next, t_next, d_next = (spread(x[0], SUB - 2) for x in (aa, bb, tt, dd))
     for section in range(SECTIONS):
-        ahead = [spread(x[-1], SUB - 1) for x in (aa, bb, tt, dd)]
         c, s = angles(alpha, beta, gamma)
-        cc = [pltpu.roll(c, b, 1, stride=SUB, stride_axis=0) for b in range(GROUPS)]
-        ss = [pltpu.roll(s, b, 1, stride=SUB, stride_axis=0) for b in range(GROUPS)]
-        new_ru = [cc[b] * ru[b] - ss[b] * rl[b] for b in range(GROUPS)]
-        new_rl = [ss[b] * ru[b] + cc[b] * rl[b] for b in range(GROUPS)]
-        ru, rl = new_ru, new_rl
+        c_up, s_up = pltpu.roll(c, WIDTH - 1, 1), pltpu.roll(s, WIDTH - 1, 1)
+        for v in range(section // SUB + 1):
+            cc = pltpu.roll(c, SUB * v, 1, stride=1, stride_axis=0)
+            ss = pltpu.roll(s, SUB * v, 1, stride=1, stride_axis=0)
+            ru[v], rl[v] = cc * ru[v] - ss * rl[v], ss * ru[v] + cc * rl[v]
         if section == SECTIONS - 1:
             break
-        rl = [pltpu.roll(rl[-1], 1, 0)] + rl[:-1]
-        a1 = [cc[b] * aa[b] - ss[b] * bb[b] for b in range(GROUPS)]
-        b1 = [ss[b] * aa[b] + cc[b] * bb[b] for b in range(GROUPS)]
-        t1 = [cc[b] * tt[b] - ss[b] * dd[b] for b in range(GROUPS)]
-        d1 = [ss[b] * tt[b] + cc[b] * dd[b] for b in range(GROUPS)]
-        aa = [c * a1[b] - s * t1[b] for b in range(GROUPS)]
-        t2 = [s * a1[b] + c * t1[b] for b in range(GROUPS)]
-        b2 = [c * b1[b] - s * d1[b] for b in range(GROUPS)]
-        d2 = [s * b1[b] + c * d1[b] for b in range(GROUPS)]
-        new_alpha = c * (c * alpha - s * gamma) - s * (c * gamma - s * beta)
+        moved = [pltpu.roll(x, 1, 0) for x in rl]
+        rl = [jnp.where(sublane == 0, before, x) for before, x in zip([zero] + moved[:-1], moved)]
+        a1, t1 = c * alpha - s * gamma, c * gamma - s * beta
         new_beta = s * (s * alpha + c * gamma) + c * (s * gamma + c * beta)
-        c_up, s_up = pltpu.roll(c, WIDTH - 1, 1), pltpu.roll(s, WIDTH - 1, 1)
-        above = s_up * ahead[0] + c_up * ahead[1]
-        below = s_up * ahead[2] + c_up * ahead[3]
-        alpha, beta, gamma = new_alpha, pltpu.roll(new_beta, WIDTH - 1, 1), c * above - s * below
-        bb = [pltpu.roll(b2[-1], 1, 0)] + b2[:-1]
-        t2 = t2[1:] + [pltpu.roll(t2[0], SUB - 1, 0)]
-        tt = [pltpu.roll(x, WIDTH - 1, 1) for x in t2]
-        dd = [pltpu.roll(x, WIDTH - 1, 1) for x in d2]
-    for b in range(GROUPS):
-        store[pl.ds(b, SUB, stride=SUB), :] = ru[b]
-        store[pl.ds(BLK + b, SUB, stride=SUB), :] = rl[b]
-    offset = jnp.where(upper_half == 0, 0, SECTIONS - 1)
-    unskew = ((rows - lanes + offset) & (BLK - 1)) + upper_half
-    return jnp.take_along_axis(store[...].T, unskew, axis=1)
+        alpha, beta, rest = c * a1 - s * t1, pltpu.roll(new_beta, WIDTH - 1, 1), s * a1 + c * t1
+        b1, d1 = s_up * a_next + c_up * b_next, s_up * t_next + c_up * d_next
+        gamma = c * b1 - s * d1
+        if section == SECTIONS - 2:
+            continue
+        a1, t1 = c_up * a_next - s_up * b_next, c_up * t_next - s_up * d_next
+        a_next = c * a1 - s * t1
+        t_next, d_next = pltpu.roll(rest, WIDTH - 1, 1), pltpu.roll(s * b1 + c * d1, WIDTH - 1, 1)
+        kept = (SECTIONS - 1 - section) // SUB + 1
+        aa, bb, tt, dd = aa[:kept], bb[:kept], tt[:kept], dd[:kept]
+        for v in range(kept):
+            cc = pltpu.roll(c, BLK - SUB * (v + 1) + 1, 1, stride=1, stride_axis=0)
+            ss = pltpu.roll(s, BLK - SUB * (v + 1) + 1, 1, stride=1, stride_axis=0)
+            a1, b1 = cc * aa[v] - ss * bb[v], ss * aa[v] + cc * bb[v]
+            t1, d1 = cc * tt[v] - ss * dd[v], ss * tt[v] + cc * dd[v]
+            b2 = c * b1 - s * d1
+            if v == 0:
+                b_next = spread(b2, SUB - 3)
+            aa[v], bb[v] = c * a1 - s * t1, pltpu.roll(b2, 1, 0)
+            tt[v] = pltpu.roll(pltpu.roll(s * a1 + c * t1, WIDTH - 1, 1), SUB - 1, 0)
+            dd[v] = pltpu.roll(s * b1 + c * d1, WIDTH - 1, 1)
+        bb = [jnp.where(sublane == 0, after, x) for x, after in zip(bb, bb[1:] + [zero])]
+        tt = [jnp.where(sublane == SUB - 1, before, x) for before, x in zip([gamma] + tt[:-1], tt)]
+    for v in range(GROUPS):
+        store[SUB * v:SUB * (v + 1), :] = ru[v]
+        store[SECTIONS + SUB * v:SECTIONS + SUB * (v + 1), :] = rl[v]
+    upper = (lanes & BLK) == 0
+    diagonal = (rows - lanes + jnp.where(upper, 0, SECTIONS - 1)) & (BLK - 1)
+    index = (diagonal & (SECTIONS - 1)) + jnp.where(upper, 0, SECTIONS)
+    return jnp.where(diagonal < SECTIONS, jnp.take_along_axis(store[...].T, index, axis=1), 0.0)
 
 
 def deal_kernel(assignment, stats, out, owners, slabs, sems):
@@ -133,11 +141,8 @@
     return high, middle, low
 
 
-def gram_of(parts):
-    high, middle, low = parts
-    left = jnp.concatenate([high, middle, low], axis=0)
-    right = jnp.concatenate([high, middle], axis=0)
-    full = lax.dot_general(left, right, (((1,), (1,)), ((), ())), preferred_element_type=jnp.float32)
+def gram_of(parts, across):
+    full = jnp.dot(jnp.concatenate(parts, axis=0), across, preferred_element_type=jnp.float32)
     crossed = full[2 * WIDTH:, :WIDTH]
     small = full[WIDTH:2 * WIDTH, WIDTH:] + (crossed + crossed.T)
     return full[:WIDTH, :WIDTH] + (full[:WIDTH, WIDTH:] + full[WIDTH:2 * WIDTH, :WIDTH] + small)
@@ -189,8 +194,10 @@
 def first_kernel(work, far, near, store):
     place = place_here()
     order = work.shape[0]
-    parts = pieces(work[...].T)
-    rotation = leave_rotation(gram_of(parts), store, place, False)
+    straight = work[...]
+    parts = pieces(straight.T)
+    across = jnp.concatenate(pieces(straight)[:2], axis=1)
+    rotation = leave_rotation(gram_of(parts, across), store, place, False)
     apply(rotation, parts, near, far, 0, True)
     post(near, far, pl.ds(order, WIDTH), rotation)
 
@@ -199,7 +206,8 @@
     place = place_here()
     swapped = place % 2 == 0
     parts = pieces(jnp.concatenate([from_near[:, :order], from_far[:, :order]], axis=0))
-    rotation = leave_rotation(gram_of(parts), store, place, swapped)
+    across = jnp.concatenate(parts[:2], axis=0).T
+    rotation = leave_rotation(gram_of(parts, across), store, place, swapped)
     rotation = swap_halves(rotation, 1, swapped)
     apply(rotation, parts, near, far, 0, not final)
     blank = jnp.zeros((BLK, WIDTH), jnp.float32)

time: 93.7 us -> 92.7 us (0.989)
  Pallas kernels: 16.9 us -> 15.9 us
where the time goes in v6:
time: 92.7 us; the launch traced here: 92.4 us
  blocking collectives  30.2 us (33%)
  waiting for transfers between devices  29.7 us (32%)
  Pallas kernels  15.9 us (17%)
  starting transfers between devices  15.9 us (17%)
    all_to_all x1, blocking collectives, shards(): moved = lax.all_to_all(dealt, axes, split_axis=0, concat_axis=0, tiled=True)  30.2 us
    ppermute x3, waiting for transfers between devices, shards(): from_far = lax.ppermute(far, axes, far_route)  28.9 us
    ppermute x3, starting transfers between devices, shards(): from_near = lax.ppermute(near, axes, near_route)  12 us
    pallas_call x2, Pallas kernels, shards(): pl.pallas_call(functools.partial(next_kernel, order, later == ROUNDS - 1)...  7.87 us
    pallas_call x1, Pallas kernels, shards(): pl.pallas_call(first_kernel, out_shape=[shape(BLK, order + WIDTH)] * 2, i...  3.95 us
    ppermute x3, starting transfers between devices, shards(): from_far = lax.ppermute(far, axes, far_route)  3.92 us
    pallas_call x1, Pallas kernels, shards(): pl.pallas_call(deal_kernel, out_shape=shape(devices, slab, WIDTH), in_spe...  2.34 us
  transfers between devices with their start and end apart: 6, of which 4 were waited for; matrix products, arithmetic and copies ran while one was open for 0% of the time, Pallas kernels for 0%

profile of v6, /device:TPU:0, one launch (start us, length us, event | category | flops | bytes accessed | tf_op | source)
XLA Modules:
  0.0 92.4 jit_solution(4715129055599923872)
XLA Ops:
  0.6 2.3 %deal.1 = f32[128,16,128]{2,1,0:T(8,128)} custom-call(s32[8]{0:T(128)} %assignment.1, f32[8,16,2048]{2,1,0:T(8,128)} %stats.1), custom_call_target="tpu_custom_call" | custom-call | tf_op jit(solution)/shard_map/deal/pallas_call | solution.py:290
  3.0 30.2 %all_to_all.5 = f32[128,16,128]{2,1,0:T(8,128)S(1)} all-to-all(f32[128,16,128]{2,1,0:T(8,128)} %deal.1), channel_id=1, replica_groups=mesh['fac'=8,'jac'=16] {'fac','jac'}, dimensions={0} | all-to-all | bytes 2097152 | tf_op jit(solution)/shard_map/all_to_all | solution.py:303
  33.2 4.0 %first_round.1 = (f32[64,2176]{1,0:T(8,128)S(1)}, f32[64,2176]{1,0:T(8,128)S(1)}) custom-call(f32[2048,128]{1,0:T(8,128)S(1)} %bitcast.3), custom_call_target="tpu_custom_call" | custom-call | tf_op jit(solution)/shard_map/first_round/pallas_call | solution.py:306
  37.1 1.9 %collective-permute-start = (f32[64,2176]{1,0:T(8,128)S(1)}, f32[64,2176]{1,0:T(8,128)S(1)}, u32[]{:S(2)}, u32[]{:S(2)}) collective-permute-start(f32[64,2176]{1,0:T(8,128)S(1)} %get-tuple-element.10), channel_id=1, source_target_pairs={{1,1},{17,0},{0,17},{16,7},{7,16},{23,6},{6,23},{22,9},{9,22},{25,... | collective-permute-start | bytes 1671176 | tf_op jit(solution)/shard_map/ppermute | solution.py:324
  39.1 1.0 %collective-permute-start.1 = (f32[64,2176]{1,0:T(8,128)S(1)}, f32[64,2176]{1,0:T(8,128)S(1)}, u32[]{:S(2)}, u32[]{:S(2)}) collective-permute-start(f32[64,2176]{1,0:T(8,128)S(1)} %get-tuple-element.11), channel_id=1, source_target_pairs={{1,17},{17,1},{0,16},{16,0},{7,23},{23,7},{6,22},{22,6},{9,25},{25... | collective-permute-start | bytes 1671176 | tf_op jit(solution)/shard_map/ppermute | solution.py:325
  40.0 8.0 %collective-permute-done.from_far = f32[64,2176]{1,0:T(8,128)S(1)} collective-permute-done((f32[64,2176]{1,0:T(8,128)S(1)}, f32[64,2176]{1,0:T(8,128)S(1)}, u32[]{:S(2)}, u32[]{:S(2)}) %collective-permute-start) | collective-permute-done | bytes 557088 | tf_op jit(solution)/shard_map/ppermute | solution.py:324
  48.0 0.0 collective-permute-done.1.from_near
  48.0 4.1 %next_round.2 = (f32[64,2304]{1,0:T(8,128)S(1)}, f32[64,2304]{1,0:T(8,128)S(1)}) custom-call(f32[64,2176]{1,0:T(8,128)S(1)} %collective-permute-done.from_far, f32[64,2176]{1,0:T(8,128)S(1)} %collective-permute-done.1.from_near), custom_call_target="tpu_custom_call" | custom-call | tf_op jit(solution)/shard_map/next_round/pallas_call | solution.py:327
  52.1 1.9 %collective-permute-start.2 = (f32[64,2304]{1,0:T(8,128)S(1)}, f32[64,2304]{1,0:T(8,128)S(1)}, u32[]{:S(2)}, u32[]{:S(2)}) collective-permute-start(f32[64,2304]{1,0:T(8,128)S(1)} %get-tuple-element.12), channel_id=1, source_target_pairs={{1,1},{17,0},{0,17},{16,7},{7,16},{23,6},{6,23},{22,9},{9,22},{25,... | collective-permute-start | bytes 1769480 | tf_op jit(solution)/shard_map/ppermute | solution.py:324
  54.0 3.1 %collective-permute-start.3 = (f32[64,2304]{1,0:T(8,128)S(1)}, f32[64,2304]{1,0:T(8,128)S(1)}, u32[]{:S(2)}, u32[]{:S(2)}) collective-permute-start(f32[64,2304]{1,0:T(8,128)S(1)} %get-tuple-element.13), channel_id=1, source_target_pairs={{1,17},{17,1},{0,16},{16,0},{7,23},{23,7},{6,22},{22,6},{9,25},{25... | collective-permute-start | bytes 1769480 | tf_op jit(solution)/shard_map/ppermute | solution.py:325
  57.1 6.2 %collective-permute-done.2.from_far = f32[64,2304]{1,0:T(8,128)S(1)} collective-permute-done((f32[64,2304]{1,0:T(8,128)S(1)}, f32[64,2304]{1,0:T(8,128)S(1)}, u32[]{:S(2)}, u32[]{:S(2)}) %collective-permute-start.2) | collective-permute-done | bytes 589856 | tf_op jit(solution)/shard_map/ppermute | solution.py:324
  63.3 0.0 collective-permute-done.3.from_near
  63.3 3.8 %next_round.3 = (f32[64,2432]{1,0:T(8,128)S(1)}, f32[64,2432]{1,0:T(8,128)S(1)}) custom-call(f32[64,2304]{1,0:T(8,128)S(1)} %collective-permute-done.2.from_far, f32[64,2304]{1,0:T(8,128)S(1)} %collective-permute-done.3.from_near), custom_call_target="tpu_custom_call" | custom-call | tf_op jit(solution)/shard_map/next_round/pallas_call | solution.py:327
  67.1 0.1 collective-permute-start.4
  67.2 8.0 %collective-permute-start.5 = (f32[64,2432]{1,0:T(8,128)S(1)}, f32[64,2432]{1,0:T(8,128)S(1)}, u32[]{:S(2)}, u32[]{:S(2)}) collective-permute-start(f32[64,2432]{1,0:T(8,128)S(1)} %get-tuple-element.15), channel_id=1, source_target_pairs={{1,1},{17,0},{0,3},{16,2},{7,5},{23,4},{6,7},{22,6},{9,9},{25,8},{... | collective-permute-start | bytes 1867784 | tf_op jit(solution)/shard_map/ppermute | solution.py:325
  75.2 14.7 %collective-permute-done.4.from_far = f32[64,2432]{1,0:T(8,128)S(1)} collective-permute-done((f32[64,2432]{1,0:T(8,128)S(1)}, f32[64,2432]{1,0:T(8,128)S(1)}, u32[]{:S(2)}, u32[]{:S(2)}) %collective-permute-start.4) | collective-permute-done | bytes 622624 | tf_op jit(solution)/shard_map/ppermute | solution.py:324
  89.9 0.9 collective-permute-done.5.from_near
  90.7 1.7 %output.1 = (f32[2048,128]{1,0:T(8,128)}, f32[2048,128]{1,0:T(8,128)}) custom-call(f32[64,2432]{1,0:T(8,128)S(1)} %collective-permute-done.4.from_far, f32[64,2432]{1,0:T(8,128)S(1)} %collective-permute-done.5.from_near), custom_call_target="tpu_custom_call" | custom-call | tf_op jit(solution)/shard_map/output/pallas_call | solution.py:336
Async XLA Ops:
  37.1 10.9 %collective-permute-start = (f32[64,2176]{1,0:T(8,128)S(1)}, f32[64,2176]{1,0:T(8,128)S(1)}, u32[]{:S(2)}, u32[]{:S(2)}) collective-permute-start(f32[64,2176]{1,0:T(8,128)S(1)} %get-tuple-element.10), channel_id=1, source_target_pairs={{1,1},{17,0},{0,17},{16,7},{7,16},{23,6},{6,23},{22,9},{9,22},{25,... | collective-permute-start | bytes 1671176 | tf_op jit(solution)/shard_map/ppermute | solution.py:324
  39.1 8.9 %collective-permute-start.1 = (f32[64,2176]{1,0:T(8,128)S(1)}, f32[64,2176]{1,0:T(8,128)S(1)}, u32[]{:S(2)}, u32[]{:S(2)}) collective-permute-start(f32[64,2176]{1,0:T(8,128)S(1)} %get-tuple-element.11), channel_id=1, source_target_pairs={{1,17},{17,1},{0,16},{16,0},{7,23},{23,7},{6,22},{22,6},{9,25},{25... | collective-permute-start | bytes 1671176 | tf_op jit(solution)/shard_map/ppermute | solution.py:325
  52.1 11.2 %collective-permute-start.2 = (f32[64,2304]{1,0:T(8,128)S(1)}, f32[64,2304]{1,0:T(8,128)S(1)}, u32[]{:S(2)}, u32[]{:S(2)}) collective-permute-start(f32[64,2304]{1,0:T(8,128)S(1)} %get-tuple-element.12), channel_id=1, source_target_pairs={{1,1},{17,0},{0,17},{16,7},{7,16},{23,6},{6,23},{22,9},{9,22},{25,... | collective-permute-start | bytes 1769480 | tf_op jit(solution)/shard_map/ppermute | solution.py:324
  54.0 9.3 %collective-permute-start.3 = (f32[64,2304]{1,0:T(8,128)S(1)}, f32[64,2304]{1,0:T(8,128)S(1)}, u32[]{:S(2)}, u32[]{:S(2)}) collective-permute-start(f32[64,2304]{1,0:T(8,128)S(1)} %get-tuple-element.13), channel_id=1, source_target_pairs={{1,17},{17,1},{0,16},{16,0},{7,23},{23,7},{6,22},{22,6},{9,25},{25... | collective-permute-start | bytes 1769480 | tf_op jit(solution)/shard_map/ppermute | solution.py:325
  67.1 22.8 %collective-permute-start.4 = (f32[64,2432]{1,0:T(8,128)S(1)}, f32[64,2432]{1,0:T(8,128)S(1)}, u32[]{:S(2)}, u32[]{:S(2)}) collective-permute-start(f32[64,2432]{1,0:T(8,128)S(1)} %get-tuple-element.14), channel_id=1, source_target_pairs={{1,0},{17,2},{0,1},{16,4},{7,3},{23,6},{6,5},{22,8},{9,7},{25,10},... | collective-permute-start | bytes 1867784 | tf_op jit(solution)/shard_map/ppermute | solution.py:324
  67.2 23.6 %collective-permute-start.5 = (f32[64,2432]{1,0:T(8,128)S(1)}, f32[64,2432]{1,0:T(8,128)S(1)}, u32[]{:S(2)}, u32[]{:S(2)}) collective-permute-start(f32[64,2432]{1,0:T(8,128)S(1)} %get-tuple-element.15), channel_id=1, source_target_pairs={{1,1},{17,0},{0,3},{16,2},{7,5},{23,4},{6,7},{22,6},{9,9},{25,8},{... | collective-permute-start | bytes 1867784 | tf_op jit(solution)/shard_map/ppermute | solution.py:325

commit v7 on v6

--- a/solution.py
+++ b/solution.py
@@ -202,57 +202,76 @@
     post(near, far, pl.ds(order, WIDTH), rotation)
 
 
-def next_kernel(order, final, from_far, from_near, far, near, store):
+def turned_pair(order, from_far, from_near, far, near, store, exact):
     place = place_here()
     swapped = place % 2 == 0
     parts = pieces(jnp.concatenate([from_near[:, :order], from_far[:, :order]], axis=0))
     across = jnp.concatenate(parts[:2], axis=0).T
     rotation = leave_rotation(gram_of(parts, across), store, place, swapped)
     rotation = swap_halves(rotation, 1, swapped)
-    apply(rotation, parts, near, far, 0, not final)
+    apply(rotation, parts, near, far, 0, exact)
+    return rotation
+
+
+def next_kernel(order, from_far, from_near, far, near, store):
+    rotation = turned_pair(order, from_far, from_near, far, near, store, True)
     blank = jnp.zeros((BLK, WIDTH), jnp.float32)
-    near_basis = [from_near[:, c:c + WIDTH] for c in range(order, from_near.shape[1], WIDTH)]
-    far_basis = [from_far[:, c:c + WIDTH] for c in range(order, from_far.shape[1], WIDTH)]
-    if final:
-        near_basis, far_basis = near_basis + [blank], [far_basis[1], blank, far_basis[0]]
-    else:
-        near_basis, far_basis = near_basis + [blank], [blank] + far_basis
-    columns = [jnp.concatenate(halves, axis=0) for halves in zip(near_basis, far_basis)]
+    columns = [
+        jnp.concatenate([from_near[:, order:], blank], axis=0),
+        jnp.concatenate([blank, from_far[:, order:]], axis=0),
+    ]
     apply(rotation, pieces(jnp.concatenate(columns, axis=1)), near, far, order, False)
 
 
-def last_kernel(from_far, from_near, work, basis, work_store, basis_store, sems):
-    order = work.shape[0]
+def final_kernel(order, from_far, from_near, far, near, turn, store):
+    turn[...] = turned_pair(order, from_far, from_near, far, near, store, False)
+
+
+def final_basis(order, turn, from_far, from_near, far, near):
+    blank = jnp.zeros((BLK, WIDTH), jnp.float32)
+    first, second = pl.ds(order, WIDTH), pl.ds(order + WIDTH, WIDTH)
+    columns = [
+        jnp.concatenate([from_near[:, first], from_far[:, second]], axis=0),
+        jnp.concatenate([from_near[:, second], blank], axis=0),
+        jnp.concatenate([blank, from_far[:, first]], axis=0),
+    ]
+    apply(turn[...], pieces(jnp.concatenate(columns, axis=1)), near, far, 0, False)
+
+
+def work_output(from_far, from_near, work, done, store, sems):
+    done[...] = jnp.zeros_like(done)
+    even = lax.axis_index("jac") % 2 == 0
+    copies = []
+    for number, begin in enumerate(range(0, work.shape[0], CHUNK)):
+        rows = pl.ds(begin, CHUNK)
+        near, far = from_near[:, rows], from_far[:, rows]
+        pair = [jnp.where(even, far, near), jnp.where(even, near, far)]
+        store[rows, :] = jnp.concatenate(pair, axis=0).T
+        copies.append(pltpu.make_async_copy(store.at[rows], work.at[rows], sems.at[number]))
+        copies[-1].start()
+    for copy in copies:
+        copy.wait()
+
+
+def basis_output(from_far, from_near, after, basis):
     place = lax.axis_index("jac")
     count = lax.axis_size("jac")
+    even = place % 2 == 0
     next_chip = far_place(place, count)
     rows = [
         [place ^ 1, next_chip, far_place(place ^ 1, count) ^ 1],
         [next_chip, far_place(next_chip ^ 1, count), far_place(next_chip, count) ^ 1],
     ]
-    even = place % 2 == 0
-    basis_store[...] = jnp.zeros_like(basis_store)
-    chunks = (from_near.shape[1] - order) // WIDTH
+    basis[...] = jnp.zeros_like(basis)
     left_half = lane_ids(WIDTH) < BLK
-    for chunk in range(chunks):
-        columns = pl.ds(order + chunk * WIDTH, WIDTH)
+    for chunk in range(len(rows[0])):
+        columns = pl.ds(chunk * WIDTH, WIDTH)
         piece = jnp.concatenate([from_near[:, columns], from_far[:, columns]], axis=0).T
         piece = swap_halves(piece, 1, even)
         for half in range(2):
             row = pl.multiple_of(rows[half][chunk] * WIDTH, WIDTH)
             left = jnp.logical_xor(even, half == 0)
-            basis_store[pl.ds(row, WIDTH), :] += jnp.where(left_half == left, piece, 0.0)
-    copies = [pltpu.make_async_copy(basis_store, basis, sems.at[0])]
-    copies[0].start()
-    for number, begin in enumerate(range(0, order, CHUNK)):
-        rows = pl.ds(begin, CHUNK)
-        near, far = from_near[:, rows], from_far[:, rows]
-        pair = [jnp.where(even, far, near), jnp.where(even, near, far)]
-        work_store[rows, :] = jnp.concatenate(pair, axis=0).T
-        copies.append(pltpu.make_async_copy(work_store.at[rows], work.at[rows], sems.at[number + 1]))
-        copies[-1].start()
-    for copy in copies:
-        copy.wait()
+            basis[pl.ds(row, WIDTH), :] += jnp.where(left_half == left, piece, 0.0)
 
 
 def far_place(place, count):
@@ -262,6 +281,17 @@
 def home_of(group, place, count):
     x, z = CHAINS[group % 2][place // 2]
     return (group // 2 * 2 + place % 2) * count + 4 * x + z
+
+
+def routes(home, goal, factors, count):
+    near, far = [], []
+    for group in range(factors):
+        for place in range(count):
+            start = int(home[group * count + place])
+            near.append((start, int(goal[group * count + (place ^ 1)])))
+            other = min(max(place + 2 * (place % 2) - 1, 0), count - 1)
+            far.append((start, int(goal[group * count + other])))
+    return near, far
 
 
 def vmem():
@@ -312,37 +342,60 @@
         compiler_params=PARAMS,
         name="first_round",
     )(work)
-    for later in range(1, ROUNDS + 1):
-        goal = home if later < ROUNDS else np.arange(devices, dtype=np.int32)
-        near_route, far_route = [], []
-        for group in range(factors):
-            for place in range(count):
-                start = int(home[group * count + place])
-                near_route.append((start, int(goal[group * count + (place ^ 1)])))
-                other = min(max(place + 2 * (place % 2) - 1, 0), count - 1)
-                far_route.append((start, int(goal[group * count + other])))
+    true_home = np.arange(devices, dtype=np.int32)
+    for later in range(1, ROUNDS):
+        near_route, far_route = routes(home, home, factors, count)
         from_far = lax.ppermute(far, axes, far_route)
         from_near = lax.ppermute(near, axes, near_route)
-        if later < ROUNDS:
+        if later < ROUNDS - 1:
             far, near = pl.pallas_call(
-                functools.partial(next_kernel, order, later == ROUNDS - 1),
-                out_shape=[shape(BLK, order + (later + 1) * WIDTH)] * 2,
-                in_specs=[vmem(), vmem()],
+                functools.partial(next_kernel, order),
+                out_shape=[shape(BLK, order + 2 * WIDTH)] * 2,
+                in_specs=[vmem()] * 2,
                 out_specs=[vmem()] * 2,
                 scratch_shapes=[store],
                 compiler_params=PARAMS,
                 name="next_round",
             )(from_far, from_near)
-    work, basis = pl.pallas_call(
-        last_kernel,
-        out_shape=[shape(order, WIDTH)] * 2,
-        in_specs=[vmem(), vmem()],
-        out_specs=[hbm()] * 2,
-        scratch_shapes=[pltpu.VMEM((order, WIDTH), jnp.float32)] * 2
-        + [pltpu.SemaphoreType.DMA((1 + order // CHUNK,))],
+    far, near, turn = pl.pallas_call(
+        functools.partial(final_kernel, order),
+        out_shape=[shape(BLK, order), shape(BLK, order), shape(WIDTH, WIDTH)],
+        in_specs=[vmem()] * 2,
+        out_specs=[vmem()] * 3,
+        scratch_shapes=[store],
         compiler_params=PARAMS,
-        name="output",
+        name="final_round",
     )(from_far, from_near)
+    far_basis, near_basis = pl.pallas_call(
+        functools.partial(final_basis, order),
+        out_shape=[shape(BLK, ROUNDS * WIDTH)] * 2,
+        in_specs=[vmem()] * 3,
+        out_specs=[vmem()] * 2,
+        compiler_params=PARAMS,
+        name="final_basis",
+    )(turn, from_far, from_near)
+    near_route, far_route = routes(home, true_home, factors, count)
+    from_far = lax.ppermute(far, axes, far_route)
+    from_near = lax.ppermute(near, axes, near_route)
+    from_far_basis = lax.ppermute(far_basis, axes, far_route)
+    from_near_basis = lax.ppermute(near_basis, axes, near_route)
+    work, done = pl.pallas_call(
+        work_output,
+        out_shape=[shape(order, WIDTH), shape(SUB, WIDTH)],
+        in_specs=[vmem()] * 2,
+        out_specs=[hbm(), vmem()],
+        scratch_shapes=[pltpu.VMEM((order, WIDTH), jnp.float32), pltpu.SemaphoreType.DMA((order // CHUNK,))],
+        compiler_params=PARAMS,
+        name="work_output",
+    )(from_far, from_near)
+    basis = pl.pallas_call(
+        basis_output,
+        out_shape=shape(order, WIDTH),
+        in_specs=[vmem()] * 3,
+        out_specs=vmem(),
+        compiler_params=PARAMS,
+        name="basis_output",
+    )(from_far_basis, from_near_basis, done)
     return work[None], basis[None]
 
 

time: 92.7 us -> 92.1 us (level)
  waiting for transfers between devices: 29.7 us -> 26.3 us
  starting transfers between devices: 15.9 us -> 17.9 us
    ppermute x3, waiting for transfers between devices: 28.9 us -> 24.5 us  [shards(): from_far = lax.ppermute(far, axes, far_route)]
    ppermute x0 -> x2, starting transfers between devices: none -> 2.01 us  [the longest x1 1.93 us: shards(): from_near_basis = lax.ppermute(near_basis, axes, near_route)]
    pallas_call x3 -> x5, Pallas kernels: 9.56 us -> 10.3 us  [the longest x1 4.08 us: shards(): pl.pallas_call(functools.partial(next_kernel, order), out_shape=[shape(BL...]
  transfers between devices with their start and end apart: 6 -> 8, of which waited for: 4 -> 5; matrix products, arithmetic and copies ran while one was open for 0% -> 0% of each run, Pallas kernels for 0% -> 1%
where the time goes in v7:
time: 92.1 us; the launch traced here: 91.8 us
  blocking collectives  30.2 us (33%)
  waiting for transfers between devices  26.3 us (29%)
  starting transfers between devices  17.9 us (19%)
  Pallas kernels  16.6 us (18%)
    all_to_all x1, blocking collectives, shards(): moved = lax.all_to_all(dealt, axes, split_axis=0, concat_axis=0, tiled=True)  30.2 us
    ppermute x3, waiting for transfers between devices, shards(): from_far = lax.ppermute(far, axes, far_route)  24.5 us
    ppermute x3, starting transfers between devices, shards(): from_near = lax.ppermute(near, axes, near_route)  12 us
    pallas_call x1, Pallas kernels, shards(): pl.pallas_call(functools.partial(next_kernel, order), out_shape=[shape(BL...  4.08 us
    pallas_call x1, Pallas kernels, shards(): pl.pallas_call(first_kernel, out_shape=[shape(BLK, order + WIDTH)] * 2, i...  3.95 us
    ppermute x3, starting transfers between devices, shards(): from_far = lax.ppermute(far, axes, far_route)  3.92 us
    pallas_call x1, Pallas kernels, shards(): pl.pallas_call(functools.partial(final_kernel, order), out_shape=[shape(B...  3.62 us
    pallas_call x1, Pallas kernels, shards(): pl.pallas_call(deal_kernel, out_shape=shape(devices, slab, WIDTH), in_spe...  2.34 us
  transfers between devices with their start and end apart: 8, of which 5 were waited for; matrix products, arithmetic and copies ran while one was open for 0% of the time, Pallas kernels for 1%

profile of v7, /device:TPU:0, one launch (start us, length us, event | category | flops | bytes accessed | tf_op | source)
XLA Modules:
  0.0 91.8 jit_solution(6501811434617181891)
XLA Ops:
  0.6 2.3 %deal.1 = f32[128,16,128]{2,1,0:T(8,128)} custom-call(s32[8]{0:T(128)} %assignment.1, f32[8,16,2048]{2,1,0:T(8,128)} %stats.1), custom_call_target="tpu_custom_call" | custom-call | tf_op jit(solution)/shard_map/deal/pallas_call | solution.py:320
  3.0 30.2 %all_to_all.5 = f32[128,16,128]{2,1,0:T(8,128)S(1)} all-to-all(f32[128,16,128]{2,1,0:T(8,128)} %deal.1), channel_id=1, replica_groups=mesh['fac'=8,'jac'=16] {'fac','jac'}, dimensions={0} | all-to-all | bytes 2097152 | tf_op jit(solution)/shard_map/all_to_all | solution.py:333
  33.2 4.0 %first_round.1 = (f32[64,2176]{1,0:T(8,128)S(1)}, f32[64,2176]{1,0:T(8,128)S(1)}) custom-call(f32[2048,128]{1,0:T(8,128)S(1)} %bitcast.3), custom_call_target="tpu_custom_call" | custom-call | tf_op jit(solution)/shard_map/first_round/pallas_call | solution.py:336
  37.1 1.9 %collective-permute-start = (f32[64,2176]{1,0:T(8,128)S(1)}, f32[64,2176]{1,0:T(8,128)S(1)}, u32[]{:S(2)}, u32[]{:S(2)}) collective-permute-start(f32[64,2176]{1,0:T(8,128)S(1)} %get-tuple-element.13), channel_id=1, source_target_pairs={{1,1},{17,0},{0,17},{16,7},{7,16},{23,6},{6,23},{22,9},{9,22},{25,... | collective-permute-start | bytes 1671176 | tf_op jit(solution)/shard_map/ppermute | solution.py:348
  39.1 1.0 %collective-permute-start.1 = (f32[64,2176]{1,0:T(8,128)S(1)}, f32[64,2176]{1,0:T(8,128)S(1)}, u32[]{:S(2)}, u32[]{:S(2)}) collective-permute-start(f32[64,2176]{1,0:T(8,128)S(1)} %get-tuple-element.14), channel_id=1, source_target_pairs={{1,17},{17,1},{0,16},{16,0},{7,23},{23,7},{6,22},{22,6},{9,25},{25... | collective-permute-start | bytes 1671176 | tf_op jit(solution)/shard_map/ppermute | solution.py:349
  40.0 8.0 %collective-permute-done.from_far = f32[64,2176]{1,0:T(8,128)S(1)} collective-permute-done((f32[64,2176]{1,0:T(8,128)S(1)}, f32[64,2176]{1,0:T(8,128)S(1)}, u32[]{:S(2)}, u32[]{:S(2)}) %collective-permute-start) | collective-permute-done | bytes 557088 | tf_op jit(solution)/shard_map/ppermute | solution.py:348
  48.0 0.0 collective-permute-done.1.from_near
  48.0 4.1 %next_round.1 = (f32[64,2304]{1,0:T(8,128)S(1)}, f32[64,2304]{1,0:T(8,128)S(1)}) custom-call(f32[64,2176]{1,0:T(8,128)S(1)} %collective-permute-done.from_far, f32[64,2176]{1,0:T(8,128)S(1)} %collective-permute-done.1.from_near), custom_call_target="tpu_custom_call" | custom-call | tf_op jit(solution)/shard_map/next_round/pallas_call | solution.py:351
  52.1 1.9 %collective-permute-start.2 = (f32[64,2304]{1,0:T(8,128)S(1)}, f32[64,2304]{1,0:T(8,128)S(1)}, u32[]{:S(2)}, u32[]{:S(2)}) collective-permute-start(f32[64,2304]{1,0:T(8,128)S(1)} %get-tuple-element.15), channel_id=1, source_target_pairs={{1,1},{17,0},{0,17},{16,7},{7,16},{23,6},{6,23},{22,9},{9,22},{25,... | collective-permute-start | bytes 1769480 | tf_op jit(solution)/shard_map/ppermute | solution.py:348
  54.0 3.1 %collective-permute-start.3 = (f32[64,2304]{1,0:T(8,128)S(1)}, f32[64,2304]{1,0:T(8,128)S(1)}, u32[]{:S(2)}, u32[]{:S(2)}) collective-permute-start(f32[64,2304]{1,0:T(8,128)S(1)} %get-tuple-element.16), channel_id=1, source_target_pairs={{1,17},{17,1},{0,16},{16,0},{7,23},{23,7},{6,22},{22,6},{9,25},{25... | collective-permute-start | bytes 1769480 | tf_op jit(solution)/shard_map/ppermute | solution.py:349
  57.1 6.2 %collective-permute-done.2.from_far = f32[64,2304]{1,0:T(8,128)S(1)} collective-permute-done((f32[64,2304]{1,0:T(8,128)S(1)}, f32[64,2304]{1,0:T(8,128)S(1)}, u32[]{:S(2)}, u32[]{:S(2)}) %collective-permute-start.2) | collective-permute-done | bytes 589856 | tf_op jit(solution)/shard_map/ppermute | solution.py:348
  63.3 0.0 collective-permute-done.3.from_near
  63.3 3.6 %final_round.1 = (f32[64,2048]{1,0:T(8,128)S(1)}, f32[64,2048]{1,0:T(8,128)S(1)}, f32[128,128]{1,0:T(8,128)S(1)}) custom-call(f32[64,2304]{1,0:T(8,128)S(1)} %collective-permute-done.2.from_far, f32[64,2304]{1,0:T(8,128)S(1)} %collective-permute-done.3.from_near), custom_call_target="tpu_custom_call" | custom-call | tf_op jit(solution)/shard_map/final_round/pallas_call | solution.py:360
  66.9 0.1 collective-permute-start.4
  67.0 8.0 %collective-permute-start.5 = (f32[64,2048]{1,0:T(8,128)S(1)}, f32[64,2048]{1,0:T(8,128)S(1)}, u32[]{:S(2)}, u32[]{:S(2)}) collective-permute-start(f32[64,2048]{1,0:T(8,128)S(1)} %get-tuple-element.18), channel_id=1, source_target_pairs={{1,1},{17,0},{0,3},{16,2},{7,5},{23,4},{6,7},{22,6},{9,9},{25,8},{... | collective-permute-start | bytes 1572872 | tf_op jit(solution)/shard_map/ppermute | solution.py:379
  75.0 0.2 final_basis.1
  75.2 0.1 collective-permute-start.6
  75.3 1.9 %collective-permute-start.7 = (f32[64,384]{1,0:T(8,128)S(1)}, f32[64,384]{1,0:T(8,128)S(1)}, u32[]{:S(2)}, u32[]{:S(2)}) collective-permute-start(f32[64,384]{1,0:T(8,128)S(1)} %get-tuple-element.22), channel_id=1, source_target_pairs={{1,1},{17,0},{0,3},{16,2},{7,5},{23,4},{6,7},{22,6},{9,9},{25,8},{... | collective-permute-start | bytes 294920 | tf_op jit(solution)/shard_map/ppermute | solution.py:381
  77.2 10.4 %collective-permute-done.4.from_far = f32[64,2048]{1,0:T(8,128)S(1)} collective-permute-done((f32[64,2048]{1,0:T(8,128)S(1)}, f32[64,2048]{1,0:T(8,128)S(1)}, u32[]{:S(2)}, u32[]{:S(2)}) %collective-permute-start.4) | collective-permute-done | bytes 524320 | tf_op jit(solution)/shard_map/ppermute | solution.py:378
  87.6 1.7 %collective-permute-done.5.from_near = f32[64,2048]{1,0:T(8,128)S(1)} collective-permute-done((f32[64,2048]{1,0:T(8,128)S(1)}, f32[64,2048]{1,0:T(8,128)S(1)}, u32[]{:S(2)}, u32[]{:S(2)}) %collective-permute-start.5) | collective-permute-done | bytes 524320 | tf_op jit(solution)/shard_map/ppermute | solution.py:379
  89.3 1.1 %work_output.1 = (f32[2048,128]{1,0:T(8,128)}, f32[8,128]{1,0:T(8,128)S(1)}) custom-call(f32[64,2048]{1,0:T(8,128)S(1)} %collective-permute-done.4.from_far, f32[64,2048]{1,0:T(8,128)S(1)} %collective-permute-done.5.from_near), custom_call_target="tpu_custom_call" | custom-call | tf_op jit(solution)/shard_map/work_output/pallas_call | solution.py:382
  90.5 0.0 collective-permute-done.6.from_far
  90.5 0.1 collective-permute-done.7.from_near
  90.6 1.2 %basis_output.1 = f32[2048,128]{1,0:T(8,128)} custom-call(f32[64,384]{1,0:T(8,128)S(1)} %collective-permute-done.6.from_far, f32[64,384]{1,0:T(8,128)S(1)} %collective-permute-done.7.from_near, f32[8,128]{1,0:T(8,128)S(1)} %get-tuple-element.23.after), custom_call_target="tpu_custom_call" | custom-call | tf_op jit(solution)/shard_map/basis_output/pallas_call | solution.py:391
Async XLA Ops:
  37.1 10.9 %collective-permute-start = (f32[64,2176]{1,0:T(8,128)S(1)}, f32[64,2176]{1,0:T(8,128)S(1)}, u32[]{:S(2)}, u32[]{:S(2)}) collective-permute-start(f32[64,2176]{1,0:T(8,128)S(1)} %get-tuple-element.13), channel_id=1, source_target_pairs={{1,1},{17,0},{0,17},{16,7},{7,16},{23,6},{6,23},{22,9},{9,22},{25,... | collective-permute-start | bytes 1671176 | tf_op jit(solution)/shard_map/ppermute | solution.py:348
  39.1 8.9 %collective-permute-start.1 = (f32[64,2176]{1,0:T(8,128)S(1)}, f32[64,2176]{1,0:T(8,128)S(1)}, u32[]{:S(2)}, u32[]{:S(2)}) collective-permute-start(f32[64,2176]{1,0:T(8,128)S(1)} %get-tuple-element.14), channel_id=1, source_target_pairs={{1,17},{17,1},{0,16},{16,0},{7,23},{23,7},{6,22},{22,6},{9,25},{25... | collective-permute-start | bytes 1671176 | tf_op jit(solution)/shard_map/ppermute | solution.py:349
  52.1 11.2 %collective-permute-start.2 = (f32[64,2304]{1,0:T(8,128)S(1)}, f32[64,2304]{1,0:T(8,128)S(1)}, u32[]{:S(2)}, u32[]{:S(2)}) collective-permute-start(f32[64,2304]{1,0:T(8,128)S(1)} %get-tuple-element.15), channel_id=1, source_target_pairs={{1,1},{17,0},{0,17},{16,7},{7,16},{23,6},{6,23},{22,9},{9,22},{25,... | collective-permute-start | bytes 1769480 | tf_op jit(solution)/shard_map/ppermute | solution.py:348
  54.0 9.3 %collective-permute-start.3 = (f32[64,2304]{1,0:T(8,128)S(1)}, f32[64,2304]{1,0:T(8,128)S(1)}, u32[]{:S(2)}, u32[]{:S(2)}) collective-permute-start(f32[64,2304]{1,0:T(8,128)S(1)} %get-tuple-element.16), channel_id=1, source_target_pairs={{1,17},{17,1},{0,16},{16,0},{7,23},{23,7},{6,22},{22,6},{9,25},{25... | collective-permute-start | bytes 1769480 | tf_op jit(solution)/shard_map/ppermute | solution.py:349
  66.9 20.7 %collective-permute-start.4 = (f32[64,2048]{1,0:T(8,128)S(1)}, f32[64,2048]{1,0:T(8,128)S(1)}, u32[]{:S(2)}, u32[]{:S(2)}) collective-permute-start(f32[64,2048]{1,0:T(8,128)S(1)} %get-tuple-element.17), channel_id=1, source_target_pairs={{1,0},{17,2},{0,1},{16,4},{7,3},{23,6},{6,5},{22,8},{9,7},{25,10},... | collective-permute-start | bytes 1572872 | tf_op jit(solution)/shard_map/ppermute | solution.py:378
  67.0 22.3 %collective-permute-start.5 = (f32[64,2048]{1,0:T(8,128)S(1)}, f32[64,2048]{1,0:T(8,128)S(1)}, u32[]{:S(2)}, u32[]{:S(2)}) collective-permute-start(f32[64,2048]{1,0:T(8,128)S(1)} %get-tuple-element.18), channel_id=1, source_target_pairs={{1,1},{17,0},{0,3},{16,2},{7,5},{23,4},{6,7},{22,6},{9,9},{25,8},{... | collective-permute-start | bytes 1572872 | tf_op jit(solution)/shard_map/ppermute | solution.py:379
  75.2 15.3 %collective-permute-start.6 = (f32[64,384]{1,0:T(8,128)S(1)}, f32[64,384]{1,0:T(8,128)S(1)}, u32[]{:S(2)}, u32[]{:S(2)}) collective-permute-start(f32[64,384]{1,0:T(8,128)S(1)} %get-tuple-element.21), channel_id=1, source_target_pairs={{1,0},{17,2},{0,1},{16,4},{7,3},{23,6},{6,5},{22,8},{9,7},{25,10},... | collective-permute-start | bytes 294920 | tf_op jit(solution)/shard_map/ppermute | solution.py:380
  75.3 15.3 %collective-permute-start.7 = (f32[64,384]{1,0:T(8,128)S(1)}, f32[64,384]{1,0:T(8,128)S(1)}, u32[]{:S(2)}, u32[]{:S(2)}) collective-permute-start(f32[64,384]{1,0:T(8,128)S(1)} %get-tuple-element.22), channel_id=1, source_target_pairs={{1,1},{17,0},{0,3},{16,2},{7,5},{23,4},{6,7},{22,6},{9,9},{25,8},{... | collective-permute-start | bytes 294920 | tf_op jit(solution)/shard_map/ppermute | solution.py:381

commit v8 on v7

--- a/solution.py
+++ b/solution.py
@@ -9,7 +9,8 @@
 from jax.sharding import PartitionSpec as P
 
 ROUNDS = 3
-CHUNK = 512
+CHUNK = 256
+PIECE = 512
 CHAINS = (
     ((0, 1), (0, 0), (1, 3), (1, 2), (2, 1), (2, 0), (3, 3), (3, 2)),
     ((0, 3), (0, 2), (1, 1), (1, 0), (2, 3), (2, 2), (3, 1), (3, 0)),
@@ -33,7 +34,9 @@
     lead = 1.0 + jnp.abs(along)
     cross = (2.0 * gamma) * inverse * along
     scale = lax.rsqrt(lead * lead + cross * cross)
-    return lead * scale, cross * scale
+    c, s = lead * scale, cross * scale
+    short = (1.0 - c * c) - s * s
+    return c + short * (0.5 * c), s + short * (0.5 * s)
 
 
 def small_rotation(gram, store, swapped):
@@ -238,12 +241,11 @@
     apply(turn[...], pieces(jnp.concatenate(columns, axis=1)), near, far, 0, False)
 
 
-def work_output(from_far, from_near, work, done, store, sems):
-    done[...] = jnp.zeros_like(done)
+def work_output(from_far, from_near, after, work, store, sems):
     even = lax.axis_index("jac") % 2 == 0
     copies = []
-    for number, begin in enumerate(range(0, work.shape[0], CHUNK)):
-        rows = pl.ds(begin, CHUNK)
+    for number, begin in enumerate(range(0, work.shape[0], PIECE)):
+        rows = pl.ds(begin, PIECE)
         near, far = from_near[:, rows], from_far[:, rows]
         pair = [jnp.where(even, far, near), jnp.where(even, near, far)]
         store[rows, :] = jnp.concatenate(pair, axis=0).T
@@ -253,7 +255,8 @@
         copy.wait()
 
 
-def basis_output(from_far, from_near, after, basis):
+def basis_output(from_far, from_near, basis, done):
+    done[...] = jnp.zeros_like(done)
     place = lax.axis_index("jac")
     count = lax.axis_size("jac")
     even = place % 2 == 0
@@ -379,23 +382,23 @@
     from_near = lax.ppermute(near, axes, near_route)
     from_far_basis = lax.ppermute(far_basis, axes, far_route)
     from_near_basis = lax.ppermute(near_basis, axes, near_route)
-    work, done = pl.pallas_call(
-        work_output,
+    basis, done = pl.pallas_call(
+        basis_output,
         out_shape=[shape(order, WIDTH), shape(SUB, WIDTH)],
         in_specs=[vmem()] * 2,
-        out_specs=[hbm(), vmem()],
-        scratch_shapes=[pltpu.VMEM((order, WIDTH), jnp.float32), pltpu.SemaphoreType.DMA((order // CHUNK,))],
+        out_specs=[vmem()] * 2,
+        compiler_params=PARAMS,
+        name="basis_output",
+    )(from_far_basis, from_near_basis)
+    work = pl.pallas_call(
+        work_output,
+        out_shape=shape(order, WIDTH),
+        in_specs=[vmem()] * 3,
+        out_specs=hbm(),
+        scratch_shapes=[pltpu.VMEM((order, WIDTH), jnp.float32), pltpu.SemaphoreType.DMA((order // PIECE,))],
         compiler_params=PARAMS,
         name="work_output",
-    )(from_far, from_near)
-    basis = pl.pallas_call(
-        basis_output,
-        out_shape=shape(order, WIDTH),
-        in_specs=[vmem()] * 3,
-        out_specs=vmem(),
-        compiler_params=PARAMS,
-        name="basis_output",
-    )(from_far_basis, from_near_basis, done)
+    )(from_far, from_near, done)
     return work[None], basis[None]
 
 

time: 92.1 us -> 93.5 us (1.015)
  waiting for transfers between devices: 26.3 us -> 27.5 us
    ppermute x1, waiting for transfers between devices: 0.01 us -> 12.5 us  [shards(): from_far_basis = lax.ppermute(far_basis, axes, far_route)]
    ppermute x3, waiting for transfers between devices: 24.5 us -> 14.1 us  [shards(): from_far = lax.ppermute(far, axes, far_route)]
    ppermute x3, waiting for transfers between devices: 1.71 us -> 0.01 us  [shards(): from_near = lax.ppermute(near, axes, near_route)]
  transfers between devices with their start and end apart: 8 -> 8, of which waited for: 5 -> 4; matrix products, arithmetic and copies ran while one was open for 0% -> 0% of each run, Pallas kernels for 1% -> 2%
where the time goes in v8:
time: 93.5 us; the launch traced here: 93.2 us
  blocking collectives  30.2 us (32%)
  waiting for transfers between devices  27.5 us (29%)
  starting transfers between devices  17.9 us (19%)
  Pallas kernels  16.8 us (18%)
    all_to_all x1, blocking collectives, shards(): moved = lax.all_to_all(dealt, axes, split_axis=0, concat_axis=0, tiled=True)  30.2 us
    ppermute x3, waiting for transfers between devices, shards(): from_far = lax.ppermute(far, axes, far_route)  14.1 us
    ppermute x1, waiting for transfers between devices, shards(): from_far_basis = lax.ppermute(far_basis, axes, far_route)  12.5 us
    ppermute x3, starting transfers between devices, shards(): from_near = lax.ppermute(near, axes, near_route)  12 us
    pallas_call x1, Pallas kernels, shards(): pl.pallas_call(functools.partial(next_kernel, order), out_shape=[shape(BL...  4.16 us
    pallas_call x1, Pallas kernels, shards(): pl.pallas_call(first_kernel, out_shape=[shape(BLK, order + WIDTH)] * 2, i...  4.04 us
    ppermute x3, starting transfers between devices, shards(): from_far = lax.ppermute(far, axes, far_route)  3.92 us
    pallas_call x1, Pallas kernels, shards(): pl.pallas_call(functools.partial(final_kernel, order), out_shape=[shape(B...  3.7 us
  transfers between devices with their start and end apart: 8, of which 4 were waited for; matrix products, arithmetic and copies ran while one was open for 0% of the time, Pallas kernels for 2%

profile of v8, /device:TPU:0, one launch (start us, length us, event | category | flops | bytes accessed | tf_op | source)
XLA Modules:
  0.0 93.2 jit_solution(5471141056287537730)
XLA Ops:
  0.6 2.3 %deal.1 = f32[128,16,128]{2,1,0:T(8,128)} custom-call(s32[8]{0:T(128)} %assignment.1, f32[8,16,2048]{2,1,0:T(8,128)} %stats.1), custom_call_target="tpu_custom_call" | custom-call | tf_op jit(solution)/shard_map/deal/pallas_call | solution.py:323
  3.0 30.2 %all_to_all.5 = f32[128,16,128]{2,1,0:T(8,128)S(1)} all-to-all(f32[128,16,128]{2,1,0:T(8,128)} %deal.1), channel_id=1, replica_groups=mesh['fac'=8,'jac'=16] {'fac','jac'}, dimensions={0} | all-to-all | bytes 2097152 | tf_op jit(solution)/shard_map/all_to_all | solution.py:336
  33.2 4.0 %first_round.1 = (f32[64,2176]{1,0:T(8,128)S(1)}, f32[64,2176]{1,0:T(8,128)S(1)}) custom-call(f32[2048,128]{1,0:T(8,128)S(1)} %bitcast.3), custom_call_target="tpu_custom_call" | custom-call | tf_op jit(solution)/shard_map/first_round/pallas_call | solution.py:339
  37.2 1.9 %collective-permute-start = (f32[64,2176]{1,0:T(8,128)S(1)}, f32[64,2176]{1,0:T(8,128)S(1)}, u32[]{:S(2)}, u32[]{:S(2)}) collective-permute-start(f32[64,2176]{1,0:T(8,128)S(1)} %get-tuple-element.13), channel_id=1, source_target_pairs={{1,1},{17,0},{0,17},{16,7},{7,16},{23,6},{6,23},{22,9},{9,22},{25,... | collective-permute-start | bytes 1671176 | tf_op jit(solution)/shard_map/ppermute | solution.py:351
  39.2 1.0 %collective-permute-start.1 = (f32[64,2176]{1,0:T(8,128)S(1)}, f32[64,2176]{1,0:T(8,128)S(1)}, u32[]{:S(2)}, u32[]{:S(2)}) collective-permute-start(f32[64,2176]{1,0:T(8,128)S(1)} %get-tuple-element.14), channel_id=1, source_target_pairs={{1,17},{17,1},{0,16},{16,0},{7,23},{23,7},{6,22},{22,6},{9,25},{25... | collective-permute-start | bytes 1671176 | tf_op jit(solution)/shard_map/ppermute | solution.py:352
  40.1 8.0 %collective-permute-done.from_far = f32[64,2176]{1,0:T(8,128)S(1)} collective-permute-done((f32[64,2176]{1,0:T(8,128)S(1)}, f32[64,2176]{1,0:T(8,128)S(1)}, u32[]{:S(2)}, u32[]{:S(2)}) %collective-permute-start) | collective-permute-done | bytes 557088 | tf_op jit(solution)/shard_map/ppermute | solution.py:351
  48.1 0.0 collective-permute-done.1.from_near
  48.1 4.2 %next_round.1 = (f32[64,2304]{1,0:T(8,128)S(1)}, f32[64,2304]{1,0:T(8,128)S(1)}) custom-call(f32[64,2176]{1,0:T(8,128)S(1)} %collective-permute-done.from_far, f32[64,2176]{1,0:T(8,128)S(1)} %collective-permute-done.1.from_near), custom_call_target="tpu_custom_call" | custom-call | tf_op jit(solution)/shard_map/next_round/pallas_call | solution.py:354
  52.3 1.9 %collective-permute-start.2 = (f32[64,2304]{1,0:T(8,128)S(1)}, f32[64,2304]{1,0:T(8,128)S(1)}, u32[]{:S(2)}, u32[]{:S(2)}) collective-permute-start(f32[64,2304]{1,0:T(8,128)S(1)} %get-tuple-element.15), channel_id=1, source_target_pairs={{1,1},{17,0},{0,17},{16,7},{7,16},{23,6},{6,23},{22,9},{9,22},{25,... | collective-permute-start | bytes 1769480 | tf_op jit(solution)/shard_map/ppermute | solution.py:351
  54.2 3.1 %collective-permute-start.3 = (f32[64,2304]{1,0:T(8,128)S(1)}, f32[64,2304]{1,0:T(8,128)S(1)}, u32[]{:S(2)}, u32[]{:S(2)}) collective-permute-start(f32[64,2304]{1,0:T(8,128)S(1)} %get-tuple-element.16), channel_id=1, source_target_pairs={{1,17},{17,1},{0,16},{16,0},{7,23},{23,7},{6,22},{22,6},{9,25},{25... | collective-permute-start | bytes 1769480 | tf_op jit(solution)/shard_map/ppermute | solution.py:352
  57.3 6.2 %collective-permute-done.2.from_far = f32[64,2304]{1,0:T(8,128)S(1)} collective-permute-done((f32[64,2304]{1,0:T(8,128)S(1)}, f32[64,2304]{1,0:T(8,128)S(1)}, u32[]{:S(2)}, u32[]{:S(2)}) %collective-permute-start.2) | collective-permute-done | bytes 589856 | tf_op jit(solution)/shard_map/ppermute | solution.py:351
  63.5 0.0 collective-permute-done.3.from_near
  63.5 3.7 %final_round.1 = (f32[64,2048]{1,0:T(8,128)S(1)}, f32[64,2048]{1,0:T(8,128)S(1)}, f32[128,128]{1,0:T(8,128)S(1)}) custom-call(f32[64,2304]{1,0:T(8,128)S(1)} %collective-permute-done.2.from_far, f32[64,2304]{1,0:T(8,128)S(1)} %collective-permute-done.3.from_near), custom_call_target="tpu_custom_call" | custom-call | tf_op jit(solution)/shard_map/final_round/pallas_call | solution.py:363
  67.2 0.1 collective-permute-start.4
  67.3 8.0 %collective-permute-start.5 = (f32[64,2048]{1,0:T(8,128)S(1)}, f32[64,2048]{1,0:T(8,128)S(1)}, u32[]{:S(2)}, u32[]{:S(2)}) collective-permute-start(f32[64,2048]{1,0:T(8,128)S(1)} %get-tuple-element.18), channel_id=1, source_target_pairs={{1,1},{17,0},{0,3},{16,2},{7,5},{23,4},{6,7},{22,6},{9,9},{25,8},{... | collective-permute-start | bytes 1572872 | tf_op jit(solution)/shard_map/ppermute | solution.py:382
  75.2 0.2 final_basis.1
  75.5 0.1 collective-permute-start.6
  75.5 1.9 %collective-permute-start.7 = (f32[64,384]{1,0:T(8,128)S(1)}, f32[64,384]{1,0:T(8,128)S(1)}, u32[]{:S(2)}, u32[]{:S(2)}) collective-permute-start(f32[64,384]{1,0:T(8,128)S(1)} %get-tuple-element.21), channel_id=1, source_target_pairs={{1,1},{17,0},{0,3},{16,2},{7,5},{23,4},{6,7},{22,6},{9,9},{25,8},{... | collective-permute-start | bytes 294920 | tf_op jit(solution)/shard_map/ppermute | solution.py:384
  77.5 12.5 %collective-permute-done.6.from_far = f32[64,384]{1,0:T(8,128)S(1)} collective-permute-done((f32[64,384]{1,0:T(8,128)S(1)}, f32[64,384]{1,0:T(8,128)S(1)}, u32[]{:S(2)}, u32[]{:S(2)}) %collective-permute-start.6) | collective-permute-done | bytes 98336 | tf_op jit(solution)/shard_map/ppermute | solution.py:383
  90.0 0.9 collective-permute-done.7.from_near
  90.8 1.2 %basis_output.1 = (f32[2048,128]{1,0:T(8,128)}, f32[8,128]{1,0:T(8,128)S(1)}) custom-call(f32[64,384]{1,0:T(8,128)S(1)} %collective-permute-done.6.from_far, f32[64,384]{1,0:T(8,128)S(1)} %collective-permute-done.7.from_near), custom_call_target="tpu_custom_call" | custom-call | tf_op jit(solution)/shard_map/basis_output/pallas_call | solution.py:385
  92.0 0.0 collective-permute-done.4.from_far
  92.0 0.0 collective-permute-done.5.from_near
  92.0 1.1 %work_output.1 = f32[2048,128]{1,0:T(8,128)} custom-call(f32[64,2048]{1,0:T(8,128)S(1)} %collective-permute-done.4.from_far, f32[64,2048]{1,0:T(8,128)S(1)} %collective-permute-done.5.from_near, f32[8,128]{1,0:T(8,128)S(1)} %get-tuple-element.22.after), custom_call_target="tpu_custom_call" | custom-call | tf_op jit(solution)/shard_map/work_output/pallas_call | solution.py:393
Async XLA Ops:
  37.2 10.9 %collective-permute-start = (f32[64,2176]{1,0:T(8,128)S(1)}, f32[64,2176]{1,0:T(8,128)S(1)}, u32[]{:S(2)}, u32[]{:S(2)}) collective-permute-start(f32[64,2176]{1,0:T(8,128)S(1)} %get-tuple-element.13), channel_id=1, source_target_pairs={{1,1},{17,0},{0,17},{16,7},{7,16},{23,6},{6,23},{22,9},{9,22},{25,... | collective-permute-start | bytes 1671176 | tf_op jit(solution)/shard_map/ppermute | solution.py:351
  39.2 8.9 %collective-permute-start.1 = (f32[64,2176]{1,0:T(8,128)S(1)}, f32[64,2176]{1,0:T(8,128)S(1)}, u32[]{:S(2)}, u32[]{:S(2)}) collective-permute-start(f32[64,2176]{1,0:T(8,128)S(1)} %get-tuple-element.14), channel_id=1, source_target_pairs={{1,17},{17,1},{0,16},{16,0},{7,23},{23,7},{6,22},{22,6},{9,25},{25... | collective-permute-start | bytes 1671176 | tf_op jit(solution)/shard_map/ppermute | solution.py:352
  52.3 11.2 %collective-permute-start.2 = (f32[64,2304]{1,0:T(8,128)S(1)}, f32[64,2304]{1,0:T(8,128)S(1)}, u32[]{:S(2)}, u32[]{:S(2)}) collective-permute-start(f32[64,2304]{1,0:T(8,128)S(1)} %get-tuple-element.15), channel_id=1, source_target_pairs={{1,1},{17,0},{0,17},{16,7},{7,16},{23,6},{6,23},{22,9},{9,22},{25,... | collective-permute-start | bytes 1769480 | tf_op jit(solution)/shard_map/ppermute | solution.py:351
  54.2 9.3 %collective-permute-start.3 = (f32[64,2304]{1,0:T(8,128)S(1)}, f32[64,2304]{1,0:T(8,128)S(1)}, u32[]{:S(2)}, u32[]{:S(2)}) collective-permute-start(f32[64,2304]{1,0:T(8,128)S(1)} %get-tuple-element.16), channel_id=1, source_target_pairs={{1,17},{17,1},{0,16},{16,0},{7,23},{23,7},{6,22},{22,6},{9,25},{25... | collective-permute-start | bytes 1769480 | tf_op jit(solution)/shard_map/ppermute | solution.py:352
  67.2 24.9 %collective-permute-start.4 = (f32[64,2048]{1,0:T(8,128)S(1)}, f32[64,2048]{1,0:T(8,128)S(1)}, u32[]{:S(2)}, u32[]{:S(2)}) collective-permute-start(f32[64,2048]{1,0:T(8,128)S(1)} %get-tuple-element.17), channel_id=1, source_target_pairs={{1,0},{17,2},{0,1},{16,4},{7,3},{23,6},{6,5},{22,8},{9,7},{25,10},... | collective-permute-start | bytes 1572872 | tf_op jit(solution)/shard_map/ppermute | solution.py:381
  67.3 24.8 %collective-permute-start.5 = (f32[64,2048]{1,0:T(8,128)S(1)}, f32[64,2048]{1,0:T(8,128)S(1)}, u32[]{:S(2)}, u32[]{:S(2)}) collective-permute-start(f32[64,2048]{1,0:T(8,128)S(1)} %get-tuple-element.18), channel_id=1, source_target_pairs={{1,1},{17,0},{0,3},{16,2},{7,5},{23,4},{6,7},{22,6},{9,9},{25,8},{... | collective-permute-start | bytes 1572872 | tf_op jit(solution)/shard_map/ppermute | solution.py:382
  75.5 14.5 %collective-permute-start.6 = (f32[64,384]{1,0:T(8,128)S(1)}, f32[64,384]{1,0:T(8,128)S(1)}, u32[]{:S(2)}, u32[]{:S(2)}) collective-permute-start(f32[64,384]{1,0:T(8,128)S(1)} %get-tuple-element.20), channel_id=1, source_target_pairs={{1,0},{17,2},{0,1},{16,4},{7,3},{23,6},{6,5},{22,8},{9,7},{25,10},... | collective-permute-start | bytes 294920 | tf_op jit(solution)/shard_map/ppermute | solution.py:383
  75.5 15.3 %collective-permute-start.7 = (f32[64,384]{1,0:T(8,128)S(1)}, f32[64,384]{1,0:T(8,128)S(1)}, u32[]{:S(2)}, u32[]{:S(2)}) collective-permute-start(f32[64,384]{1,0:T(8,128)S(1)} %get-tuple-element.21), channel_id=1, source_target_pairs={{1,1},{17,0},{0,3},{16,2},{7,5},{23,4},{6,7},{22,6},{9,9},{25,8},{... | collective-permute-start | bytes 294920 | tf_op jit(solution)/shard_map/ppermute | solution.py:384

commit v9 on v6

--- a/solution.py
+++ b/solution.py
@@ -33,7 +33,9 @@
     lead = 1.0 + jnp.abs(along)
     cross = (2.0 * gamma) * inverse * along
     scale = lax.rsqrt(lead * lead + cross * cross)
-    return lead * scale, cross * scale
+    c, s = lead * scale, cross * scale
+    short = (1.0 - c * c) - s * s
+    return c + short * (0.5 * c), s + short * (0.5 * s)
 
 
 def small_rotation(gram, store, swapped):

time: 92.7 us -> 93 us (level)
  no operation moved by 1% of the time
where the time goes in v9:
time: 93 us; the launch traced here: 92.7 us
  blocking collectives  30.2 us (32%)
  waiting for transfers between devices  29.7 us (32%)
  Pallas kernels  16.1 us (17%)
  starting transfers between devices  15.9 us (17%)
    all_to_all x1, blocking collectives, shards(): moved = lax.all_to_all(dealt, axes, split_axis=0, concat_axis=0, tiled=True)  30.2 us
    ppermute x3, waiting for transfers between devices, shards(): from_far = lax.ppermute(far, axes, far_route)  28.9 us
    ppermute x3, starting transfers between devices, shards(): from_near = lax.ppermute(near, axes, near_route)  12 us
    pallas_call x2, Pallas kernels, shards(): pl.pallas_call(functools.partial(next_kernel, order, later == ROUNDS - 1)...  8.04 us
    pallas_call x1, Pallas kernels, shards(): pl.pallas_call(first_kernel, out_shape=[shape(BLK, order + WIDTH)] * 2, i...  4.04 us
    ppermute x3, starting transfers between devices, shards(): from_far = lax.ppermute(far, axes, far_route)  3.92 us
    pallas_call x1, Pallas kernels, shards(): pl.pallas_call(deal_kernel, out_shape=shape(devices, slab, WIDTH), in_spe...  2.34 us
  transfers between devices with their start and end apart: 6, of which 4 were waited for; matrix products, arithmetic and copies ran while one was open for 0% of the time, Pallas kernels for 0%

profile of v9, /device:TPU:0, one launch (start us, length us, event | category | flops | bytes accessed | tf_op | source)
XLA Modules:
  0.0 92.7 jit_solution(12549742974260510699)
XLA Ops:
  0.6 2.3 %deal.1 = f32[128,16,128]{2,1,0:T(8,128)} custom-call(s32[8]{0:T(128)} %assignment.1, f32[8,16,2048]{2,1,0:T(8,128)} %stats.1), custom_call_target="tpu_custom_call" | custom-call | tf_op jit(solution)/shard_map/deal/pallas_call | solution.py:292
  3.0 30.2 %all_to_all.5 = f32[128,16,128]{2,1,0:T(8,128)S(1)} all-to-all(f32[128,16,128]{2,1,0:T(8,128)} %deal.1), channel_id=1, replica_groups=mesh['fac'=8,'jac'=16] {'fac','jac'}, dimensions={0} | all-to-all | bytes 2097152 | tf_op jit(solution)/shard_map/all_to_all | solution.py:305
  33.2 4.0 %first_round.1 = (f32[64,2176]{1,0:T(8,128)S(1)}, f32[64,2176]{1,0:T(8,128)S(1)}) custom-call(f32[2048,128]{1,0:T(8,128)S(1)} %bitcast.3), custom_call_target="tpu_custom_call" | custom-call | tf_op jit(solution)/shard_map/first_round/pallas_call | solution.py:308
  37.2 1.9 %collective-permute-start = (f32[64,2176]{1,0:T(8,128)S(1)}, f32[64,2176]{1,0:T(8,128)S(1)}, u32[]{:S(2)}, u32[]{:S(2)}) collective-permute-start(f32[64,2176]{1,0:T(8,128)S(1)} %get-tuple-element.10), channel_id=1, source_target_pairs={{1,1},{17,0},{0,17},{16,7},{7,16},{23,6},{6,23},{22,9},{9,22},{25,... | collective-permute-start | bytes 1671176 | tf_op jit(solution)/shard_map/ppermute | solution.py:326
  39.2 1.0 %collective-permute-start.1 = (f32[64,2176]{1,0:T(8,128)S(1)}, f32[64,2176]{1,0:T(8,128)S(1)}, u32[]{:S(2)}, u32[]{:S(2)}) collective-permute-start(f32[64,2176]{1,0:T(8,128)S(1)} %get-tuple-element.11), channel_id=1, source_target_pairs={{1,17},{17,1},{0,16},{16,0},{7,23},{23,7},{6,22},{22,6},{9,25},{25... | collective-permute-start | bytes 1671176 | tf_op jit(solution)/shard_map/ppermute | solution.py:327
  40.1 8.0 %collective-permute-done.from_far = f32[64,2176]{1,0:T(8,128)S(1)} collective-permute-done((f32[64,2176]{1,0:T(8,128)S(1)}, f32[64,2176]{1,0:T(8,128)S(1)}, u32[]{:S(2)}, u32[]{:S(2)}) %collective-permute-start) | collective-permute-done | bytes 557088 | tf_op jit(solution)/shard_map/ppermute | solution.py:326
  48.1 0.0 collective-permute-done.1.from_near
  48.1 4.2 %next_round.2 = (f32[64,2304]{1,0:T(8,128)S(1)}, f32[64,2304]{1,0:T(8,128)S(1)}) custom-call(f32[64,2176]{1,0:T(8,128)S(1)} %collective-permute-done.from_far, f32[64,2176]{1,0:T(8,128)S(1)} %collective-permute-done.1.from_near), custom_call_target="tpu_custom_call" | custom-call | tf_op jit(solution)/shard_map/next_round/pallas_call | solution.py:329
  52.3 1.9 %collective-permute-start.2 = (f32[64,2304]{1,0:T(8,128)S(1)}, f32[64,2304]{1,0:T(8,128)S(1)}, u32[]{:S(2)}, u32[]{:S(2)}) collective-permute-start(f32[64,2304]{1,0:T(8,128)S(1)} %get-tuple-element.12), channel_id=1, source_target_pairs={{1,1},{17,0},{0,17},{16,7},{7,16},{23,6},{6,23},{22,9},{9,22},{25,... | collective-permute-start | bytes 1769480 | tf_op jit(solution)/shard_map/ppermute | solution.py:326
  54.2 3.1 %collective-permute-start.3 = (f32[64,2304]{1,0:T(8,128)S(1)}, f32[64,2304]{1,0:T(8,128)S(1)}, u32[]{:S(2)}, u32[]{:S(2)}) collective-permute-start(f32[64,2304]{1,0:T(8,128)S(1)} %get-tuple-element.13), channel_id=1, source_target_pairs={{1,17},{17,1},{0,16},{16,0},{7,23},{23,7},{6,22},{22,6},{9,25},{25... | collective-permute-start | bytes 1769480 | tf_op jit(solution)/shard_map/ppermute | solution.py:327
  57.3 6.2 %collective-permute-done.2.from_far = f32[64,2304]{1,0:T(8,128)S(1)} collective-permute-done((f32[64,2304]{1,0:T(8,128)S(1)}, f32[64,2304]{1,0:T(8,128)S(1)}, u32[]{:S(2)}, u32[]{:S(2)}) %collective-permute-start.2) | collective-permute-done | bytes 589856 | tf_op jit(solution)/shard_map/ppermute | solution.py:326
  63.5 0.0 collective-permute-done.3.from_near
  63.5 3.9 %next_round.3 = (f32[64,2432]{1,0:T(8,128)S(1)}, f32[64,2432]{1,0:T(8,128)S(1)}) custom-call(f32[64,2304]{1,0:T(8,128)S(1)} %collective-permute-done.2.from_far, f32[64,2304]{1,0:T(8,128)S(1)} %collective-permute-done.3.from_near), custom_call_target="tpu_custom_call" | custom-call | tf_op jit(solution)/shard_map/next_round/pallas_call | solution.py:329
  67.3 0.1 collective-permute-start.4
  67.4 8.0 %collective-permute-start.5 = (f32[64,2432]{1,0:T(8,128)S(1)}, f32[64,2432]{1,0:T(8,128)S(1)}, u32[]{:S(2)}, u32[]{:S(2)}) collective-permute-start(f32[64,2432]{1,0:T(8,128)S(1)} %get-tuple-element.15), channel_id=1, source_target_pairs={{1,1},{17,0},{0,3},{16,2},{7,5},{23,4},{6,7},{22,6},{9,9},{25,8},{... | collective-permute-start | bytes 1867784 | tf_op jit(solution)/shard_map/ppermute | solution.py:327
  75.4 14.7 %collective-permute-done.4.from_far = f32[64,2432]{1,0:T(8,128)S(1)} collective-permute-done((f32[64,2432]{1,0:T(8,128)S(1)}, f32[64,2432]{1,0:T(8,128)S(1)}, u32[]{:S(2)}, u32[]{:S(2)}) %collective-permute-start.4) | collective-permute-done | bytes 622624 | tf_op jit(solution)/shard_map/ppermute | solution.py:326
  90.1 0.9 collective-permute-done.5.from_near
  91.0 1.7 %output.1 = (f32[2048,128]{1,0:T(8,128)}, f32[2048,128]{1,0:T(8,128)}) custom-call(f32[64,2432]{1,0:T(8,128)S(1)} %collective-permute-done.4.from_far, f32[64,2432]{1,0:T(8,128)S(1)} %collective-permute-done.5.from_near), custom_call_target="tpu_custom_call" | custom-call | tf_op jit(solution)/shard_map/output/pallas_call | solution.py:338
Async XLA Ops:
  37.2 10.9 %collective-permute-start = (f32[64,2176]{1,0:T(8,128)S(1)}, f32[64,2176]{1,0:T(8,128)S(1)}, u32[]{:S(2)}, u32[]{:S(2)}) collective-permute-start(f32[64,2176]{1,0:T(8,128)S(1)} %get-tuple-element.10), channel_id=1, source_target_pairs={{1,1},{17,0},{0,17},{16,7},{7,16},{23,6},{6,23},{22,9},{9,22},{25,... | collective-permute-start | bytes 1671176 | tf_op jit(solution)/shard_map/ppermute | solution.py:326
  39.2 8.9 %collective-permute-start.1 = (f32[64,2176]{1,0:T(8,128)S(1)}, f32[64,2176]{1,0:T(8,128)S(1)}, u32[]{:S(2)}, u32[]{:S(2)}) collective-permute-start(f32[64,2176]{1,0:T(8,128)S(1)} %get-tuple-element.11), channel_id=1, source_target_pairs={{1,17},{17,1},{0,16},{16,0},{7,23},{23,7},{6,22},{22,6},{9,25},{25... | collective-permute-start | bytes 1671176 | tf_op jit(solution)/shard_map/ppermute | solution.py:327
  52.3 11.2 %collective-permute-start.2 = (f32[64,2304]{1,0:T(8,128)S(1)}, f32[64,2304]{1,0:T(8,128)S(1)}, u32[]{:S(2)}, u32[]{:S(2)}) collective-permute-start(f32[64,2304]{1,0:T(8,128)S(1)} %get-tuple-element.12), channel_id=1, source_target_pairs={{1,1},{17,0},{0,17},{16,7},{7,16},{23,6},{6,23},{22,9},{9,22},{25,... | collective-permute-start | bytes 1769480 | tf_op jit(solution)/shard_map/ppermute | solution.py:326
  54.2 9.3 %collective-permute-start.3 = (f32[64,2304]{1,0:T(8,128)S(1)}, f32[64,2304]{1,0:T(8,128)S(1)}, u32[]{:S(2)}, u32[]{:S(2)}) collective-permute-start(f32[64,2304]{1,0:T(8,128)S(1)} %get-tuple-element.13), channel_id=1, source_target_pairs={{1,17},{17,1},{0,16},{16,0},{7,23},{23,7},{6,22},{22,6},{9,25},{25... | collective-permute-start | bytes 1769480 | tf_op jit(solution)/shard_map/ppermute | solution.py:327
  67.3 22.8 %collective-permute-start.4 = (f32[64,2432]{1,0:T(8,128)S(1)}, f32[64,2432]{1,0:T(8,128)S(1)}, u32[]{:S(2)}, u32[]{:S(2)}) collective-permute-start(f32[64,2432]{1,0:T(8,128)S(1)} %get-tuple-element.14), channel_id=1, source_target_pairs={{1,0},{17,2},{0,1},{16,4},{7,3},{23,6},{6,5},{22,8},{9,7},{25,10},... | collective-permute-start | bytes 1867784 | tf_op jit(solution)/shard_map/ppermute | solution.py:326
  67.4 23.6 %collective-permute-start.5 = (f32[64,2432]{1,0:T(8,128)S(1)}, f32[64,2432]{1,0:T(8,128)S(1)}, u32[]{:S(2)}, u32[]{:S(2)}) collective-permute-start(f32[64,2432]{1,0:T(8,128)S(1)} %get-tuple-element.15), channel_id=1, source_target_pairs={{1,1},{17,0},{0,3},{16,2},{7,5},{23,4},{6,7},{22,6},{9,9},{25,8},{... | collective-permute-start | bytes 1867784 | tf_op jit(solution)/shard_map/ppermute | solution.py:327

commit v10 on v9

--- a/solution.py
+++ b/solution.py
@@ -9,7 +9,7 @@
 from jax.sharding import PartitionSpec as P
 
 ROUNDS = 3
-CHUNK = 512
+CHUNK = 256
 CHAINS = (
     ((0, 1), (0, 0), (1, 3), (1, 2), (2, 1), (2, 0), (3, 3), (3, 2)),
     ((0, 3), (0, 2), (1, 1), (1, 0), (2, 3), (2, 2), (3, 1), (3, 0)),

time: 93 us -> 93 us (level)
  no operation moved by 1% of the time
where the time goes in v10:
time: 93 us; the launch traced here: 92.7 us
  blocking collectives  30.2 us (32%)
  waiting for transfers between devices  29.7 us (32%)
  Pallas kernels  16.1 us (17%)
  starting transfers between devices  15.9 us (17%)
    all_to_all x1, blocking collectives, shards(): moved = lax.all_to_all(dealt, axes, split_axis=0, concat_axis=0, tiled=True)  30.2 us
    ppermute x3, waiting for transfers between devices, shards(): from_far = lax.ppermute(far, axes, far_route)  28.9 us
    ppermute x3, starting transfers between devices, shards(): from_near = lax.ppermute(near, axes, near_route)  12 us
    pallas_call x2, Pallas kernels, shards(): pl.pallas_call(functools.partial(next_kernel, order, later == ROUNDS - 1)...  8.04 us
    pallas_call x1, Pallas kernels, shards(): pl.pallas_call(first_kernel, out_shape=[shape(BLK, order + WIDTH)] * 2, i...  4.04 us
    ppermute x3, starting transfers between devices, shards(): from_far = lax.ppermute(far, axes, far_route)  3.92 us
    pallas_call x1, Pallas kernels, shards(): pl.pallas_call(deal_kernel, out_shape=shape(devices, slab, WIDTH), in_spe...  2.34 us
  transfers between devices with their start and end apart: 6, of which 4 were waited for; matrix products, arithmetic and copies ran while one was open for 0% of the time, Pallas kernels for 0%

profile of v10, /device:TPU:0, one launch (start us, length us, event | category | flops | bytes accessed | tf_op | source)
XLA Modules:
  0.0 92.7 jit_solution(1119416128512537752)
XLA Ops:
  0.6 2.3 %deal.1 = f32[128,16,128]{2,1,0:T(8,128)} custom-call(s32[8]{0:T(128)} %assignment.1, f32[8,16,2048]{2,1,0:T(8,128)} %stats.1), custom_call_target="tpu_custom_call" | custom-call | tf_op jit(solution)/shard_map/deal/pallas_call | solution.py:292
  3.0 30.2 %all_to_all.5 = f32[128,16,128]{2,1,0:T(8,128)S(1)} all-to-all(f32[128,16,128]{2,1,0:T(8,128)} %deal.1), channel_id=1, replica_groups=mesh['fac'=8,'jac'=16] {'fac','jac'}, dimensions={0} | all-to-all | bytes 2097152 | tf_op jit(solution)/shard_map/all_to_all | solution.py:305
  33.2 4.0 %first_round.1 = (f32[64,2176]{1,0:T(8,128)S(1)}, f32[64,2176]{1,0:T(8,128)S(1)}) custom-call(f32[2048,128]{1,0:T(8,128)S(1)} %bitcast.3), custom_call_target="tpu_custom_call" | custom-call | tf_op jit(solution)/shard_map/first_round/pallas_call | solution.py:308
  37.2 1.9 %collective-permute-start = (f32[64,2176]{1,0:T(8,128)S(1)}, f32[64,2176]{1,0:T(8,128)S(1)}, u32[]{:S(2)}, u32[]{:S(2)}) collective-permute-start(f32[64,2176]{1,0:T(8,128)S(1)} %get-tuple-element.10), channel_id=1, source_target_pairs={{1,1},{17,0},{0,17},{16,7},{7,16},{23,6},{6,23},{22,9},{9,22},{25,... | collective-permute-start | bytes 1671176 | tf_op jit(solution)/shard_map/ppermute | solution.py:326
  39.2 1.0 %collective-permute-start.1 = (f32[64,2176]{1,0:T(8,128)S(1)}, f32[64,2176]{1,0:T(8,128)S(1)}, u32[]{:S(2)}, u32[]{:S(2)}) collective-permute-start(f32[64,2176]{1,0:T(8,128)S(1)} %get-tuple-element.11), channel_id=1, source_target_pairs={{1,17},{17,1},{0,16},{16,0},{7,23},{23,7},{6,22},{22,6},{9,25},{25... | collective-permute-start | bytes 1671176 | tf_op jit(solution)/shard_map/ppermute | solution.py:327
  40.1 8.0 %collective-permute-done.from_far = f32[64,2176]{1,0:T(8,128)S(1)} collective-permute-done((f32[64,2176]{1,0:T(8,128)S(1)}, f32[64,2176]{1,0:T(8,128)S(1)}, u32[]{:S(2)}, u32[]{:S(2)}) %collective-permute-start) | collective-permute-done | bytes 557088 | tf_op jit(solution)/shard_map/ppermute | solution.py:326
  48.1 0.0 collective-permute-done.1.from_near
  48.1 4.2 %next_round.2 = (f32[64,2304]{1,0:T(8,128)S(1)}, f32[64,2304]{1,0:T(8,128)S(1)}) custom-call(f32[64,2176]{1,0:T(8,128)S(1)} %collective-permute-done.from_far, f32[64,2176]{1,0:T(8,128)S(1)} %collective-permute-done.1.from_near), custom_call_target="tpu_custom_call" | custom-call | tf_op jit(solution)/shard_map/next_round/pallas_call | solution.py:329
  52.3 1.9 %collective-permute-start.2 = (f32[64,2304]{1,0:T(8,128)S(1)}, f32[64,2304]{1,0:T(8,128)S(1)}, u32[]{:S(2)}, u32[]{:S(2)}) collective-permute-start(f32[64,2304]{1,0:T(8,128)S(1)} %get-tuple-element.12), channel_id=1, source_target_pairs={{1,1},{17,0},{0,17},{16,7},{7,16},{23,6},{6,23},{22,9},{9,22},{25,... | collective-permute-start | bytes 1769480 | tf_op jit(solution)/shard_map/ppermute | solution.py:326
  54.2 3.1 %collective-permute-start.3 = (f32[64,2304]{1,0:T(8,128)S(1)}, f32[64,2304]{1,0:T(8,128)S(1)}, u32[]{:S(2)}, u32[]{:S(2)}) collective-permute-start(f32[64,2304]{1,0:T(8,128)S(1)} %get-tuple-element.13), channel_id=1, source_target_pairs={{1,17},{17,1},{0,16},{16,0},{7,23},{23,7},{6,22},{22,6},{9,25},{25... | collective-permute-start | bytes 1769480 | tf_op jit(solution)/shard_map/ppermute | solution.py:327
  57.3 6.2 %collective-permute-done.2.from_far = f32[64,2304]{1,0:T(8,128)S(1)} collective-permute-done((f32[64,2304]{1,0:T(8,128)S(1)}, f32[64,2304]{1,0:T(8,128)S(1)}, u32[]{:S(2)}, u32[]{:S(2)}) %collective-permute-start.2) | collective-permute-done | bytes 589856 | tf_op jit(solution)/shard_map/ppermute | solution.py:326
  63.5 0.0 collective-permute-done.3.from_near
  63.5 3.9 %next_round.3 = (f32[64,2432]{1,0:T(8,128)S(1)}, f32[64,2432]{1,0:T(8,128)S(1)}) custom-call(f32[64,2304]{1,0:T(8,128)S(1)} %collective-permute-done.2.from_far, f32[64,2304]{1,0:T(8,128)S(1)} %collective-permute-done.3.from_near), custom_call_target="tpu_custom_call" | custom-call | tf_op jit(solution)/shard_map/next_round/pallas_call | solution.py:329
  67.4 0.1 collective-permute-start.4
  67.4 8.0 %collective-permute-start.5 = (f32[64,2432]{1,0:T(8,128)S(1)}, f32[64,2432]{1,0:T(8,128)S(1)}, u32[]{:S(2)}, u32[]{:S(2)}) collective-permute-start(f32[64,2432]{1,0:T(8,128)S(1)} %get-tuple-element.15), channel_id=1, source_target_pairs={{1,1},{17,0},{0,3},{16,2},{7,5},{23,4},{6,7},{22,6},{9,9},{25,8},{... | collective-permute-start | bytes 1867784 | tf_op jit(solution)/shard_map/ppermute | solution.py:327
  75.4 14.7 %collective-permute-done.4.from_far = f32[64,2432]{1,0:T(8,128)S(1)} collective-permute-done((f32[64,2432]{1,0:T(8,128)S(1)}, f32[64,2432]{1,0:T(8,128)S(1)}, u32[]{:S(2)}, u32[]{:S(2)}) %collective-permute-start.4) | collective-permute-done | bytes 622624 | tf_op jit(solution)/shard_map/ppermute | solution.py:326
  90.1 0.9 collective-permute-done.5.from_near
  91.0 1.7 %output.1 = (f32[2048,128]{1,0:T(8,128)}, f32[2048,128]{1,0:T(8,128)}) custom-call(f32[64,2432]{1,0:T(8,128)S(1)} %collective-permute-done.4.from_far, f32[64,2432]{1,0:T(8,128)S(1)} %collective-permute-done.5.from_near), custom_call_target="tpu_custom_call" | custom-call | tf_op jit(solution)/shard_map/output/pallas_call | solution.py:338
Async XLA Ops:
  37.2 10.9 %collective-permute-start = (f32[64,2176]{1,0:T(8,128)S(1)}, f32[64,2176]{1,0:T(8,128)S(1)}, u32[]{:S(2)}, u32[]{:S(2)}) collective-permute-start(f32[64,2176]{1,0:T(8,128)S(1)} %get-tuple-element.10), channel_id=1, source_target_pairs={{1,1},{17,0},{0,17},{16,7},{7,16},{23,6},{6,23},{22,9},{9,22},{25,... | collective-permute-start | bytes 1671176 | tf_op jit(solution)/shard_map/ppermute | solution.py:326
  39.2 8.9 %collective-permute-start.1 = (f32[64,2176]{1,0:T(8,128)S(1)}, f32[64,2176]{1,0:T(8,128)S(1)}, u32[]{:S(2)}, u32[]{:S(2)}) collective-permute-start(f32[64,2176]{1,0:T(8,128)S(1)} %get-tuple-element.11), channel_id=1, source_target_pairs={{1,17},{17,1},{0,16},{16,0},{7,23},{23,7},{6,22},{22,6},{9,25},{25... | collective-permute-start | bytes 1671176 | tf_op jit(solution)/shard_map/ppermute | solution.py:327
  52.3 11.2 %collective-permute-start.2 = (f32[64,2304]{1,0:T(8,128)S(1)}, f32[64,2304]{1,0:T(8,128)S(1)}, u32[]{:S(2)}, u32[]{:S(2)}) collective-permute-start(f32[64,2304]{1,0:T(8,128)S(1)} %get-tuple-element.12), channel_id=1, source_target_pairs={{1,1},{17,0},{0,17},{16,7},{7,16},{23,6},{6,23},{22,9},{9,22},{25,... | collective-permute-start | bytes 1769480 | tf_op jit(solution)/shard_map/ppermute | solution.py:326
  54.2 9.3 %collective-permute-start.3 = (f32[64,2304]{1,0:T(8,128)S(1)}, f32[64,2304]{1,0:T(8,128)S(1)}, u32[]{:S(2)}, u32[]{:S(2)}) collective-permute-start(f32[64,2304]{1,0:T(8,128)S(1)} %get-tuple-element.13), channel_id=1, source_target_pairs={{1,17},{17,1},{0,16},{16,0},{7,23},{23,7},{6,22},{22,6},{9,25},{25... | collective-permute-start | bytes 1769480 | tf_op jit(solution)/shard_map/ppermute | solution.py:327
  67.4 22.8 %collective-permute-start.4 = (f32[64,2432]{1,0:T(8,128)S(1)}, f32[64,2432]{1,0:T(8,128)S(1)}, u32[]{:S(2)}, u32[]{:S(2)}) collective-permute-start(f32[64,2432]{1,0:T(8,128)S(1)} %get-tuple-element.14), channel_id=1, source_target_pairs={{1,0},{17,2},{0,1},{16,4},{7,3},{23,6},{6,5},{22,8},{9,7},{25,10},... | collective-permute-start | bytes 1867784 | tf_op jit(solution)/shard_map/ppermute | solution.py:326
  67.4 23.6 %collective-permute-start.5 = (f32[64,2432]{1,0:T(8,128)S(1)}, f32[64,2432]{1,0:T(8,128)S(1)}, u32[]{:S(2)}, u32[]{:S(2)}) collective-permute-start(f32[64,2432]{1,0:T(8,128)S(1)} %get-tuple-element.15), channel_id=1, source_target_pairs={{1,1},{17,0},{0,3},{16,2},{7,5},{23,4},{6,7},{22,6},{9,9},{25,8},{... | collective-permute-start | bytes 1867784 | tf_op jit(solution)/shard_map/ppermute | solution.py:327
